TPU v7x, 32 devices: a whole 2x2x4 slice. The times are simulated.
32 devices in a mesh: dp: 4 (over z), expert: 8 (over y, x, core).
Axes of the slice: x: 2, y: 2, z: 4, core: 2. Of those that a mesh axis runs over, the one named last changes fastest.
Arguments:
- tokens: bfloat16 [16384, 768], P(('dp', 'expert')), may hold values from -6 to 6
- out_grad: bfloat16 [16384, 768], P(('dp', 'expert')), may hold values from -6 to 6
- routes: int32 [16384, 2], P(('dp', 'expert')), may hold values from 0 to 7, all different within a row; in each aligned block of 256 rows (0 to 255, 256 to 511, ...) at most 128 rows name the same one
- lengths: int32 [64], P(('dp', 'expert')), may hold values from 128 to 256, as said below
- attention: float32 [4, 768, 768], P(None, ('dp', 'expert'))
- gain_bias: float32 [7, 768], P(None, ('dp', 'expert')), may hold values from -2 to 2
- router: float32 [8, 768], P(None, ('dp', 'expert')), may hold values from -0.21875 to 0.21875
- expert_up: float32 [8, 3072, 768], P('expert', 'dp'), may hold values from -0.625 to 0.625
- up_bias: float32 [8, 3072], P('expert', 'dp'), may hold values from -3 to 3
- expert_down: float32 [8, 3072, 768], P('expert', 'dp'), may hold values from -0.109375 to 0.109375
- down_bias: float32 [8, 768], P('expert', 'dp'), may hold values from -3 to 3
- first_attention: float32 [4, 768, 768], P(None, ('dp', 'expert'))
- first_gain_bias: float32 [7, 768], P(None, ('dp', 'expert'))
- first_router: float32 [8, 768], P(None, ('dp', 'expert'))
- first_expert_up: float32 [8, 3072, 768], P('expert', 'dp')
- first_up_bias: float32 [8, 3072], P('expert', 'dp')
- first_expert_down: float32 [8, 3072, 768], P('expert', 'dp')
- first_down_bias: float32 [8, 768], P('expert', 'dp')
- square_attention: float32 [4, 768, 768], P(None, ('dp', 'expert')), as said below
- square_gain_bias: float32 [7, 768], P(None, ('dp', 'expert')), as said below
- square_router: float32 [8, 768], P(None, ('dp', 'expert')), as said below
- square_expert_up: float32 [8, 3072, 768], P('expert', 'dp'), as said below
- square_up_bias: float32 [8, 3072], P('expert', 'dp'), as said below
- square_expert_down: float32 [8, 3072, 768], P('expert', 'dp'), as said below
- square_down_bias: float32 [8, 768], P('expert', 'dp'), as said below
Outputs:
- output: float32 [16384, 768], P(('dp', 'expert'))
- input_grad: float32 [16384, 768], P(('dp', 'expert'))
- grad_attention: float32 [4, 768, 768], P(None, ('dp', 'expert'))
- grad_gain_bias: float32 [7, 768], P(None, ('dp', 'expert'))
- grad_router: float32 [8, 768], P(None, ('dp', 'expert'))
- grad_expert_up: float32 [8, 3072, 768], P('expert', 'dp')
- grad_up_bias: float32 [8, 3072], P('expert', 'dp')
- grad_expert_down: float32 [8, 3072, 768], P('expert', 'dp')
- grad_down_bias: float32 [8, 768], P('expert', 'dp')
- new_attention: float32 [4, 768, 768], P(None, ('dp', 'expert'))
- new_gain_bias: float32 [7, 768], P(None, ('dp', 'expert'))
- new_router: float32 [8, 768], P(None, ('dp', 'expert'))
- new_expert_up: float32 [8, 3072, 768], P('expert', 'dp')
- new_up_bias: float32 [8, 3072], P('expert', 'dp')
- new_expert_down: float32 [8, 3072, 768], P('expert', 'dp')
- new_down_bias: float32 [8, 768], P('expert', 'dp')
- new_first_attention: float32 [4, 768, 768], P(None, ('dp', 'expert'))
- new_first_gain_bias: float32 [7, 768], P(None, ('dp', 'expert'))
- new_first_router: float32 [8, 768], P(None, ('dp', 'expert'))
- new_first_expert_up: float32 [8, 3072, 768], P('expert', 'dp')
- new_first_up_bias: float32 [8, 3072], P('expert', 'dp')
- new_first_expert_down: float32 [8, 3072, 768], P('expert', 'dp')
- new_first_down_bias: float32 [8, 768], P('expert', 'dp')
- new_square_attention: float32 [4, 768, 768], P(None, ('dp', 'expert'))
- new_square_gain_bias: float32 [7, 768], P(None, ('dp', 'expert'))
- new_square_router: float32 [8, 768], P(None, ('dp', 'expert'))
- new_square_expert_up: float32 [8, 3072, 768], P('expert', 'dp')
- new_square_up_bias: float32 [8, 3072], P('expert', 'dp')
- new_square_expert_down: float32 [8, 3072, 768], P('expert', 'dp')
- new_square_down_bias: float32 [8, 768], P('expert', 'dp')
Inputs may be any that keep to these rules, and one draw needn't show every extreme that they name: `routes`: each row names two different experts. In each aligned block of 256 rows (the rows of one device's micro-batch) no expert is named by more than 128 rows, and some block reaches 128. `lengths`: the first sequence is full. `square_attention`: Positive. `square_gain_bias`: Positive. `square_router`: Positive. `square_expert_up`: Positive. `square_up_bias`: Positive. `square_expert_down`: Positive. `square_down_bias`: Positive.
All inputs are finite; a program needn't handle non-finite values.
Results may differ from a plain program's by a relative error of at most 0.018.
Values may be sent and summed in bfloat16 or wider, within the bound.
A program may use at most 256 MiB of HBM per device.

v0:
```python
import jax
import jax.numpy as jnp
from jax import lax
from jax.sharding import PartitionSpec as P

D = 768
HEADS = 12
HEAD_DIM = 64
FF = 3072
LEN = 256
SEQ_MB = 1
MICRO = 2
STEP = 3
ROWS = 256


NORM_EPS = 1e-06
NEG_FILL = -1000000000.0
BETA_ONE = 0.9
BETA_TWO = 0.95
WEIGHT_DECAY = 0.1
ADAM_EPS = 1e-08
HIGHEST = lax.Precision.HIGHEST


def norm_rows(values, gain, bias):
    center = values - jnp.mean(values, axis=-1, keepdims=True)
    spread = jnp.mean(center * center, axis=-1, keepdims=True)
    return center * lax.rsqrt(spread + NORM_EPS) * gain + bias


def slot_tables(route_rows, experts_all, capacity):
    flat = route_rows.reshape(-1)
    count = flat.shape[0]
    onehot = (flat[:, None] == jnp.arange(experts_all, dtype=jnp.int32)[None, :]).astype(jnp.int32)
    before = jnp.cumsum(onehot, axis=0) - onehot
    slot = jnp.sum(before * onehot, axis=1)
    positions = flat * capacity + slot
    table = (
        jnp.full((experts_all * capacity,), count, jnp.int32)
        .at[positions]
        .set(jnp.arange(count, dtype=jnp.int32))
    )
    return (positions.reshape(route_rows.shape), table)


def gate_pair(picked):
    return jnp.stack(
        [jax.nn.sigmoid(picked[:, 0] - picked[:, 1]), jax.nn.sigmoid(picked[:, 1] - picked[:, 0])],
        axis=1,
    )


def adam_step(weight, grad, first, square, rate):
    new_first = BETA_ONE * first + (1.0 - BETA_ONE) * grad
    new_square = BETA_TWO * square + (1.0 - BETA_TWO) * grad * grad
    first_hat = new_first / (1.0 - BETA_ONE**STEP)
    square_hat = new_square / (1.0 - BETA_TWO**STEP)
    update = -rate * (first_hat / (jnp.sqrt(square_hat) + ADAM_EPS) + WEIGHT_DECAY * weight)
    return (weight + update, new_first, new_square)


def body(
    tokens,
    out_grad,
    routes,
    lengths,
    attention,
    gain_bias,
    router,
    expert_up,
    up_bias,
    expert_down,
    down_bias,
    first_attention,
    first_gain_bias,
    first_router,
    first_expert_up,
    first_up_bias,
    first_expert_down,
    first_down_bias,
    square_attention,
    square_gain_bias,
    square_router,
    square_expert_up,
    square_up_bias,
    square_expert_down,
    square_down_bias,
):
    f32 = jnp.float32
    b16 = jnp.bfloat16
    experts_all = router.shape[0]
    capacity = 4 * ROWS // experts_all
    senders = lax.axis_size("expert")
    local_count = expert_up.shape[0]
    scale = HEAD_DIM ** (-0.5)
    dense_local = (attention.astype(b16), gain_bias.astype(b16), router.astype(b16))
    expert_local = (
        expert_up.astype(b16),
        up_bias.astype(b16),
        expert_down.astype(b16),
        down_bias.astype(b16),
    )
    grad_weights = jnp.zeros((4, D, D), f32)
    grad_vector = jnp.zeros((7, D), f32)
    grad_router = jnp.zeros((experts_all, D), f32)
    grad_up = jnp.zeros((local_count, FF, D), f32)
    grad_up_bias = jnp.zeros((local_count, FF), f32)
    grad_down = jnp.zeros((local_count, FF, D), f32)
    grad_down_bias = jnp.zeros((local_count, D), f32)
    output_rows = []
    input_rows = []
    head_shape = (SEQ_MB, LEN, HEADS, HEAD_DIM)
    for micro in range(MICRO):
        first_row = micro * ROWS
        rows_in = tokens[first_row : first_row + ROWS].astype(f32)
        grad_out = out_grad[first_row : first_row + ROWS].astype(f32)
        route_rows = routes[first_row : first_row + ROWS]
        seq_len = lengths[micro * SEQ_MB : (micro + 1) * SEQ_MB]
        dense_full = (
            lax.all_gather(dense_local[0], ("dp", "expert"), axis=1, tiled=True),
            lax.all_gather(dense_local[1], ("dp", "expert"), axis=1, tiled=True),
            lax.all_gather(dense_local[2], ("dp", "expert"), axis=1, tiled=True),
        )
        weights_b, vector_b, router_b = dense_full
        vector = vector_b.astype(f32)
        normed_one = norm_rows(rows_in, vector[0], vector[1])
        normed_one_b = normed_one.astype(b16)
        proj = jnp.einsum("rd,jde->jre", normed_one_b, weights_b[:3], preferred_element_type=f32)
        queries = (proj[0] + vector[2]).astype(b16).reshape(head_shape)
        key_rows = proj[1].astype(b16).reshape(head_shape)
        values = (proj[2] + vector[3]).astype(b16).reshape(head_shape)
        valid = (jnp.arange(LEN, dtype=jnp.int32)[None, :] < seq_len[:, None])[:, None, None, :]
        scores = (
            jnp.einsum("bqhe,bkhe->bhqk", queries, key_rows, preferred_element_type=f32) * scale
        )
        scores = jnp.where(valid, scores, NEG_FILL)
        top_score = jnp.max(scores, axis=-1, keepdims=True)
        log_total = top_score + jnp.log(
            jnp.sum(jnp.exp(scores - top_score), axis=-1, keepdims=True)
        )
        chance_b = jnp.exp(scores - log_total).astype(b16)
        context_b = (
            jnp.einsum("bhqk,bkhe->bqhe", chance_b, values, preferred_element_type=f32)
            .astype(b16)
            .reshape(ROWS, D)
        )
        branch = jnp.dot(context_b, weights_b[3], preferred_element_type=f32) + vector[4]
        resid = rows_in + branch
        normed_two_b = norm_rows(resid, vector[5], vector[6]).astype(b16)
        logits = jnp.einsum("rd,ed->re", normed_two_b, router_b, preferred_element_type=f32)
        chooser = (
            route_rows[:, :, None] == jnp.arange(experts_all, dtype=jnp.int32)[None, None, :]
        ).astype(f32)
        picked = jnp.sum(logits[:, None, :] * chooser, axis=-1)
        gates = gate_pair(picked)
        positions, table = slot_tables(route_rows, experts_all, capacity)
        flat_positions = positions.reshape(-1)
        expert_full = (
            lax.all_gather(expert_local[0], "dp", axis=1, tiled=True),
            lax.all_gather(expert_local[1], "dp", axis=1, tiled=True),
            lax.all_gather(expert_local[2], "dp", axis=1, tiled=True),
            lax.all_gather(expert_local[3], "dp", axis=1, tiled=True),
        )
        up_b, up_bias_b, down_b, down_bias_b = expert_full
        padded_two = jnp.concatenate([normed_two_b, jnp.zeros((1, D), b16)], axis=0)
        send = padded_two[table // 2].reshape(senders, local_count, capacity, D)
        received = lax.all_to_all(send, "expert", split_axis=0, concat_axis=0, tiled=True)
        pre = (
            jnp.einsum("secd,efd->secf", received, up_b, preferred_element_type=f32)
            + up_bias_b.astype(f32)[None, :, None, :]
        )
        hidden_b = jax.nn.gelu(pre).astype(b16)
        result = (
            jnp.einsum("secf,efd->secd", hidden_b, down_b, preferred_element_type=f32)
            + down_bias_b.astype(f32)[None, :, None, :]
        )
        back = lax.all_to_all(result.astype(b16), "expert", split_axis=0, concat_axis=0, tiled=True)
        back, pre_act, hidden_b, received = (back, pre, hidden_b, received)
        expert_out = (
            back.reshape(experts_all * capacity, D)[flat_positions].reshape(ROWS, 2, D).astype(f32)
        )
        output = resid + gates[:, 0:1] * expert_out[:, 0] + gates[:, 1:2] * expert_out[:, 1]
        output_rows.append(output)
        gate_grad = jnp.sum(grad_out[:, None, :] * expert_out, axis=-1)
        to_expert = (gates[:, :, None] * grad_out[:, None, :]).astype(b16).reshape(2 * ROWS, D)
        padded_grad = jnp.concatenate([to_expert, jnp.zeros((1, D), b16)], axis=0)
        grad_send = padded_grad[table].reshape(senders, local_count, capacity, D)
        arrived = lax.all_to_all(grad_send, "expert", split_axis=0, concat_axis=0, tiled=True)
        expert_full = (
            lax.all_gather(expert_local[0], "dp", axis=1, tiled=True),
            lax.all_gather(expert_local[1], "dp", axis=1, tiled=True),
            lax.all_gather(expert_local[2], "dp", axis=1, tiled=True),
            lax.all_gather(expert_local[3], "dp", axis=1, tiled=True),
        )
        up_b, up_bias_b, down_b, down_bias_b = expert_full
        grad_down = grad_down + jnp.einsum(
            "secf,secd->efd", hidden_b, arrived, preferred_element_type=f32
        )
        grad_down_bias = grad_down_bias + jnp.sum(arrived, axis=(0, 2), dtype=f32)
        grad_hidden = jnp.einsum("secd,efd->secf", arrived, down_b, preferred_element_type=f32)
        gelu_value, gelu_back = jax.vjp(jax.nn.gelu, pre_act)
        grad_pre_b = gelu_back(grad_hidden)[0].astype(b16)
        grad_up = grad_up + jnp.einsum(
            "secf,secd->efd", grad_pre_b, received, preferred_element_type=f32
        )
        grad_up_bias = grad_up_bias + jnp.sum(grad_pre_b, axis=(0, 2), dtype=f32)
        grad_input_slots = jnp.einsum(
            "secf,efd->secd", grad_pre_b, up_b, preferred_element_type=f32
        ).astype(b16)
        returned = lax.all_to_all(
            grad_input_slots, "expert", split_axis=0, concat_axis=0, tiled=True
        )
        grad_slots = (
            returned.reshape(experts_all * capacity, D)[flat_positions]
            .reshape(ROWS, 2, D)
            .astype(f32)
        )
        gate_value, pair_back = jax.vjp(gate_pair, picked)
        grad_picked = pair_back(gate_grad)[0]
        grad_logits = jnp.sum(grad_picked[:, :, None] * chooser, axis=1)
        grad_router = grad_router + jnp.einsum(
            "re,rd->ed", grad_logits, normed_two_b.astype(f32), precision=HIGHEST
        )
        grad_normed = (
            grad_slots[:, 0]
            + grad_slots[:, 1]
            + jnp.dot(grad_logits, router_b.astype(f32), precision=HIGHEST)
        )
        norm_value, norm_back_two = jax.vjp(norm_rows, resid, vector[5], vector[6])
        grad_from_norm, grad_gain_two, grad_bias_two = norm_back_two(grad_normed)
        grad_resid = grad_out + grad_from_norm
        dense_full = (
            lax.all_gather(dense_local[0], ("dp", "expert"), axis=1, tiled=True),
            lax.all_gather(dense_local[1], ("dp", "expert"), axis=1, tiled=True),
            lax.all_gather(dense_local[2], ("dp", "expert"), axis=1, tiled=True),
        )
        weights_b, vector_b, router_b = dense_full
        grad_branch_b = grad_resid.astype(b16)
        grad_out_proj = jnp.einsum(
            "rd,re->de", context_b, grad_branch_b, preferred_element_type=f32
        )
        grad_context_b = (
            jnp.einsum("re,de->rd", grad_branch_b, weights_b[3], preferred_element_type=f32)
            .astype(b16)
            .reshape(head_shape)
        )
        scores = (
            jnp.einsum("bqhe,bkhe->bhqk", queries, key_rows, preferred_element_type=f32) * scale
        )
        scores = jnp.where(valid, scores, NEG_FILL)
        chance = jnp.exp(scores - log_total)
        chance_b = chance.astype(b16)
        grad_values = jnp.einsum(
            "bhqk,bqhe->bkhe", chance_b, grad_context_b, preferred_element_type=f32
        ).astype(b16)
        grad_chance = jnp.einsum(
            "bqhe,bkhe->bhqk", grad_context_b, values, preferred_element_type=f32
        )
        grad_scores_b = (
            chance * (grad_chance - jnp.sum(chance * grad_chance, axis=-1, keepdims=True))
        ).astype(b16)
        grad_queries = (
            jnp.einsum("bhqk,bkhe->bqhe", grad_scores_b, key_rows, preferred_element_type=f32)
            * scale
        ).astype(b16)
        grad_keys = (
            jnp.einsum("bhqk,bqhe->bkhe", grad_scores_b, queries, preferred_element_type=f32)
            * scale
        ).astype(b16)
        grad_proj = jnp.stack(
            [
                grad_queries.reshape(ROWS, D),
                grad_keys.reshape(ROWS, D),
                grad_values.reshape(ROWS, D),
            ]
        )
        grad_in_proj = jnp.einsum(
            "rd,jre->jde", normed_one_b, grad_proj, preferred_element_type=f32
        )
        grad_weights = grad_weights + jnp.concatenate([grad_in_proj, grad_out_proj[None]], axis=0)
        grad_normed_one = jnp.einsum(
            "jre,jde->rd", grad_proj, weights_b[:3], preferred_element_type=f32
        )
        norm_value_one, norm_back_one = jax.vjp(norm_rows, rows_in, vector[0], vector[1])
        grad_from_first, grad_gain_one, grad_bias_one = norm_back_one(grad_normed_one)
        grad_vector = grad_vector + jnp.stack(
            [
                grad_gain_one,
                grad_bias_one,
                jnp.sum(grad_proj[0], axis=0, dtype=f32),
                jnp.sum(grad_proj[2], axis=0, dtype=f32),
                jnp.sum(grad_branch_b, axis=0, dtype=f32),
                grad_gain_two,
                grad_bias_two,
            ]
        )
        input_rows.append(grad_resid + grad_from_first)
    shard_weights, shard_vector, shard_router = (
        lax.psum_scatter(grad_weights, ("dp", "expert"), scatter_dimension=1, tiled=True),
        lax.psum_scatter(grad_vector, ("dp", "expert"), scatter_dimension=1, tiled=True),
        lax.psum_scatter(grad_router, ("dp", "expert"), scatter_dimension=1, tiled=True),
    )
    shard_up, shard_up_bias, shard_down, shard_down_bias = (
        lax.psum_scatter(
            grad_up.astype(jnp.bfloat16), "dp", scatter_dimension=1, tiled=True
        ).astype(jnp.float32),
        lax.psum_scatter(
            grad_up_bias.astype(jnp.bfloat16), "dp", scatter_dimension=1, tiled=True
        ).astype(jnp.float32),
        lax.psum_scatter(
            grad_down.astype(jnp.bfloat16), "dp", scatter_dimension=1, tiled=True
        ).astype(jnp.float32),
        lax.psum_scatter(
            grad_down_bias.astype(jnp.bfloat16), "dp", scatter_dimension=1, tiled=True
        ).astype(jnp.float32),
    )
    params = (attention, gain_bias, router, expert_up, up_bias, expert_down, down_bias)
    grads = (
        shard_weights,
        shard_vector,
        shard_router,
        shard_up,
        shard_up_bias,
        shard_down,
        shard_down_bias,
    )
    firsts = (
        first_attention,
        first_gain_bias,
        first_router,
        first_expert_up,
        first_up_bias,
        first_expert_down,
        first_down_bias,
    )
    squares = (
        square_attention,
        square_gain_bias,
        square_router,
        square_expert_up,
        square_up_bias,
        square_expert_down,
        square_down_bias,
    )
    rates = (
        1.6 * D ** (-0.5),
        0.3,
        0.5 * D ** (-0.5),
        1.5 * D ** (-0.5),
        0.25,
        0.5 * FF ** (-0.5),
        0.25,
    )
    updated = [adam_step(params[i], grads[i], firsts[i], squares[i], rates[i]) for i in range(7)]
    return (
        jnp.concatenate(output_rows, axis=0),
        jnp.concatenate(input_rows, axis=0),
        grads[0],
        grads[1],
        grads[2],
        grads[3],
        grads[4],
        grads[5],
        grads[6],
        updated[0][0],
        updated[1][0],
        updated[2][0],
        updated[3][0],
        updated[4][0],
        updated[5][0],
        updated[6][0],
        updated[0][1],
        updated[1][1],
        updated[2][1],
        updated[3][1],
        updated[4][1],
        updated[5][1],
        updated[6][1],
        updated[0][2],
        updated[1][2],
        updated[2][2],
        updated[3][2],
        updated[4][2],
        updated[5][2],
        updated[6][2],
    )


def solution(mesh):
    return jax.shard_map(
        body,
        mesh=mesh,
        in_specs=(
            P(("dp", "expert"), None),
            P(("dp", "expert"), None),
            P(("dp", "expert"), None),
            P(("dp", "expert")),
            P(None, ("dp", "expert"), None),
            P(None, ("dp", "expert")),
            P(None, ("dp", "expert")),
            P("expert", "dp", None),
            P("expert", "dp"),
            P("expert", "dp", None),
            P("expert", "dp"),
            P(None, ("dp", "expert"), None),
            P(None, ("dp", "expert")),
            P(None, ("dp", "expert")),
            P("expert", "dp", None),
            P("expert", "dp"),
            P("expert", "dp", None),
            P("expert", "dp"),
            P(None, ("dp", "expert"), None),
            P(None, ("dp", "expert")),
            P(None, ("dp", "expert")),
            P("expert", "dp", None),
            P("expert", "dp"),
            P("expert", "dp", None),
            P("expert", "dp"),
        ),
        out_specs=(
            P(("dp", "expert"), None),
            P(("dp", "expert"), None),
            P(None, ("dp", "expert"), None),
            P(None, ("dp", "expert")),
            P(None, ("dp", "expert")),
            P("expert", "dp", None),
            P("expert", "dp"),
            P("expert", "dp", None),
            P("expert", "dp"),
            P(None, ("dp", "expert"), None),
            P(None, ("dp", "expert")),
            P(None, ("dp", "expert")),
            P("expert", "dp", None),
            P("expert", "dp"),
            P("expert", "dp", None),
            P("expert", "dp"),
            P(None, ("dp", "expert"), None),
            P(None, ("dp", "expert")),
            P(None, ("dp", "expert")),
            P("expert", "dp", None),
            P("expert", "dp"),
            P("expert", "dp", None),
            P("expert", "dp"),
            P(None, ("dp", "expert"), None),
            P(None, ("dp", "expert")),
            P(None, ("dp", "expert")),
            P("expert", "dp", None),
            P("expert", "dp"),
            P("expert", "dp", None),
            P("expert", "dp"),
        ),
        check_vma=False,
    )
```

profile of v0, /device:TPU:0, one launch (start us, length us, event | category | flops | bytes accessed | tf_op | source)
XLA Modules:
  0.0 884.2 jit_solution(10414498698142596629)
XLA Ops:
  14.4 43.6 %all-gather = bf16[32,24,7]{1,2,0:T(8,128)(2,1)S(1)} all-gather(bf16[1,24,7]{1,2,0:T(8,128)(2,1)S(1)} %convert_bitcast_fusion.1), channel_id=1, replica_groups=mesh['dp'=4,'expert'=8] {'dp','expert'}, dimensions={0}, use_global_device_ids=true | all-gather | bytes 11088 | tf_op jit(solution)/shard_map/all_gather | solution.py:122
  70.1 8.0 all-gather.6.cloned.1.call-done
  78.1 3.3 fusion.87
  102.5 5.2 gather_fusion.2
  107.8 4.4 all-to-all-start.2
  115.3 10.9 %all-reduce.12 = bf16[768]{0:T(1024)(128)(2,1)S(1)} all-reduce(bf16[768]{0:T(1024)(128)(2,1)S(1)} %dynamic-update-slice), channel_id=1, replica_groups=mesh['dp'=4,'expert'=8] {'dp'}, use_global_device_ids=true, to_apply=%add.12 | all-reduce | flops 768 | bytes 3072
  126.8 13.3 %all_gather.18 = bf16[1,3072]{1,0:T(2,128)(2,1)S(1)} all-gather(bf16[1,768]{1,0:T(2,128)(2,1)S(1)} %convert_element_type.404), channel_id=1, replica_groups=mesh['dp'=4,'expert'=8] {'dp'}, dimensions={1}, use_global_device_ids=true | all-gather | bytes 7680 | tf_op jit(solution)/shard_map/all_gather | solution.py:161
  140.8 43.2 %all-gather.1 = bf16[32,24,8]{1,2,0:T(8,128)(2,1)S(1)} all-gather(bf16[1,24,8]{1,2,0:T(8,128)(2,1)S(1)} %copy-done.152), channel_id=1, replica_groups=mesh['dp'=4,'expert'=8] {'dp','expert'}, dimensions={0}, use_global_device_ids=true | all-gather | bytes 12672 | tf_op jit(solution)/shard_map/all_gather | solution.py:123
  197.5 5.2 gather_fusion
  203.6 3.6 all-to-all-start
  207.2 10.2 %fusion.50 = f32[8,128,3072]{2,1,0:T(8,128)} fusion(bf16[1,3072,768]{2,1,0:T(8,128)(2,1)} %all-gather.8.cloned.1.call-done, bf16[8,1,128,768]{3,2,1,0:T(8,128)(2,1)} %all-to-all-done.2), kind=kOutput, calls=%fused_computation.77 | convolution fusion | flops 4831838208 | bytes 18874368 | tf_op jit(solution)/shard_map/secd,efd->secf/dot_general | solution.py:170
  217.5 41.7 %all-gather.10.cloned.1.call-done = bf16[1,3072,768]{2,1,0:T(8,128)(2,1)} async-done(((bf16[1,768,768]{2,1,0:T(8,128)(2,1)}), bf16[1,3072,768]{2,1,0:T(8,128)(2,1)}) %all-gather.10.cloned.1.call-update) | async-done | bytes 4718608 | tf_op jit(solution)/shard_map/all_gather | solution.py:162
  259.2 12.9 %fusion.125 = bf16[8,1,128,768]{3,2,1,0:T(8,128)(2,1)} fusion(f32[768]{0:T(1024)S(1)} %copy-done.161, bf16[1,3072,768]{2,1,0:T(8,128)(2,1)} %all-gather.10.cloned.1.call-done, f32[8,128,3072]{2,1,0:T(8,128)} %fusion.50, f32[3072]{0:T(1024)S(1)} %bitcast.541), kind=kOutput, calls=%fused_computation.142 | convolution fusion | flops 4864868352 | bytes 18889728 | tf_op jit(solution)/shard_map/secf,efd->secd/dot_general | solution.py:175
  272.1 3.9 all-to-all-start.3
  276.0 7.0 fusion.52
  283.0 4.6 copy-done.175
  287.6 11.2 %fusion.120 = bf16[8,1,128,768]{3,2,1,0:T(8,128)(2,1)} fusion(f32[768]{0:T(1024)S(1)} %copy-done.161, bf16[1,3072,768]{2,1,0:T(8,128)(2,1)} %all-gather.10.cloned.1.call-done, f32[8,128,3072]{2,1,0:T(8,128)S(1)} %fusion.52, f32[3072]{0:T(1024)S(1)} %bitcast.542), kind=kOutput, calls=%fused_computation.141 | convolution fusion | flops 4864868352 | bytes 18889728 | tf_op jit(solution)/shard_map/secf,efd->secd/dot_general | solution.py:175
  298.7 4.3 all-to-all-start.1
  313.9 5.2 gather_fusion.6
  319.2 4.9 all-to-all-done.1
  324.1 4.5 all-to-all-start.6
  334.6 5.2 gather_fusion.4
  344.7 5.0 all-to-all-done.6
  349.7 3.8 all-to-all-start.4
  353.5 16.4 %convert_reduce_fusion = (f32[3072]{0:T(1024)S(1)}, bf16[8,1,128,3072]{3,2,0,1:T(8,128)(2,1)S(1)}) fusion(f32[3072]{0:T(1024)S(1)} %bitcast.543, f32[8,128,3072]{2,1,0:T(8,128)} %fusion.50, bf16[1,3072,768]{2,1,0:T(8,128)(2,1)} %all-gather.10.cloned.1.call-done, bf16[8,1,128,768]{3,2,1,0:T(8,128)(2,1)} %all-to-all-done.6), kind=kOutput, calls=%fused_computation.42 | convolution fusion | flops 4904186880 | bytes 25190400 | tf_op jit(solution)/shard_map/secd,efd->secf/dot_general | solution.py:201
  372.8 6.2 fusion.110
  379.0 4.2 all-to-all-start.7
  384.8 14.7 %convert_reduce_fusion.1 = (f32[3072]{0:T(1024)S(1)}, bf16[8,1,128,3072]{3,2,0,1:T(8,128)(2,1)S(1)}) fusion(f32[3072]{0:T(1024)S(1)} %bitcast.544, f32[8,128,3072]{2,1,0:T(8,128)} %copy-done.175, bf16[1,3072,768]{2,1,0:T(8,128)(2,1)} %all-gather.10.cloned.1.call-done, bf16[8,1,128,768]{3,2,1,0:T(8,128)(2,1)S(1)} %all-to-all-done.4), kind=kOutput, calls=%fused_computation.43 | convolution fusion | flops 4904186880 | bytes 25190400 | tf_op jit(solution)/shard_map/secd,efd->secf/dot_general | solution.py:201
  402.2 8.5 fusion.115
  410.6 4.3 all-to-all-start.5
  419.2 3.0 reshape.753
  422.2 3.3 fusion.264
  427.7 8.2 all-to-all-done.5
  464.8 3.0 convert_reduce_fusion.10
  490.0 4.1 maximum_add_fusion
  494.1 12.1 %copy.429 = f32[4,768,768]{2,0,1:T(4,128)} copy(f32[4,768,768]{1,2,0:T(8,128)} %maximum_add_fusion) | data formatting | bytes 18874368 | tf_op jit(solution)/shard_map/add | solution.py:281
  506.3 8.3 fusion.24
  514.7 10.6 %fusion.40 = bf16[1,3072,768]{2,1,0:T(8,128)(2,1)} fusion(f32[3072,768,1]{1,0,2:T(8,128)S(1)} %fusion.24, bf16[8,1,128,3072]{3,2,0,1:T(8,128)(2,1)} %copy-done.176, bf16[8,1,128,768]{3,2,1,0:T(8,128)(2,1)S(1)} %copy-done.54), kind=kOutput, calls=%fused_computation.67 | convolution fusion | flops 4836556800 | bytes 22020096 | tf_op jit(solution)/shard_map/secf,secd->efd/dot_general | solution.py:204
  526.0 12.0 %fusion.32 = f32[3072,768,1]{1,0,2:T(8,128)S(1)} fusion(bf16[8,1,128,768]{3,2,1,0:T(8,128)(2,1)} %all-to-all-done.6, f32[8,128,3072]{2,1,0:T(8,128)} %fusion.50, f32[3072]{0:T(1024)S(1)} %bitcast.545), kind=kOutput, calls=%fused_computation.59 | convolution fusion | flops 4863295488 | bytes 23605248 | tf_op jit(solution)/shard_map/secf,secd->efd/dot_general | solution.py:197
  538.0 12.7 %fusion.41 = bf16[1,3072,768]{2,1,0:T(8,128)(2,1)} fusion(f32[3072,768,1]{1,0,2:T(8,128)S(1)} %fusion.32, bf16[8,1,128,768]{3,2,1,0:T(8,128)(2,1)S(1)} %copy-done.32, f32[8,128,3072]{2,1,0:T(8,128)} %copy-done.175, f32[3072]{0:T(1024)S(1)} %bitcast.546), kind=kOutput, calls=%fused_computation.68 | convolution fusion | flops 4868014080 | bytes 28323840 | tf_op jit(solution)/shard_map/secf,secd->efd/dot_general | solution.py:197
  556.2 3.2 fusion.133
  559.5 4.3 fusion.161
  571.5 38.2 %all-reduce.16 = (f32[7,768]{1,0:T(8,128)S(1)}, f32[8,768]{1,0:T(8,128)S(1)}) all-reduce(f32[7,768]{1,0:T(8,128)S(1)} %add.618, f32[8,768]{1,0:T(8,128)} %convolution_add_fusion.4), channel_id=3, replica_groups=mesh['dp'=4,'expert'=8] {'dp','expert'}, use_global_device_ids=true, to_apply=%region_51.52.clone | all-reduce | flops 11520 | bytes 92160
  616.1 77.8 %all-reduce.19.cloned.1.call-done = f32[4,768,768]{2,0,1:T(4,128)} async-done(((f32[4,768,768]{2,0,1:T(4,128)}), f32[4,768,768]{2,0,1:T(4,128)}) %all-reduce.19.cloned.1.call-update) | async-done | bytes 9437200
  696.0 85.5 %reduce-scatter.11.cloned.1.call-done = bf16[1,768,768]{2,1,0:T(8,128)(2,1)} async-done(((bf16[1,3072,768]{2,1,0:T(8,128)(2,1)}), bf16[1,768,768]{2,1,0:T(8,128)(2,1)}) %reduce-scatter.11.cloned.1.call-update) | async-done | bytes 1179664 | tf_op jit(solution)/shard_map/reduce_scatter | solution.py:305
  781.5 6.9 multiply_add_fusion.2
  788.4 81.3 %reduce-scatter.13.cloned.1.call-done = bf16[1,768,768]{2,1,0:T(8,128)(2,1)} async-done(((bf16[1,3072,768]{2,1,0:T(8,128)(2,1)}), bf16[1,768,768]{2,1,0:T(8,128)(2,1)}) %reduce-scatter.13.cloned.1.call-update) | async-done | bytes 1179664 | tf_op jit(solution)/shard_map/reduce_scatter | solution.py:311
  869.6 7.5 multiply_add_fusion
  (595 shorter events, 164.9 us)
Async XLA Ops:
  7.2 70.8 %all-gather.6.cloned.1.call-start = ((), (), s32[]{:S(2)}) async-start(), calls=%async_computation.12 | async-start | bytes 4866048 | tf_op jit(solution)/shard_map/all_gather | solution.py:121
  9.1 198.2 %all-gather.8.cloned.1.call-start = ((), (), s32[]{:S(2)}) async-start(), calls=%async_computation.13 | async-start | bytes 5898240 | tf_op jit(solution)/shard_map/all_gather | solution.py:160
  11.9 47.0 %copy-start.8 = (bf16[512,768]{1,0:T(8,128)(2,1)S(1)}, bf16[512,768]{1,0:T(8,128)(2,1)}, u32[]{:S(2)}) copy-start(bf16[512,768]{1,0:T(8,128)(2,1)} %param.25) | copy-start | bytes 2359300
  12.0 48.2 %copy-start.168 = (s32[2]{0:T(128)S(1)}, s32[2]{0:T(128)}, u32[]{:S(2)}) copy-start(s32[2]{0:T(128)} %param.28) | copy-start | bytes 28
  12.0 247.2 %all-gather.10.cloned.1.call-start = ((), (), s32[]{:S(2)}) async-start(), calls=%async_computation.14 | async-start | bytes 5898240 | tf_op jit(solution)/shard_map/all_gather | solution.py:162
  13.2 55.3 %copy-start.23 = (bf16[512,768]{1,0:T(8,128)(2,1)S(1)}, bf16[512,768]{1,0:T(8,128)(2,1)}, u32[]{:S(2)}) copy-start(bf16[512,768]{1,0:T(8,128)(2,1)} %param.26) | copy-start | bytes 2359300
  13.2 56.3 %copy-start.116 = (f32[8,24]{1,0:T(8,128)S(1)}, f32[8,24]{1,0:T(8,128)}, u32[]{:S(2)}) copy-start(f32[8,24]{1,0:T(8,128)} %param.31) | copy-start | bytes 2308
  58.9 22.7 %copy-start.91 = (f32[768]{0:T(1024)}, f32[768]{0:T(1024)S(1)}, u32[]{:S(2)}) copy-start(f32[768]{0:T(1024)S(1)} %get-tuple-element.236) | copy-start | bytes 9220
  58.9 22.7 %copy-start.158 = (f32[768]{0:T(1024)}, f32[768]{0:T(1024)S(1)}, u32[]{:S(2)}) copy-start(f32[768]{0:T(1024)S(1)} %get-tuple-element.235) | copy-start | bytes 9220
  58.9 42.5 %copy-start.82 = (f32[768]{0:T(1024)}, f32[768]{0:T(1024)S(1)}, u32[]{:S(2)}) copy-start(f32[768]{0:T(1024)S(1)} %get-tuple-element.230) | copy-start | bytes 9220
  59.1 22.3 %copy-start.105 = (f32[256]{0:T(256)}, f32[256]{0:T(256)S(1)}, u32[]{:S(2)}) copy-start(f32[256]{0:T(256)S(1)} %get-tuple-element.359) | copy-start | bytes 3076
  59.1 22.5 %copy-start.109 = (f32[256]{0:T(256)}, f32[256]{0:T(256)S(1)}, u32[]{:S(2)}) copy-start(f32[256]{0:T(256)S(1)} %get-tuple-element.360) | copy-start | bytes 3076
  62.0 36.0 %copy-start.75 = (f32[12,64]{1,0:T(8,128)}, f32[12,64]{1,0:T(8,128)S(1)}, u32[]{:S(2)}) copy-start(f32[12,64]{1,0:T(8,128)S(1)} %add.554) | copy-start | bytes 9220
  69.5 119.9 %copy-start.26 = (f32[256,768]{1,0:T(8,128)}, f32[256,768]{1,0:T(8,128)S(1)}, u32[]{:S(2)}) copy-start(f32[256,768]{1,0:T(8,128)S(1)} %get-tuple-element.305) | copy-start | bytes 2359300
  102.4 100.3 %copy-start.33 = (bf16[256,768]{1,0:T(8,128)(2,1)}, bf16[256,768]{1,0:T(8,128)(2,1)S(1)}, u32[]{:S(2)}) copy-start(bf16[256,768]{1,0:T(8,128)(2,1)S(1)} %get-tuple-element.312) | copy-start | bytes 1179652
  107.7 33.1 %copy-start.152 = (bf16[1,24,8]{1,2,0:T(8,128)(2,1)S(1)}, bf16[1,24,8]{1,2,0:T(8,128)(2,1)}, u32[]{:S(2)}) copy-start(bf16[1,24,8]{1,2,0:T(8,128)(2,1)} %convert_bitcast_fusion) | copy-start | bytes 1156
  107.7 76.4 %copy-start.28 = (f32[256,768]{1,0:T(8,128)S(1)}, f32[256,768]{1,0:T(8,128)}, u32[]{:S(2)}) copy-start(f32[256,768]{1,0:T(8,128)} %get-tuple-element.306) | copy-start | bytes 2359300
  107.8 95.8 %all-to-all-start.2 = ((bf16[8,1,128,768]{3,2,1,0:T(8,128)(2,1)}), bf16[8,1,128,768]{3,2,1,0:T(8,128)(2,1)}, u32[]{:S(2)}, u32[]{:S(2)}) async-start(bf16[8,1,128,768]{3,2,1,0:T(8,128)(2,1)} %bitcast.56), calls=%async_computation.2 | async-start | bytes 3145728 | tf_op jit(solution)/shard_map/all_to_all | solution.py:168
  203.6 68.5 %all-to-all-start = ((bf16[8,1,128,768]{3,2,1,0:T(8,128)(2,1)}), bf16[8,1,128,768]{3,2,1,0:T(8,128)(2,1)S(1)}, u32[]{:S(2)}, u32[]{:S(2)}) async-start(bf16[8,1,128,768]{3,2,1,0:T(8,128)(2,1)} %bitcast.21), calls=%async_computation | async-start | bytes 3145728 | tf_op jit(solution)/shard_map/all_to_all | solution.py:168
  207.2 52.0 %copy-start.125 = (f32[1,3072]{1,0:T(1,128)S(1)}, f32[1,3072]{1,0:T(1,128)}, u32[]{:S(2)}) copy-start(f32[1,3072]{1,0:T(1,128)} %add.664) | copy-start | bytes 36868
  207.2 52.0 %copy-start.161 = (f32[768]{0:T(1024)S(1)}, f32[768]{0:T(1024)}, u32[]{:S(2)}) copy-start(f32[768]{0:T(1024)} %add.668) | copy-start | bytes 9220
  272.1 26.6 %all-to-all-start.3 = ((bf16[8,1,128,768]{3,2,1,0:T(8,128)(2,1)}), bf16[8,1,128,768]{3,2,1,0:T(8,128)(2,1)S(1)}, u32[]{:S(2)}, u32[]{:S(2)}) async-start(bf16[8,1,128,768]{3,2,1,0:T(8,128)(2,1)} %fusion.125), calls=%async_computation.3 | async-start | bytes 3145728 | tf_op jit(solution)/shard_map/all_to_all | solution.py:178
  298.7 25.4 %all-to-all-start.1 = ((bf16[8,1,128,768]{3,2,1,0:T(8,128)(2,1)}), bf16[8,1,128,768]{3,2,1,0:T(8,128)(2,1)S(1)}, u32[]{:S(2)}, u32[]{:S(2)}) async-start(bf16[8,1,128,768]{3,2,1,0:T(8,128)(2,1)} %fusion.120), calls=%async_computation.1 | async-start | bytes 3145728 | tf_op jit(solution)/shard_map/all_to_all | solution.py:178
  324.1 25.6 %all-to-all-start.6 = ((bf16[8,1,128,768]{3,2,1,0:T(8,128)(2,1)}), bf16[8,1,128,768]{3,2,1,0:T(8,128)(2,1)}, u32[]{:S(2)}, u32[]{:S(2)}) async-start(bf16[8,1,128,768]{3,2,1,0:T(8,128)(2,1)} %bitcast.515), calls=%async_computation.6 | async-start | bytes 3145728 | tf_op jit(solution)/shard_map/all_to_all | solution.py:189
  339.9 85.6 %copy-start.87 = (f32[256,8]{0,1:T(8,128)}, f32[256,8]{0,1:T(8,128)S(1)}, u32[]{:S(2)}) copy-start(f32[256,8]{0,1:T(8,128)S(1)} %select_reduce_fusion) | copy-start | bytes 24580
  339.9 102.4 %copy-start.89 = (f32[256,8]{0,1:T(8,128)}, f32[256,8]{0,1:T(8,128)S(1)}, u32[]{:S(2)}) copy-start(f32[256,8]{0,1:T(8,128)S(1)} %select_reduce_fusion.1) | copy-start | bytes 24580
  342.3 30.5 %slice-start.2 = ((s8[4718592]{0:T(1024)(128)(4,1)}), s8[524288]{0:T(1024)(128)(4,1)S(1)}, s32[]{:S(2)}) async-start(s8[4718592]{0:T(1024)(128)(4,1)} %bitcast.559), calls=%async_computation.22 | async-start | bytes 1048576
  349.7 29.3 %all-to-all-start.4 = ((bf16[8,1,128,768]{3,2,1,0:T(8,128)(2,1)}), bf16[8,1,128,768]{3,2,1,0:T(8,128)(2,1)S(1)}, u32[]{:S(2)}, u32[]{:S(2)}) async-start(bf16[8,1,128,768]{3,2,1,0:T(8,128)(2,1)} %bitcast.71), calls=%async_computation.4 | async-start | bytes 3145728 | tf_op jit(solution)/shard_map/all_to_all | solution.py:189
  379.0 31.7 %all-to-all-start.7 = ((bf16[8,1,128,768]{3,2,1,0:T(8,128)(2,1)}), bf16[8,1,128,768]{3,2,1,0:T(8,128)(2,1)S(1)}, u32[]{:S(2)}, u32[]{:S(2)}) async-start(bf16[8,1,128,768]{3,2,1,0:T(8,128)(2,1)} %fusion.110), calls=%async_computation.7 | async-start | bytes 3145728 | tf_op jit(solution)/shard_map/all_to_all | solution.py:211
  383.1 169.8 %reduce-scatter.17.cloned.1.call-start = ((), (), s32[]{:S(2)}) async-start(), calls=%async_computation.18 | async-start | bytes 245760
  410.6 25.3 %all-to-all-start.5 = ((bf16[8,1,128,768]{3,2,1,0:T(8,128)(2,1)}), bf16[8,1,128,768]{3,2,1,0:T(8,128)(2,1)S(1)}, u32[]{:S(2)}, u32[]{:S(2)}) async-start(bf16[8,1,128,768]{3,2,1,0:T(8,128)(2,1)} %fusion.115), calls=%async_computation.5 | async-start | bytes 3145728 | tf_op jit(solution)/shard_map/all_to_all | solution.py:211
  414.9 139.5 %reduce-scatter.15.cloned.1.call-start = ((), (), s32[]{:S(2)}) async-start(), calls=%async_computation.17 | async-start | bytes 983040
  416.4 277.5 %all-reduce.19.cloned.1.call-start = ((), (), s32[]{:S(2)}) async-start(), calls=%async_computation.19 | async-start | bytes 18874368
  506.3 275.2 %reduce-scatter.11.cloned.1.call-start = ((), (), s32[]{:S(2)}) async-start(), calls=%async_computation.15 | async-start | bytes 5898240 | tf_op jit(solution)/shard_map/reduce_scatter | solution.py:305
  525.3 344.3 %reduce-scatter.13.cloned.1.call-start = ((), (), s32[]{:S(2)}) async-start(), calls=%async_computation.16 | async-start | bytes 5898240 | tf_op jit(solution)/shard_map/reduce_scatter | solution.py:311
  563.8 48.7 %copy-start.22 = (f32[256,768]{1,0:T(8,128)S(1)}, f32[256,768]{1,0:T(8,128)}, u32[]{:S(2)}) copy-start(f32[256,768]{1,0:T(8,128)} %copy-done.21) | copy-start | bytes 2359300
  563.8 48.7 %copy-start.25 = (bf16[512,768]{1,0:T(8,128)(2,1)S(1)}, bf16[512,768]{1,0:T(8,128)(2,1)}, u32[]{:S(2)}) copy-start(bf16[512,768]{1,0:T(8,128)(2,1)} %param.26) | copy-start | bytes 2359300
  563.8 48.7 %copy-start.30 = (f32[256,768]{1,0:T(8,128)S(1)}, f32[256,768]{1,0:T(8,128)}, u32[]{:S(2)}) copy-start(f32[256,768]{1,0:T(8,128)} %copy-done.29) | copy-start | bytes 2359300
  563.8 48.7 %copy-start.108 = (f32[256]{0:T(256)S(1)}, f32[256]{0:T(256)}, u32[]{:S(2)}) copy-start(f32[256]{0:T(256)} %copy-done.105) | copy-start | bytes 3076
  563.8 48.7 %copy-start.112 = (f32[256]{0:T(256)S(1)}, f32[256]{0:T(256)}, u32[]{:S(2)}) copy-start(f32[256]{0:T(256)} %copy-done.109) | copy-start | bytes 3076
  563.8 48.7 %copy-start.131 = (f32[256]{0:T(256)S(1)}, f32[256]{0:T(256)}, u32[]{:S(2)}) copy-start(f32[256]{0:T(256)} %copy-done.128) | copy-start | bytes 3076
  563.8 48.7 %copy-start.135 = (f32[256]{0:T(256)S(1)}, f32[256]{0:T(256)}, u32[]{:S(2)}) copy-start(f32[256]{0:T(256)} %copy-done.132) | copy-start | bytes 3076
  563.9 48.7 %copy-start.137 = (f32[256]{0:T(256)S(1)}, f32[256]{0:T(256)}, u32[]{:S(2)}) copy-start(f32[256]{0:T(256)} %copy-done.136) | copy-start | bytes 3076
  563.9 48.7 %copy-start.139 = (f32[256]{0:T(256)S(1)}, f32[256]{0:T(256)}, u32[]{:S(2)}) copy-start(f32[256]{0:T(256)} %copy-done.138) | copy-start | bytes 3076
  613.4 81.4 %copy-start.60 = (f32[4,24,768]{2,1,0:T(8,128)S(1)}, f32[4,24,768]{2,1,0:T(8,128)}, u32[]{:S(2)}) copy-start(f32[4,24,768]{2,1,0:T(8,128)} %param.29) | copy-start | bytes 884740
  613.4 81.4 %copy-start.73 = (f32[4,24,768]{2,1,0:T(8,128)S(1)}, f32[4,24,768]{2,1,0:T(8,128)}, u32[]{:S(2)}) copy-start(f32[4,24,768]{2,1,0:T(8,128)} %param.36) | copy-start | bytes 884740
  613.4 81.4 %copy-start.74 = (f32[4,24,768]{2,1,0:T(8,128)S(1)}, f32[4,24,768]{2,1,0:T(8,128)}, u32[]{:S(2)}) copy-start(f32[4,24,768]{2,1,0:T(8,128)} %param.43) | copy-start | bytes 884740
  613.4 168.1 %copy-start.14 = (f32[1,768,768]{2,1,0:T(8,128)S(1)}, f32[1,768,768]{2,1,0:T(8,128)}, u32[]{:S(2)}) copy-start(f32[1,768,768]{2,1,0:T(8,128)} %param.32) | copy-start | bytes 7077892
  (150 other events, 695.1 us)
Sparse Core Ops, SparseCore 0:
  11.6 66.4 all-gather.5
  80.2 88.7 all-gather.7
  171.2 87.9 all-gather.9
  386.5 18.2 reduce-scatter.16
  417.9 22.2 reduce-scatter.14
  506.4 187.4 all-reduce.18
  696.1 85.3 reduce-scatter.10
  783.8 85.7 reduce-scatter.12
where the time goes:
time: 890 us; the launch traced here: 884 us
  waiting for transfers between devices  313 us (35%)
  matrix products  181 us (20%)
  blocking collectives  149 us (17%)
  local copies, waits for them, and re-layouts  126 us (14%)
  other arithmetic  64.1 us (7%)
  starting transfers between devices  33.9 us (4%)
  between operations  17.7 us (2%)
    reduce_scatter x1, waiting for transfers between devices, body(): lax.psum_scatter(grad_up.astype(jnp.bfloat16), 'dp', scatter_dimension=1,...  85.5 us
    reduce_scatter x1, waiting for transfers between devices, body(): lax.psum_scatter(grad_down.astype(jnp.bfloat16), 'dp', scatter_dimension=...  81.3 us
    unnamed x11, waiting for transfers between devices  77.9 us
    unnamed x2, blocking collectives  49.1 us
    all_gather x1, blocking collectives, body(): lax.all_gather(dense_local[1], ('dp', 'expert'), axis=1, tiled=True)  43.6 us
    all_gather x1, blocking collectives, body(): lax.all_gather(dense_local[2], ('dp', 'expert'), axis=1, tiled=True)  43.2 us
    all_gather x1, waiting for transfers between devices, body(): lax.all_gather(expert_local[2], 'dp', axis=1, tiled=True)  41.7 us
    dot_general x2, matrix products, body(): jnp.einsum('secd,efd->secf', arrived, down_b, preferred_element_type=f32)  31.1 us
  transfers between devices with their start and end apart: 16, of which 8 were waited for; matrix products, arithmetic and copies ran while one was open for 40% of the time, Pallas kernels for 0%

commit v1 on v0

v1 whole, which is shorter than its diff:
```python
import jax
import jax.numpy as jnp
from jax import lax
from jax.sharding import PartitionSpec as P

D = 768
HEADS = 12
HEAD_DIM = 64
LEN = 256
STEP = 3
ROWS = 256
BIAS_ROWS = 16

NORM_EPS = 1e-06
NEG_FILL = -1000000000.0
BETA_ONE = 0.9
BETA_TWO = 0.95
WEIGHT_DECAY = 0.1
ADAM_EPS = 1e-08
HIGHEST = lax.Precision.HIGHEST
GELU_C = 0.7978845608028654
GELU_K = 0.044715
f32 = jnp.float32
b16 = jnp.bfloat16


def norm_rows(values, gain, bias):
    center = values - jnp.mean(values, axis=-1, keepdims=True)
    spread = jnp.mean(center * center, axis=-1, keepdims=True)
    return center * lax.rsqrt(spread + NORM_EPS) * gain + bias


def gate_pair(picked):
    return jnp.stack(
        [jax.nn.sigmoid(picked[:, 0] - picked[:, 1]), jax.nn.sigmoid(picked[:, 1] - picked[:, 0])],
        axis=1,
    )


def adam_step(weight, grad, first, square, rate):
    new_first = BETA_ONE * first + (1.0 - BETA_ONE) * grad
    new_square = BETA_TWO * square + (1.0 - BETA_TWO) * grad * grad
    first_hat = new_first / (1.0 - BETA_ONE**STEP)
    square_hat = new_square / (1.0 - BETA_TWO**STEP)
    update = -rate * (first_hat / (jnp.sqrt(square_hat) + ADAM_EPS) + WEIGHT_DECAY * weight)
    return (weight + update, new_first, new_square)


def slots_of(routes, experts, capacity):
    flat = routes.reshape(-1, 2 * ROWS)
    onehot = (flat[:, :, None] == jnp.arange(experts, dtype=jnp.int32)).astype(b16)
    row = lax.broadcasted_iota(jnp.int32, (2 * ROWS, 2 * ROWS), 0)
    col = lax.broadcasted_iota(jnp.int32, (2 * ROWS, 2 * ROWS), 1)
    earlier = (col < row).astype(b16)
    before = jnp.einsum("ij,bje->bie", earlier, onehot, preferred_element_type=f32)
    slot = jnp.sum(before * onehot.astype(f32), axis=-1).astype(jnp.int32)
    return (flat * capacity + slot).reshape(-1, ROWS, 2)


def expert_chunk(x, dout, up, up_bias, down):
    pre = jnp.einsum("sd,fd->sf", x, up, preferred_element_type=f32) + up_bias
    inner = jnp.tanh(GELU_C * (pre + GELU_K * pre * pre * pre))
    hidden = (0.5 * pre * (1.0 + inner)).astype(b16)
    slope = 0.5 * (1.0 + inner) + 0.5 * pre * (1.0 - inner * inner) * (
        GELU_C * (1.0 + 3.0 * GELU_K * pre * pre)
    )
    out = jnp.einsum("sf,fd->sd", hidden, down, preferred_element_type=f32)
    grad_down = jnp.einsum("sf,sd->fd", hidden, dout, preferred_element_type=f32)
    grad_hidden = jnp.einsum("sd,fd->sf", dout, down, preferred_element_type=f32)
    grad_pre = (slope * grad_hidden).astype(b16)
    grad_up = jnp.einsum("sf,sd->fd", grad_pre, x, preferred_element_type=f32)
    grad_up_bias = jnp.sum(grad_pre.astype(f32), axis=0)
    grad_x = jnp.einsum("sf,fd->sd", grad_pre, up, preferred_element_type=f32)
    return out, grad_x, grad_up, grad_up_bias, grad_down


def pack_expert(up, down, up_bias, down_bias, dtype):
    part = up.shape[0]
    tail = jnp.zeros((BIAS_ROWS, D), dtype)
    tail = tail.at[0, :part].set(up_bias.astype(dtype))
    tail = tail.at[1, : down_bias.shape[0]].set(down_bias.astype(dtype))
    return jnp.concatenate([up.astype(dtype), down.astype(dtype), tail], axis=0)


def shift(x, step, least):
    n = lax.axis_size("dp")
    if step > 0:
        pairs = [(i, i + 1) for i in range(least, n - 1)]
    else:
        pairs = [(i, i - 1) for i in range(1, n - least)]
    return lax.ppermute(x, "dp", pairs)


def body(
    tokens, out_grad, routes, lengths,
    attention, gain_bias, router, expert_up, up_bias, expert_down, down_bias,
    first_attention, first_gain_bias, first_router, first_expert_up, first_up_bias, first_expert_down, first_down_bias,
    square_attention, square_gain_bias, square_router, square_expert_up, square_up_bias, square_expert_down, square_down_bias,
):
    experts = router.shape[0]
    capacity = 4 * ROWS // experts
    count = tokens.shape[0]
    blocks = count // ROWS
    seqs = count // LEN
    part = expert_up.shape[1]
    narrow = down_bias.shape[1]
    cols = attention.shape[1]
    devices = D // cols
    n_dp = lax.axis_size("dp")
    assert n_dp == 4 and expert_up.shape[0] == 1
    me = lax.axis_index("dp")
    mine = lax.axis_index("expert")
    scale = HEAD_DIM ** (-0.5)
    both = ("dp", "expert")

    own = pack_expert(expert_up[0], expert_down[0], up_bias[0], down_bias[0], b16)
    right, left = [own], [own]
    for step in range(n_dp - 1):
        right.append(shift(right[-1], 1, step))
        left.append(shift(left[-1], -1, step))

    flat_len = (7 + experts) * cols
    extra = -(-flat_len // D)
    small = jnp.concatenate([gain_bias, router], axis=0).astype(b16).reshape(-1)
    small = jnp.pad(small, (0, extra * D - flat_len)).reshape(extra, D)
    packed = jnp.concatenate([attention.astype(b16).reshape(4 * cols, D), small], axis=0)
    whole = lax.all_gather(packed, both, axis=0, tiled=False)
    weights_b = whole[:, : 4 * cols].reshape(devices, 4, cols, D).transpose(1, 0, 2, 3).reshape(4, D, D)
    small = whole[:, 4 * cols :].reshape(devices, extra * D)[:, :flat_len].reshape(devices, 7 + experts, cols)
    small = small.transpose(1, 0, 2).reshape(7 + experts, D)
    vector = small[:7].astype(f32)
    router_b = small[7:]

    positions = slots_of(routes, experts, capacity)
    slot_ids = jnp.arange(experts * capacity, dtype=jnp.int32)
    hit = positions[:, :, :, None] == slot_ids
    choose = hit.astype(b16)
    both_choose = choose[:, :, 0] + choose[:, :, 1]
    split = both_choose.reshape(blocks, ROWS, experts, capacity)
    other = jnp.flip(routes, axis=1).reshape(blocks, ROWS, 2)
    partner = jnp.sum(jnp.where(hit, other[:, :, :, None], 0), axis=(1, 2)).astype(f32)
    partner = partner.reshape(blocks, experts, capacity).transpose(1, 0, 2)
    partner = lax.all_to_all(partner, "expert", split_axis=0, concat_axis=0, tiled=True)
    grad_rows = out_grad.reshape(blocks, ROWS, D)

    def dispatch(rows):
        sent = jnp.einsum("btec,btd->ebcd", split, rows, preferred_element_type=f32).astype(b16)
        got = lax.all_to_all(sent, "expert", split_axis=0, concat_axis=0, tiled=True)
        return got.reshape(experts * blocks * capacity, D)

    grad_slots = dispatch(grad_rows)

    head_shape = (seqs, LEN, HEADS, HEAD_DIM)
    rows_in = tokens.astype(f32)
    grad_out = out_grad.astype(f32)
    normed_one_b = norm_rows(rows_in, vector[0], vector[1]).astype(b16)
    proj = jnp.einsum("rd,jde->jre", normed_one_b, weights_b[:3], preferred_element_type=f32)
    queries = (proj[0] + vector[2]).astype(b16).reshape(head_shape)
    key_rows = proj[1].astype(b16).reshape(head_shape)
    values = (proj[2] + vector[3]).astype(b16).reshape(head_shape)
    valid = (jnp.arange(LEN, dtype=jnp.int32)[None, :] < lengths[:, None])[:, None, None, :]
    scores = jnp.einsum("bqhe,bkhe->bhqk", queries, key_rows, preferred_element_type=f32) * scale
    scores = jnp.where(valid, scores, NEG_FILL)
    top_score = jnp.max(scores, axis=-1, keepdims=True)
    log_total = top_score + jnp.log(jnp.sum(jnp.exp(scores - top_score), axis=-1, keepdims=True))
    chance_b = jnp.exp(scores - log_total).astype(b16)
    context_b = (
        jnp.einsum("bhqk,bkhe->bqhe", chance_b, values, preferred_element_type=f32)
        .astype(b16)
        .reshape(count, D)
    )
    resid = rows_in + (jnp.dot(context_b, weights_b[3], preferred_element_type=f32) + vector[4])
    normed_two_b = norm_rows(resid, vector[5], vector[6]).astype(b16)
    slots_in = dispatch(normed_two_b.reshape(blocks, ROWS, D))
    logits = jnp.einsum("rd,ed->re", normed_two_b, router_b, preferred_element_type=f32)
    chooser = (routes[:, :, None] == jnp.arange(experts, dtype=jnp.int32)).astype(f32)
    picked = jnp.sum(logits[:, None, :] * chooser, axis=-1)
    gates = gate_pair(picked)

    slot_logits = jnp.einsum("sd,ed->se", slots_in, router_b, preferred_element_type=f32)
    ids = jnp.arange(experts, dtype=jnp.int32)
    rival = partner.reshape(-1).astype(jnp.int32)
    margin = jnp.sum(
        slot_logits * ((ids == mine).astype(f32) - (rival[:, None] == ids).astype(f32)), axis=-1
    )
    dout = (jax.nn.sigmoid(margin)[:, None] * grad_slots.astype(f32)).astype(b16)
    grad_down_bias = jnp.sum(dout.astype(f32), axis=0)

    def pick(*arrays):
        out = arrays[-1]
        for i in range(len(arrays) - 2, -1, -1):
            out = jnp.where(me == i, arrays[i], out)
        return out

    parts = [
        own,
        pick(left[1], right[1], left[1], right[1]),
        pick(left[2], left[1], right[1], right[2]),
        pick(left[3], left[2], right[2], right[3]),
    ]
    names = [
        me,
        pick(1, 0, 3, 2),
        pick(2, 2, 1, 1),
        pick(3, 3, 0, 0),
    ]
    out_slots = jnp.zeros((slots_in.shape[0], D), f32)
    grad_slots_in = jnp.zeros((slots_in.shape[0], D), f32)
    part_grads = []
    bias_rows = []
    for packed_part, name in zip(parts, names):
        up, down, tail = packed_part[:part], packed_part[part : 2 * part], packed_part[2 * part :]
        out, grad_x, grad_up, grad_up_bias, grad_down = expert_chunk(
            slots_in, dout, up, tail[0, :part].astype(f32), down
        )
        out_slots = out_slots + out
        grad_slots_in = grad_slots_in + grad_x
        bias_rows.append(tail[1, :narrow])
        part_grads.append(
            (
                grad_up,
                grad_down,
                grad_up_bias,
                lax.dynamic_slice(grad_down_bias, (name * narrow,), (narrow,)),
            )
        )
    place = jnp.stack(names)
    down_bias_full = jnp.zeros((n_dp, narrow), b16).at[place].set(jnp.stack(bias_rows)).reshape(D)
    out_b = (out_slots + down_bias_full.astype(f32)).astype(b16)
    grad_b = grad_slots_in.astype(b16)

    def give_back(rows):
        sent = rows.reshape(experts, blocks, capacity, D)
        got = lax.all_to_all(sent, "expert", split_axis=0, concat_axis=0, tiled=True)
        return got.transpose(1, 0, 2, 3).reshape(blocks, experts * capacity, D)

    back = give_back(out_b)
    returned = give_back(grad_b)

    packs = [pack_expert(g[0], g[1], g[2], g[3], b16) for g in part_grads]
    zero = jnp.zeros_like(packs[0])
    ahead = [pick(p, q, r, s) for p, q, r, s in (
        (packs[1], packs[2], packs[1], zero),
        (packs[2], packs[3], zero, zero),
        (packs[3], zero, zero, zero),
    )]
    behind = [pick(p, q, r, s) for p, q, r, s in (
        (zero, packs[1], packs[2], packs[1]),
        (zero, zero, packs[3], packs[2]),
        (zero, zero, zero, packs[3]),
    )]
    going, coming = None, None
    for offset in range(n_dp - 1, 0, -1):
        send = ahead[offset - 1]
        if going is not None:
            send = (send.astype(f32) + going.astype(f32)).astype(b16)
        n = n_dp
        going = lax.ppermute(send, "dp", [(i, i + 1) for i in range(n - offset)])
        send = behind[offset - 1]
        if coming is not None:
            send = (send.astype(f32) + coming.astype(f32)).astype(b16)
        coming = lax.ppermute(send, "dp", [(i, i - 1) for i in range(offset, n)])
    arrived = going.astype(f32) + coming.astype(f32)
    mine_up, mine_down, mine_up_bias, mine_down_bias = part_grads[0]
    shard_up = (mine_up + arrived[:part])[None]
    shard_down = (mine_down + arrived[part : 2 * part])[None]
    shard_up_bias = (mine_up_bias + arrived[2 * part, :part])[None]
    shard_down_bias = (mine_down_bias + arrived[2 * part + 1, :narrow])[None]

    expert_out = jnp.einsum("btks,bsd->kbtd", choose, back, preferred_element_type=f32)
    expert_out = expert_out.reshape(2, count, D)
    output = resid + gates[:, 0:1] * expert_out[0] + gates[:, 1:2] * expert_out[1]
    gate_grad = jnp.stack([jnp.sum(grad_out * expert_out[k], axis=-1) for k in range(2)], axis=1)
    pair_back = jax.vjp(gate_pair, picked)[1]
    grad_picked = pair_back(gate_grad)[0]
    grad_logits = jnp.sum(grad_picked[:, :, None] * chooser, axis=1)
    grad_router = jnp.einsum("re,rd->ed", grad_logits, normed_two_b.astype(f32), precision=HIGHEST)
    grad_normed = jnp.einsum("bts,bsd->btd", both_choose, returned, preferred_element_type=f32)
    grad_normed = grad_normed.reshape(count, D) + jnp.dot(
        grad_logits, router_b.astype(f32), precision=HIGHEST
    )
    norm_back_two = jax.vjp(norm_rows, resid, vector[5], vector[6])[1]
    grad_from_norm, grad_gain_two, grad_bias_two = norm_back_two(grad_normed)
    grad_resid = grad_out + grad_from_norm
    grad_branch_b = grad_resid.astype(b16)
    grad_out_proj = jnp.einsum("rd,re->de", context_b, grad_branch_b, preferred_element_type=f32)
    grad_context_b = (
        jnp.einsum("re,de->rd", grad_branch_b, weights_b[3], preferred_element_type=f32)
        .astype(b16)
        .reshape(head_shape)
    )
    scores = jnp.einsum("bqhe,bkhe->bhqk", queries, key_rows, preferred_element_type=f32) * scale
    scores = jnp.where(valid, scores, NEG_FILL)
    chance = jnp.exp(scores - log_total)
    chance_b = chance.astype(b16)
    grad_values = jnp.einsum(
        "bhqk,bqhe->bkhe", chance_b, grad_context_b, preferred_element_type=f32
    ).astype(b16)
    grad_chance = jnp.einsum("bqhe,bkhe->bhqk", grad_context_b, values, preferred_element_type=f32)
    grad_scores_b = (
        chance * (grad_chance - jnp.sum(chance * grad_chance, axis=-1, keepdims=True))
    ).astype(b16)
    grad_queries = (
        jnp.einsum("bhqk,bkhe->bqhe", grad_scores_b, key_rows, preferred_element_type=f32) * scale
    ).astype(b16)
    grad_keys = (
        jnp.einsum("bhqk,bqhe->bkhe", grad_scores_b, queries, preferred_element_type=f32) * scale
    ).astype(b16)
    grad_proj = jnp.stack([g.reshape(count, D) for g in (grad_queries, grad_keys, grad_values)])
    grad_in_proj = jnp.einsum("rd,jre->jde", normed_one_b, grad_proj, preferred_element_type=f32)
    grad_weights = jnp.concatenate([grad_in_proj, grad_out_proj[None]], axis=0)
    grad_normed_one = jnp.einsum("jre,jde->rd", grad_proj, weights_b[:3], preferred_element_type=f32)
    norm_back_one = jax.vjp(norm_rows, rows_in, vector[0], vector[1])[1]
    grad_from_first, grad_gain_one, grad_bias_one = norm_back_one(grad_normed_one)
    grad_vector = jnp.stack(
        [
            grad_gain_one,
            grad_bias_one,
            jnp.sum(grad_proj[0], axis=0, dtype=f32),
            jnp.sum(grad_proj[2], axis=0, dtype=f32),
            jnp.sum(grad_branch_b, axis=0, dtype=f32),
            grad_gain_two,
            grad_bias_two,
        ]
    )
    input_grad = grad_resid + grad_from_first

    small = jnp.concatenate([grad_vector, grad_router], axis=0).reshape(7 + experts, devices, cols)
    small = jnp.pad(small.transpose(1, 0, 2).reshape(devices, flat_len), ((0, 0), (0, extra * D - flat_len)))
    big = grad_weights.reshape(4, devices, cols, D).transpose(1, 0, 2, 3).reshape(devices, 4 * cols, D)
    packed = jnp.concatenate([big, small.reshape(devices, extra, D)], axis=1).astype(b16)
    packed = lax.psum_scatter(packed, both, scatter_dimension=0, tiled=False).astype(f32)
    shard_weights = packed[: 4 * cols].reshape(4, cols, D)
    small = packed[4 * cols :].reshape(extra * D)[:flat_len].reshape(7 + experts, cols)
    shard_vector, shard_router = small[:7], small[7:]

    params = (attention, gain_bias, router, expert_up, up_bias, expert_down, down_bias)
    grads = (shard_weights, shard_vector, shard_router, shard_up, shard_up_bias, shard_down, shard_down_bias)
    firsts = (first_attention, first_gain_bias, first_router, first_expert_up, first_up_bias, first_expert_down, first_down_bias)
    squares = (square_attention, square_gain_bias, square_router, square_expert_up, square_up_bias, square_expert_down, square_down_bias)
    hidden_units = n_dp * part
    rates = (1.6 * D ** (-0.5), 0.3, 0.5 * D ** (-0.5), 1.5 * D ** (-0.5), 0.25, 0.5 * hidden_units ** (-0.5), 0.25)
    updated = [adam_step(params[i], grads[i], firsts[i], squares[i], rates[i]) for i in range(7)]
    return (output, input_grad, *grads, *(u[0] for u in updated), *(u[1] for u in updated), *(u[2] for u in updated))


def solution(mesh):
    rows = P(("dp", "expert"), None)
    state = (
        P(None, ("dp", "expert"), None),
        P(None, ("dp", "expert")),
        P(None, ("dp", "expert")),
        P("expert", "dp", None),
        P("expert", "dp"),
        P("expert", "dp", None),
        P("expert", "dp"),
    )
    return jax.shard_map(
        body,
        mesh=mesh,
        in_specs=(rows, rows, rows, P(("dp", "expert")), *state, *state, *state),
        out_specs=(rows, rows, *state, *state, *state, *state),
        check_vma=False,
    )
```

time: 890 us -> 652 us (0.73)
  blocking collectives: 149 us -> 0 us
  waiting for transfers between devices: 313 us -> 215 us
  local copies, waits for them, and re-layouts: 126 us -> 98.1 us
  starting transfers between devices: 33.9 us -> 51.2 us
  other arithmetic: 64.1 us -> 75.8 us
    ppermute x0 -> x12, waiting for transfers between devices: none -> 136 us  [the longest x6 97.3 us: shift(): return lax.ppermute(x, 'dp', pairs)]
    reduce_scatter x2 -> x1, waiting for transfers between devices: 167 us -> 34.9 us  [body(): lax.psum_scatter(packed, both, scatter_dimension=0, tiled=False).astype(f32)]
    all_gather x3 -> x0, blocking collectives: 100 us -> none  [the longest x1 43.6 us: body(): lax.all_gather(dense_local[1], ('dp', 'expert'), axis=1, tiled=True)]
    unnamed x11 -> x2, waiting for transfers between devices: 77.9 us -> 0.03 us
    all_gather x3 -> x1, waiting for transfers between devices: 49.7 us -> 0.02 us  [body(): whole = lax.all_gather(packed, both, axis=0, tiled=False)]
    unnamed x2 -> x0, blocking collectives: 49.1 us -> none
    gather x8 -> x0, local copies, waits for them, and re-layouts: 31.1 us -> none  [the longest x2 10.4 us: body(): send = padded_two[table // 2].reshape(senders, local_count, capacity, D)]
    ppermute x0 -> x12, starting transfers between devices: none -> 28.5 us  [the longest x6 14.6 us: shift(): return lax.ppermute(x, 'dp', pairs)]
  transfers between devices with their start and end apart: 16 -> 19, of which waited for: 8 -> 10; matrix products, arithmetic and copies ran while one was open for 40% -> 42% of each run, Pallas kernels for 0% -> 0%
where the time goes in v1:
time: 652 us; the launch traced here: 643 us
  waiting for transfers between devices  215 us (33%)
  matrix products  186 us (29%)
  local copies, waits for them, and re-layouts  98.1 us (15%)
  other arithmetic  75.8 us (12%)
  starting transfers between devices  51.2 us (8%)
  between operations  16.5 us (3%)
    ppermute x6, waiting for transfers between devices, shift(): return lax.ppermute(x, 'dp', pairs)  97.3 us
    reduce_scatter x1, waiting for transfers between devices, body(): lax.psum_scatter(packed, both, scatter_dimension=0, tiled=False).astype(f32)  34.9 us
    ppermute x3, waiting for transfers between devices, body(): going = lax.ppermute(send, 'dp', [(i, i + 1) for i in range(n - offset)])  33.3 us
    dot_general x4, matrix products, expert_chunk(): jnp.einsum('sf,sd->fd', hidden, dout, preferred_element_type=f32)  31.7 us
    dot_general x4, matrix products, expert_chunk(): out = jnp.einsum('sf,fd->sd', hidden, down, preferred_element_type=f32)  30 us
    dot_general x4, matrix products, expert_chunk(): jnp.einsum('sd,fd->sf', dout, down, preferred_element_type=f32)  28.7 us
    all_to_all x2, waiting for transfers between devices, give_back(): lax.all_to_all(sent, 'expert', split_axis=0, concat_axis=0, tiled=True)  25.2 us
    concatenate x15, local copies, waits for them, and re-layouts, body(): jnp.concatenate([grad_vector, grad_router], axis=0)  22.8 us
  transfers between devices with their start and end apart: 19, of which 10 were waited for; matrix products, arithmetic and copies ran while one was open for 42% of the time, Pallas kernels for 0%

profile of v1, /device:TPU:0, one launch (start us, length us, event | category | flops | bytes accessed | tf_op | source)
XLA Modules:
  0.0 643.0 jit_solution(5074114862023815960)
XLA Ops:
  16.9 6.3 collective-permute-start.1
  27.1 3.9 all-to-all-start.2
  35.4 61.7 %collective-permute-done.1 = bf16[1552,768]{1,0:T(8,128)(2,1)} collective-permute-done((bf16[1552,768]{1,0:T(8,128)(2,1)}, bf16[1552,768]{1,0:T(8,128)(2,1)}, u32[]{:S(2)}, u32[]{:S(2)}) %collective-permute-start.1) | collective-permute-done | bytes 2383904 | tf_op jit(solution)/shard_map/ppermute | solution.py:91
  123.3 3.6 squeeze.12
  140.8 4.6 all-to-all-start
  147.6 9.8 %collective-permute-done.2 = bf16[1552,768]{1,0:T(8,128)(2,1)} collective-permute-done((bf16[1552,768]{1,0:T(8,128)(2,1)}, bf16[1552,768]{1,0:T(8,128)(2,1)}, u32[]{:S(2)}, u32[]{:S(2)}) %collective-permute-start.2) | collective-permute-done | bytes 2383904 | tf_op jit(solution)/shard_map/ppermute | solution.py:91
  164.5 18.9 %all-to-all-done = bf16[8,2,128,768]{2,3,1,0:T(8,128)(2,1)} async-done(((bf16[8,2,128,768]{2,3,1,0:T(8,128)(2,1)}), bf16[8,2,128,768]{2,3,1,0:T(8,128)(2,1)}, u32[]{:S(2)}, u32[]{:S(2)}) %all-to-all-start) | async-done | bytes 3145760 | tf_op jit(solution)/shard_map/all_to_all | solution.py:148
  183.3 4.4 all-to-all-start.3
  187.9 23.4 %collective-permute-done.4 = bf16[1552,768]{1,0:T(8,128)(2,1)} collective-permute-done((bf16[1552,768]{1,0:T(8,128)(2,1)}, bf16[1552,768]{1,0:T(8,128)(2,1)}, u32[]{:S(2)}, u32[]{:S(2)}) %collective-permute-start.4) | collective-permute-done | bytes 2383904 | tf_op jit(solution)/shard_map/ppermute | solution.py:91
  211.3 5.5 select_select_fusion.3
  227.6 3.2 copy.193
  231.8 5.8 fusion.79
  241.4 4.5 convolution_convert_fusion.1
  245.9 7.4 %fusion.167 = (bf16[768]{0:T(1024)(128)(2,1)S(1)}, bf16[2048,768]{1,0:T(8,128)(2,1)S(1)}) fusion(bf16[2048,768]{1,0:T(8,128)(2,1)S(1)} %fusion.32, bf16[1552,768]{1,0:T(8,128)(2,1)} %copy-done.24, f32[2048,768]{1,0:T(8,128)S(1)} %copy-done.138, f32[768]{0:T(1024)S(1)} %copy-done.122), kind=kOutput, calls=%fused_computation.309 | convolution fusion | flops 2448948480 | bytes 13767168 | tf_op jit(solution)/shard_map/sd,fd->sf/dot_general | solution.py:69
  256.0 4.5 convolution_convert_fusion.3
  260.6 7.1 %fusion.168 = (bf16[768]{0:T(1024)(128)(2,1)S(1)}, bf16[2048,768]{1,0:T(8,128)(2,1)}) fusion(bf16[2048,768]{1,0:T(8,128)(2,1)S(1)} %fusion.32, bf16[1552,768]{1,0:T(8,128)(2,1)S(1)} %copy-done.43, f32[2048,768]{1,0:T(8,128)S(1)} %fusion.86, f32[768]{0:T(1024)S(1)} %copy-done.123), kind=kOutput, calls=%fused_computation.310 | convolution fusion | flops 2448948480 | bytes 13768192 | tf_op jit(solution)/shard_map/sd,fd->sf/dot_general | solution.py:69
  267.6 5.9 fusion.82
  276.3 7.5 %fusion.169 = (bf16[768]{0:T(1024)(128)(2,1)S(1)}, bf16[2048,768]{1,0:T(8,128)(2,1)}) fusion(bf16[2048,768]{1,0:T(8,128)(2,1)S(1)} %fusion.32, bf16[1552,768]{1,0:T(8,128)(2,1)S(1)} %copy-done.41, f32[2048,768]{1,0:T(8,128)S(1)} %fusion.93, f32[768]{0:T(1024)S(1)} %copy-done.120), kind=kOutput, calls=%fused_computation.311 | convolution fusion | flops 2448948480 | bytes 13768192 | tf_op jit(solution)/shard_map/sd,fd->sf/dot_general | solution.py:69
  283.8 5.8 fusion.89
  289.6 4.3 convert_reduce_fusion.1
  294.5 3.7 convolution_convert_fusion.2
  298.4 4.2 broadcast_select_fusion
  307.5 4.0 fusion.84
  311.6 4.0 fusion.91
  315.7 5.5 multiply_convert_fusion.5
  321.2 6.8 %convert_reduce_fusion = (f32[768]{0:T(1024)}, bf16[2048,768]{1,0:T(8,128)(2,1)S(1)}) fusion(bf16[2048,768]{1,0:T(8,128)(2,1)S(1)} %bitcast.272, bf16[768,768]{1,0:T(8,128)(2,1)S(1)} %copy-done.26, f32[2048,768]{1,0:T(8,128)S(1)} %get-tuple-element.210, f32[768]{0:T(1024)S(1)} %copy-done.121), kind=kOutput, calls=%fused_computation.43 | convolution fusion | flops 2450521344 | bytes 13768704 | tf_op jit(solution)/shard_map/sd,fd->sf/dot_general | solution.py:69
  332.3 7.4 %add_convert_fusion = bf16[2048,768]{1,0:T(8,128)(2,1)} fusion(f32[2048,768]{1,0:T(8,128)S(1)} %fusion.84, f32[2048,768]{1,0:T(8,128)S(1)} %fusion.172, f32[2048,768]{1,0:T(8,128)S(1)} %fusion.91, bf16[2048,768]{1,0:T(8,128)(2,1)} %copy-done.36, bf16[1552,768]{1,0:T(8,128)(2,1)} %copy-done.24), kind=kOutput, calls=%fused_computation.47 | convolution fusion | flops 2422210560 | bytes 26345472 | tf_op jit(solution)/shard_map/sf,fd->sd/dot_general | solution.py:73
  339.7 4.7 all-to-all-start.4
  344.4 4.9 fusion.171
  349.4 13.4 %add_convert_fusion.1 = bf16[2048,768]{1,0:T(8,128)(2,1)} fusion(f32[2048,768]{1,0:T(8,128)} %fusion.82, f32[2048,768]{1,0:T(8,128)S(1)} %fusion.171, f32[2048,768]{1,0:T(8,128)} %fusion.89, f32[768]{0:T(1024)S(1)} %copy-done.124, bf16[1552,768]{1,0:T(8,128)(2,1)} %copy-done.24, f32[2048,768]{1,0:T(8,128)} %fusion.79, f32[768]{0:T(1024)S(1)} %copy-done.122), kind=kOutput, calls=%fused_computation.49 | convolution fusion | flops 2439512064 | bytes 29497344 | tf_op jit(solution)/shard_map/sf,fd->sd/dot_general | solution.py:67
  362.7 3.7 convolution_convert_fusion.4
  366.5 15.9 %all-to-all-done.4 = bf16[8,2,128,768]{3,2,1,0:T(8,128)(2,1)} async-done(((bf16[8,2,128,768]{3,2,1,0:T(8,128)(2,1)}), bf16[8,2,128,768]{3,2,1,0:T(8,128)(2,1)}, u32[]{:S(2)}, u32[]{:S(2)}) %all-to-all-start.4) | async-done | bytes 3145760 | tf_op jit(solution)/shard_map/all_to_all | solution.py:234
  382.3 4.4 all-to-all-start.1
  387.3 5.5 convolution_convert_fusion.6
  393.5 8.3 %convolution_convert_fusion.5 = bf16[768,768]{1,0:T(8,128)(2,1)} fusion(bf16[2048,768]{1,0:T(8,128)(2,1)} %copy-done.37, f32[2048,768]{1,0:T(8,128)} %copy-done.137, f32[768]{0:T(1024)S(1)} %copy-done.120), kind=kOutput, calls=%fused_computation.146 | convolution fusion | flops 2432237568 | bytes 10619904 | tf_op jit(solution)/shard_map/sf,sd->fd/dot_general | solution.py:68
  401.8 5.2 add_convert_fusion.5
  415.3 9.3 %all-to-all-done.1 = bf16[8,2,128,768]{3,2,1,0:T(8,128)(2,1)} async-done(((bf16[8,2,128,768]{3,2,1,0:T(8,128)(2,1)}), bf16[8,2,128,768]{3,2,1,0:T(8,128)(2,1)}, u32[]{:S(2)}, u32[]{:S(2)}) %all-to-all-start.1) | async-done | bytes 3145760 | tf_op jit(solution)/shard_map/all_to_all | solution.py:234
  444.0 5.5 fusion.166
  465.9 5.4 bitcast_reduce_fusion
  494.0 3.4 convolution_convert_fusion.11
  497.4 3.6 concatenate.96
  511.8 5.4 add_convert_fusion.4
  525.8 6.1 fusion.173
  533.8 33.3 %collective-permute-done.8 = bf16[1552,768]{1,0:T(8,128)(2,1)} collective-permute-done((bf16[1552,768]{1,0:T(8,128)(2,1)}, bf16[1552,768]{1,0:T(8,128)(2,1)}, u32[]{:S(2)}, u32[]{:S(2)}) %collective-permute-start.8) | collective-permute-done | bytes 2383904 | tf_op jit(solution)/shard_map/ppermute | solution.py:258
  567.1 5.5 collective-permute-done.11
  577.5 14.3 %multiply_add_fusion.4 = (f32[1,768,768]{2,1,0:T(8,128)}, f32[1,768,768]{2,1,0:T(8,128)}, f32[1,768,768]{2,1,0:T(8,128)}, f32[1,768,768]{2,1,0:T(8,128)}, f32[1,...) fusion(f32[1,768,768]{2,1,0:T(8,128)} %param.50, f32[1552,768]{1,0:T(8,128)S(1)} %convert_add_fusion, ...), kind=kOutput, calls=%fused_computation.108 | convolution fusion | flops 2434793472 | bytes 44040192 | tf_op jit(solution)/shard_map/sf,sd->fd/dot_general | solution.py:68
  592.0 4.6 fusion.147
  596.5 34.9 %reduce-scatter.2.cloned.1.call-done = bf16[1,97,768]{2,1,0:T(8,128)(2,1)} async-done(((bf16[32,97,768]{2,1,0:T(8,128)(2,1)}), bf16[1,97,768]{2,1,0:T(8,128)(2,1)}) %reduce-scatter.2.cloned.1.call-update) | async-done | bytes 149008 | tf_op jit(solution)/shard_map/reduce_scatter | solution.py:332
  (490 shorter events, 195.3 us)
Async XLA Ops:
  7.2 95.7 %all-gather.4.cloned.1.call-start = ((), (), s32[]{:S(2)}) async-start(), calls=%async_computation.7 | async-start | bytes 5271552 | tf_op jit(solution)/shard_map/all_gather | solution.py:127
  16.9 80.2 %collective-permute-start.1 = (bf16[1552,768]{1,0:T(8,128)(2,1)}, bf16[1552,768]{1,0:T(8,128)(2,1)}, u32[]{:S(2)}, u32[]{:S(2)}) collective-permute-start(bf16[1552,768]{1,0:T(8,128)(2,1)} %pad_maximum_fusion.2), channel_id=1, source_target_pairs={{0,8},{8,16},{16,24},{1,9},{9,17},{17,25},{2,10},{10,18},{18,26},{... | collective-permute-start | bytes 7151624 | tf_op jit(solution)/shard_map/ppermute | solution.py:91
  23.3 78.3 %collective-permute-start = (bf16[1552,768]{1,0:T(8,128)(2,1)}, bf16[1552,768]{1,0:T(8,128)(2,1)}, u32[]{:S(2)}, u32[]{:S(2)}) collective-permute-start(bf16[1552,768]{1,0:T(8,128)(2,1)} %pad_maximum_fusion.2), channel_id=1, source_target_pairs={{8,0},{16,8},{24,16},{9,1},{17,9},{25,17},{10,2},{18,10},{26,18},{... | collective-permute-start | bytes 7151624 | tf_op jit(solution)/shard_map/ppermute | solution.py:91
  27.1 113.8 %all-to-all-start.2 = ((f32[8,2,128]{2,1,0:T(2,128)}), f32[8,2,128]{2,1,0:T(2,128)}, u32[]{:S(2)}, u32[]{:S(2)}) async-start(f32[8,2,128]{2,1,0:T(2,128)} %convert_bitcast_fusion.5), calls=%async_computation.2 | async-start | bytes 16384 | tf_op jit(solution)/shard_map/all_to_all | solution.py:143
  32.9 72.6 %copy-start.15 = (bf16[2,256,1,1024]{3,1,0,2:T(8,128)(2,1)}, bf16[2,256,1,1024]{3,1,0,2:T(8,128)(2,1)S(1)}, u32[]{:S(2)}) copy-start(bf16[2,256,1,1024]{3,1,0,2:T(8,128)(2,1)S(1)} %slice_add_fusion.2) | copy-start | bytes 3145732
  34.4 78.4 %copy-start.91 = (f32[512]{0:T(512)}, f32[512]{0:T(512)S(1)}, u32[]{:S(2)}) copy-start(f32[512]{0:T(512)S(1)} %broadcast_multiply_fusion.2) | copy-start | bytes 6148
  34.8 70.8 %copy-start.99 = (f32[512]{0:T(512)}, f32[512]{0:T(512)S(1)}, u32[]{:S(2)}) copy-start(f32[512]{0:T(512)S(1)} %fusion.56) | copy-start | bytes 6148
  35.4 77.4 %copy-start.97 = (f32[512]{0:T(512)}, f32[512]{0:T(512)S(1)}, u32[]{:S(2)}) copy-start(f32[512]{0:T(512)S(1)} %fusion.135) | copy-start | bytes 6148
  97.2 48.3 %collective-permute-start.3 = (bf16[1552,768]{1,0:T(8,128)(2,1)}, bf16[1552,768]{1,0:T(8,128)(2,1)}, u32[]{:S(2)}, u32[]{:S(2)}) collective-permute-start(bf16[1552,768]{1,0:T(8,128)(2,1)} %collective-permute-done.1), channel_id=1, source_target_pairs={{8,16},{16,24},{9,17},{17,25},{10,18},{18,26},{11,19},{19,27},{12,... | collective-permute-start | bytes 7151624 | tf_op jit(solution)/shard_map/ppermute | solution.py:91
  101.6 55.8 %collective-permute-start.2 = (bf16[1552,768]{1,0:T(8,128)(2,1)}, bf16[1552,768]{1,0:T(8,128)(2,1)}, u32[]{:S(2)}, u32[]{:S(2)}) collective-permute-start(bf16[1552,768]{1,0:T(8,128)(2,1)} %collective-permute-done), channel_id=1, source_target_pairs={{8,0},{16,8},{9,1},{17,9},{10,2},{18,10},{11,3},{19,11},{12,4},{20... | collective-permute-start | bytes 7151624 | tf_op jit(solution)/shard_map/ppermute | solution.py:91
  117.3 107.7 %copy-start.73 = (f32[768]{0:T(1024)}, f32[768]{0:T(1024)S(1)}, u32[]{:S(2)}) copy-start(f32[768]{0:T(1024)S(1)} %mul.667) | copy-start | bytes 9220
  136.0 89.0 %copy-start.1 = (f32[512,768]{1,0:T(8,128)}, f32[512,768]{1,0:T(8,128)S(1)}, u32[]{:S(2)}) copy-start(f32[512,768]{1,0:T(8,128)S(1)} %get-tuple-element.208) | copy-start | bytes 4718596
  140.8 42.5 %all-to-all-start = ((bf16[8,2,128,768]{2,3,1,0:T(8,128)(2,1)}), bf16[8,2,128,768]{2,3,1,0:T(8,128)(2,1)}, u32[]{:S(2)}, u32[]{:S(2)}) async-start(bf16[8,2,128,768]{2,3,1,0:T(8,128)(2,1)} %copy.192), calls=%async_computation | async-start | bytes 6291456 | tf_op jit(solution)/shard_map/all_to_all | solution.py:148
  145.5 42.4 %collective-permute-start.5 = (bf16[1552,768]{1,0:T(8,128)(2,1)}, bf16[1552,768]{1,0:T(8,128)(2,1)}, u32[]{:S(2)}, u32[]{:S(2)}) collective-permute-start(bf16[1552,768]{1,0:T(8,128)(2,1)} %collective-permute-done.3), channel_id=1, source_target_pairs={{16,24},{17,25},{18,26},{19,27},{20,28},{21,29},{22,30},{23,31}} | collective-permute-start | bytes 7151624 | tf_op jit(solution)/shard_map/ppermute | solution.py:91
  157.4 53.9 %collective-permute-start.4 = (bf16[1552,768]{1,0:T(8,128)(2,1)}, bf16[1552,768]{1,0:T(8,128)(2,1)}, u32[]{:S(2)}, u32[]{:S(2)}) collective-permute-start(bf16[1552,768]{1,0:T(8,128)(2,1)} %collective-permute-done.2), channel_id=1, source_target_pairs={{8,0},{9,1},{10,2},{11,3},{12,4},{13,5},{14,6},{15,7}} | collective-permute-start | bytes 7151624 | tf_op jit(solution)/shard_map/ppermute | solution.py:91
  183.3 54.3 %all-to-all-start.3 = ((bf16[8,2,128,768]{3,2,1,0:T(8,128)(2,1)}), bf16[8,2,128,768]{3,2,1,0:T(8,128)(2,1)}, u32[]{:S(2)}, u32[]{:S(2)}) async-start(bf16[8,2,128,768]{3,2,1,0:T(8,128)(2,1)} %copy.197), calls=%async_computation.3 | async-start | bytes 6291456 | tf_op jit(solution)/shard_map/all_to_all | solution.py:148
  187.8 37.2 %copy-start.78 = (f32[512]{0:T(512)S(1)}, f32[512]{0:T(512)}, u32[]{:S(2)}) copy-start(f32[512]{0:T(512)} %copy-done.77) | copy-start | bytes 6148
  187.8 37.2 %copy-start.83 = (f32[512]{0:T(512)S(1)}, f32[512]{0:T(512)}, u32[]{:S(2)}) copy-start(f32[512]{0:T(512)} %copy-done.82) | copy-start | bytes 6148
  187.8 37.2 %copy-start.88 = (f32[768]{0:T(1024)S(1)}, f32[768]{0:T(1024)}, u32[]{:S(2)}) copy-start(f32[768]{0:T(1024)} %add.496) | copy-start | bytes 9220
  230.8 156.5 %copy-start.3 = (bf16[8,2,128,768]{3,2,1,0:T(8,128)(2,1)}, bf16[8,2,128,768]{3,2,1,0:T(8,128)(2,1)S(1)}, u32[]{:S(2)}) copy-start(bf16[8,2,128,768]{3,2,1,0:T(8,128)(2,1)S(1)} %copy.193) | copy-start | bytes 9437188
  253.3 40.8 %copy-start.36 = (bf16[2048,768]{1,0:T(8,128)(2,1)}, bf16[2048,768]{1,0:T(8,128)(2,1)S(1)}, u32[]{:S(2)}) copy-start(bf16[2048,768]{1,0:T(8,128)(2,1)S(1)} %get-tuple-element.220) | copy-start | bytes 9437188
  302.6 99.2 %collective-permute-start.6 = (bf16[1552,768]{1,0:T(8,128)(2,1)}, bf16[1552,768]{1,0:T(8,128)(2,1)}, u32[]{:S(2)}, u32[]{:S(2)}) collective-permute-start(bf16[1552,768]{1,0:T(8,128)(2,1)} %get-tuple-element.194), channel_id=1, source_target_pairs={{0,8},{1,9},{2,10},{3,11},{4,12},{5,13},{6,14},{7,15}} | collective-permute-start | bytes 7151624 | tf_op jit(solution)/shard_map/ppermute | solution.py:258
  305.3 96.5 %collective-permute-start.9 = (bf16[1552,768]{1,0:T(8,128)(2,1)}, bf16[1552,768]{1,0:T(8,128)(2,1)}, u32[]{:S(2)}, u32[]{:S(2)}) collective-permute-start(bf16[1552,768]{1,0:T(8,128)(2,1)} %get-tuple-element.195), channel_id=1, source_target_pairs={{24,16},{25,17},{26,18},{27,19},{28,20},{29,21},{30,22},{31,23}} | collective-permute-start | bytes 7151624 | tf_op jit(solution)/shard_map/ppermute | solution.py:262
  339.7 42.6 %all-to-all-start.4 = ((bf16[8,2,128,768]{3,2,1,0:T(8,128)(2,1)}), bf16[8,2,128,768]{3,2,1,0:T(8,128)(2,1)}, u32[]{:S(2)}, u32[]{:S(2)}) async-start(bf16[8,2,128,768]{3,2,1,0:T(8,128)(2,1)} %bitcast.261), calls=%async_computation.4 | async-start | bytes 6291456 | tf_op jit(solution)/shard_map/all_to_all | solution.py:234
  382.3 42.3 %all-to-all-start.1 = ((bf16[8,2,128,768]{3,2,1,0:T(8,128)(2,1)}), bf16[8,2,128,768]{3,2,1,0:T(8,128)(2,1)}, u32[]{:S(2)}, u32[]{:S(2)}) async-start(bf16[8,2,128,768]{3,2,1,0:T(8,128)(2,1)} %bitcast.268), calls=%async_computation.1 | async-start | bytes 6291456 | tf_op jit(solution)/shard_map/all_to_all | solution.py:234
  386.7 244.7 %reduce-scatter.2.cloned.1.call-start = ((), (), s32[]{:S(2)}) async-start(), calls=%async_computation.6 | async-start | bytes 5271552 | tf_op jit(solution)/shard_map/reduce_scatter | solution.py:332
  407.0 103.4 %collective-permute-start.7 = (bf16[1552,768]{1,0:T(8,128)(2,1)}, bf16[1552,768]{1,0:T(8,128)(2,1)}, u32[]{:S(2)}, u32[]{:S(2)}) collective-permute-start(bf16[1552,768]{1,0:T(8,128)(2,1)} %get-tuple-element.185), channel_id=1, source_target_pairs={{0,8},{8,16},{1,9},{9,17},{2,10},{10,18},{3,11},{11,19},{4,12},{12... | collective-permute-start | bytes 7151624 | tf_op jit(solution)/shard_map/ppermute | solution.py:258
  409.8 100.7 %collective-permute-start.10 = (bf16[1552,768]{1,0:T(8,128)(2,1)}, bf16[1552,768]{1,0:T(8,128)(2,1)}, u32[]{:S(2)}, u32[]{:S(2)}) collective-permute-start(bf16[1552,768]{1,0:T(8,128)(2,1)} %get-tuple-element.186), channel_id=1, source_target_pairs={{16,8},{24,16},{17,9},{25,17},{18,10},{26,18},{19,11},{27,19},{20,... | collective-permute-start | bytes 7151624 | tf_op jit(solution)/shard_map/ppermute | solution.py:262
  517.2 49.9 %collective-permute-start.8 = (bf16[1552,768]{1,0:T(8,128)(2,1)}, bf16[1552,768]{1,0:T(8,128)(2,1)}, u32[]{:S(2)}, u32[]{:S(2)}) collective-permute-start(bf16[1552,768]{1,0:T(8,128)(2,1)} %get-tuple-element.183), channel_id=1, source_target_pairs={{0,8},{8,16},{16,24},{1,9},{9,17},{17,25},{2,10},{10,18},{18,26},{... | collective-permute-start | bytes 7151624 | tf_op jit(solution)/shard_map/ppermute | solution.py:258
  519.9 52.7 %collective-permute-start.11 = (bf16[1552,768]{1,0:T(8,128)(2,1)}, bf16[1552,768]{1,0:T(8,128)(2,1)}, u32[]{:S(2)}, u32[]{:S(2)}) collective-permute-start(bf16[1552,768]{1,0:T(8,128)(2,1)} %get-tuple-element.184), channel_id=1, source_target_pairs={{8,0},{16,8},{24,16},{9,1},{17,9},{25,17},{10,2},{18,10},{26,18},{... | collective-permute-start | bytes 7151624 | tf_op jit(solution)/shard_map/ppermute | solution.py:262
  533.8 42.5 %copy-start.126 = (f32[1,192]{1,0:T(1,128)S(1)}, f32[1,192]{1,0:T(1,128)}, u32[]{:S(2)}) copy-start(f32[1,192]{1,0:T(1,128)} %param.51) | copy-start | bytes 2308
  533.8 42.5 %copy-start.130 = (f32[1,192]{1,0:T(1,128)S(1)}, f32[1,192]{1,0:T(1,128)}, u32[]{:S(2)}) copy-start(f32[1,192]{1,0:T(1,128)} %param.58) | copy-start | bytes 2308
  533.8 42.5 %copy-start.131 = (f32[1,192]{1,0:T(1,128)S(1)}, f32[1,192]{1,0:T(1,128)}, u32[]{:S(2)}) copy-start(f32[1,192]{1,0:T(1,128)} %param.65) | copy-start | bytes 2308
  533.8 43.1 %copy-start.107 = (f32[1,768]{1,0:T(1,128)S(1)}, f32[1,768]{1,0:T(1,128)}, u32[]{:S(2)}) copy-start(f32[1,768]{1,0:T(1,128)} %param.49) | copy-start | bytes 9220
  533.8 43.1 %copy-start.118 = (f32[768]{0:T(1024)S(1)}, f32[768]{0:T(1024)}, u32[]{:S(2)}) copy-start(f32[768]{0:T(1024)} %get-tuple-element.225) | copy-start | bytes 9220
  533.8 43.1 %copy-start.127 = (f32[1,768]{1,0:T(1,128)S(1)}, f32[1,768]{1,0:T(1,128)}, u32[]{:S(2)}) copy-start(f32[1,768]{1,0:T(1,128)} %param.56) | copy-start | bytes 9220
  533.8 43.1 %copy-start.128 = (f32[1,768]{1,0:T(1,128)S(1)}, f32[1,768]{1,0:T(1,128)}, u32[]{:S(2)}) copy-start(f32[1,768]{1,0:T(1,128)} %param.63) | copy-start | bytes 9220
  533.8 43.7 %copy-start.38 = (bf16[2048,768]{1,0:T(8,128)(2,1)S(1)}, bf16[2048,768]{1,0:T(8,128)(2,1)}, u32[]{:S(2)}) copy-start(bf16[2048,768]{1,0:T(8,128)(2,1)} %copy-done.37) | copy-start | bytes 9437188
  533.8 43.7 %copy-start.44 = (f32[768,768]{1,0:T(8,128)S(1)}, f32[768,768]{1,0:T(8,128)}, u32[]{:S(2)}) copy-start(f32[768,768]{1,0:T(8,128)} %fusion.173) | copy-start | bytes 7077892
  591.9 40.8 %copy-start.104 = (f32[8,24]{1,0:T(8,128)S(1)}, f32[8,24]{1,0:T(8,128)}, u32[]{:S(2)}) copy-start(f32[8,24]{1,0:T(8,128)} %param.47) | copy-start | bytes 2308
  591.9 40.8 %copy-start.112 = (f32[8,24]{1,0:T(8,128)S(1)}, f32[8,24]{1,0:T(8,128)}, u32[]{:S(2)}) copy-start(f32[8,24]{1,0:T(8,128)} %param.54) | copy-start | bytes 2308
  591.9 40.8 %copy-start.113 = (f32[8,24]{1,0:T(8,128)S(1)}, f32[8,24]{1,0:T(8,128)}, u32[]{:S(2)}) copy-start(f32[8,24]{1,0:T(8,128)} %param.61) | copy-start | bytes 2308
  591.9 41.4 %copy-start.105 = (f32[7,24]{1,0:T(8,128)S(1)}, f32[7,24]{1,0:T(8,128)}, u32[]{:S(2)}) copy-start(f32[7,24]{1,0:T(8,128)} %param.46) | copy-start | bytes 2020
  591.9 41.4 %copy-start.114 = (f32[7,24]{1,0:T(8,128)S(1)}, f32[7,24]{1,0:T(8,128)}, u32[]{:S(2)}) copy-start(f32[7,24]{1,0:T(8,128)} %param.53) | copy-start | bytes 2020
  591.9 41.4 %copy-start.115 = (f32[7,24]{1,0:T(8,128)S(1)}, f32[7,24]{1,0:T(8,128)}, u32[]{:S(2)}) copy-start(f32[7,24]{1,0:T(8,128)} %param.60) | copy-start | bytes 2020
  591.9 43.0 %copy-start.48 = (f32[4,24,768]{2,1,0:T(8,128)S(1)}, f32[4,24,768]{2,1,0:T(8,128)}, u32[]{:S(2)}) copy-start(f32[4,24,768]{2,1,0:T(8,128)} %param.45) | copy-start | bytes 884740
  591.9 43.0 %copy-start.60 = (f32[4,24,768]{2,1,0:T(8,128)S(1)}, f32[4,24,768]{2,1,0:T(8,128)}, u32[]{:S(2)}) copy-start(f32[4,24,768]{2,1,0:T(8,128)} %param.52) | copy-start | bytes 884740
  592.0 43.0 %copy-start.61 = (f32[4,24,768]{2,1,0:T(8,128)S(1)}, f32[4,24,768]{2,1,0:T(8,128)}, u32[]{:S(2)}) copy-start(f32[4,24,768]{2,1,0:T(8,128)} %param.59) | copy-start | bytes 884740
  (112 other events, 580.3 us)
Sparse Core Ops, SparseCore 0:
  11.5 79.0 all-gather.3
  524.0 107.4 reduce-scatter.1

commit v2 on v1

v2 whole, which is shorter than its diff:
```python
import functools
import math

import jax
import jax.numpy as jnp
from jax import lax
from jax.experimental import pallas as pl
from jax.experimental.pallas import tpu as pltpu
from jax.sharding import PartitionSpec as P

D = 768
HEADS = 12
HEAD_DIM = 64
LEN = 256
STEP = 3
ROWS = 256
BIAS_ROWS = 16

NORM_EPS = 1e-06
NEG_FILL = -1000000000.0
BETA_ONE = 0.9
BETA_TWO = 0.95
WEIGHT_DECAY = 0.1
ADAM_EPS = 1e-08
GELU_C = 0.7978845608028654
GELU_K = 0.044715
f32 = jnp.float32
b16 = jnp.bfloat16
MESH = pl.DeviceIdType.MESH


def adam_step(weight, grad, first, square, rate):
    new_first = BETA_ONE * first + (1.0 - BETA_ONE) * grad
    new_square = BETA_TWO * square + (1.0 - BETA_TWO) * grad * grad
    first_hat = new_first / (1.0 - BETA_ONE**STEP)
    square_hat = new_square / (1.0 - BETA_TWO**STEP)
    update = -rate * (first_hat / (jnp.sqrt(square_hat) + ADAM_EPS) + WEIGHT_DECAY * weight)
    return (weight + update, new_first, new_square)


def slots_of(routes, experts, capacity):
    flat = routes.reshape(-1, 2 * ROWS)
    onehot = (flat[:, :, None] == jnp.arange(experts, dtype=jnp.int32)).astype(b16)
    row = lax.broadcasted_iota(jnp.int32, (2 * ROWS, 2 * ROWS), 0)
    col = lax.broadcasted_iota(jnp.int32, (2 * ROWS, 2 * ROWS), 1)
    earlier = (col < row).astype(b16)
    before = jnp.einsum("ij,bje->bie", earlier, onehot, preferred_element_type=f32)
    slot = jnp.sum(before * onehot.astype(f32), axis=-1).astype(jnp.int32)
    return (flat * capacity + slot).reshape(-1, ROWS, 2)


def where_am_i():
    side = math.isqrt(lax.axis_size("expert") // 2)
    spot = lax.axis_index("expert")
    return side, lax.axis_index("dp"), spot // (2 * side), spot // 2 % side, spot % 2


def greet(peers):
    barrier = pltpu.get_barrier_semaphore()
    for peer in peers:
        pl.semaphore_signal(barrier, inc=1, device_id=peer, device_id_type=MESH)
    pl.semaphore_wait(barrier, len(peers))


def peers_of(n, side, z, y, x, core):
    def at(z_, y_, x_, core_):
        return (z_, (y_ * side + x_) * 2 + core_)

    along_z = [at((z + k) % n, y, x, core) for k in range(1, n)]
    first = [at(z, (y + core * k) % side, (x + (1 - core) * k) % side, core) for k in range(1, side)]
    second = [at(z, (y + (1 - core) * k) % side, (x + core * k) % side, core) for k in range(1, side)]
    return along_z, first, second, at(z, y, x, 1 - core)


def gather_kernel(n, in_ref, out_ref, local_sem, z_s, z_r, a_s, a_r, b_s, b_r, c_s, c_r):
    side, z, y, x, core = where_am_i()
    along_z, first, second, sibling = peers_of(n, side, z, y, x, core)
    greet([*along_z, *first, *second, sibling])

    def block(j, ka, kb, core_):
        y_ = (y - core * ka - (1 - core) * kb + 2 * side) % side
        x_ = (x - (1 - core) * ka - core * kb + 2 * side) % side
        return out_ref.at[((((z - j + n) % n) * side + y_) * side + x_) * 2 + core_]

    def remote(src, dst, send, recv, peer):
        return pltpu.make_async_remote_copy(
            src_ref=src, dst_ref=dst, send_sem=send, recv_sem=recv, device_id=peer, device_id_type=MESH
        )

    own = pltpu.make_async_copy(in_ref, block(0, 0, 0, core), local_sem)
    own.start()
    sent = []

    def pass_on(src, dst, j, ka, kb):
        if kb == 0:
            if ka == 0:
                for k in range(1, side):
                    copy = remote(src, dst, a_s.at[j * side + k], a_r.at[j * side + k], first[k - 1])
                    copy.start()
                    sent.append(copy)
            for k in range(1, side):
                place = (j * side + ka) * side + k
                copy = remote(src, dst, b_s.at[place], b_r.at[place], second[k - 1])
                copy.start()
                sent.append(copy)
        place = (j * side + kb) * side + ka
        copy = remote(src, dst, c_s.at[place], c_r.at[place], sibling)
        copy.start()
        sent.append(copy)

    for k in range(1, n):
        copy = remote(in_ref, block(0, 0, 0, core), z_s.at[k], z_r.at[k], along_z[k - 1])
        copy.start()
        sent.append(copy)
    pass_on(in_ref, block(0, 0, 0, core), 0, 0, 0)
    for j in range(1, n):
        here = block(j, 0, 0, core)
        remote(here, here, z_s.at[j], z_r.at[j], sibling).wait_recv()
        pass_on(here, here, j, 0, 0)
    for j in range(n):
        for ka in range(1, side):
            here = block(j, ka, 0, core)
            remote(here, here, a_s.at[j * side + ka], a_r.at[j * side + ka], sibling).wait_recv()
            pass_on(here, here, j, ka, 0)
    for j in range(n):
        for ka in range(side):
            for kb in range(1, side):
                here = block(j, ka, kb, core)
                place = (j * side + ka) * side + kb
                remote(here, here, b_s.at[place], b_r.at[place], sibling).wait_recv()
                pass_on(here, here, j, ka, kb)
    for j in range(n):
        for ka in range(side):
            for kb in range(side):
                here = block(j, ka, kb, 1 - core)
                place = (j * side + ka) * side + kb
                remote(here, here, c_s.at[place], c_r.at[place], sibling).wait_recv()
    for copy in sent:
        copy.wait_send()
    own.wait()


def gather_dense(packed, n, side):
    devices = n * side * side * 2
    sems = [
        pltpu.SemaphoreType.DMA,
        *[pltpu.SemaphoreType.DMA((n,))] * 2,
        *[pltpu.SemaphoreType.DMA((n * side,))] * 2,
        *[pltpu.SemaphoreType.DMA((n * side * side,))] * 4,
    ]
    size = devices * packed.size * 2
    return pl.pallas_call(
        functools.partial(gather_kernel, n),
        out_shape=jax.ShapeDtypeStruct((devices, *packed.shape), packed.dtype),
        in_specs=[pl.BlockSpec(memory_space=pltpu.VMEM)],
        out_specs=pl.BlockSpec(memory_space=pltpu.VMEM),
        scratch_shapes=sems,
        compiler_params=pltpu.CompilerParams(
            collective_id=0, has_side_effects=True, vmem_limit_bytes=size + (4 << 20)
        ),
        cost_estimate=CHEAP,
        name="gather_dense",
    )(packed)


def scatter_kernel(n, in_ref, out_ref, stage, c_buf, b_buf, a_buf, z_buf, c_s, c_r, b_s, b_r, a_s, a_r, z_s, z_r):
    side, z, y, x, core = where_am_i()
    along_z, first, second, sibling = peers_of(n, side, z, y, x, core)
    greet([*along_z, *first, *second, sibling])

    def piece(ka, kb, core_):
        y_ = (y + core * ka + (1 - core) * kb) % side
        x_ = (x + (1 - core) * ka + core * kb) % side
        return (core_ * side + y_) * side + x_

    def remote(src, dst, send, recv, peer):
        return pltpu.make_async_remote_copy(
            src_ref=src, dst_ref=dst, send_sem=send, recv_sem=recv, device_id=peer, device_id_type=MESH
        )

    sent = []

    def send(src, dst, send_sem, recv_sem, peer):
        copy = remote(src, dst, send_sem, recv_sem, peer)
        copy.start()
        sent.append(copy)

    order = [(ka, kb) for kb in [*range(1, side), 0] for ka in [*range(1, side), 0]]
    for ka, kb in order:
        place = ka * side + kb
        send(in_ref.at[piece(kb, ka, 1 - core)], c_buf.at[place], c_s.at[place], c_r.at[place], sibling)
    for ka, kb in order:
        place = ka * side + kb
        remote(c_buf.at[place], c_buf.at[place], c_s.at[place], c_r.at[place], sibling).wait_recv()
        mine = piece(ka, kb, core)
        if kb:
            stage[place] = (in_ref[mine].astype(f32) + c_buf[place].astype(f32)).astype(b16)
            slot = ka * side + kb
            send(stage.at[place], b_buf.at[slot], b_s.at[slot], b_r.at[slot], second[kb - 1])
        else:
            total = in_ref[mine].astype(f32) + c_buf[place].astype(f32)
            for k in range(1, side):
                slot = ka * side + k
                remote(b_buf.at[slot], b_buf.at[slot], b_s.at[slot], b_r.at[slot], sibling).wait_recv()
                total = total + b_buf[slot].astype(f32)
            if ka:
                stage[place] = total.astype(b16)
                send(stage.at[place], a_buf.at[ka], a_s.at[ka], a_r.at[ka], first[ka - 1])
            else:
                for k in range(1, side):
                    remote(a_buf.at[k], a_buf.at[k], a_s.at[k], a_r.at[k], sibling).wait_recv()
                    total = total + a_buf[k].astype(f32)
                stage[place] = total.astype(b16)
    for k in range(1, n):
        send(stage.at[0, (z + k) % n], z_buf.at[k], z_s.at[k], z_r.at[k], along_z[k - 1])
    result = stage[0, z].astype(f32)
    for k in range(1, n):
        remote(z_buf.at[k], z_buf.at[k], z_s.at[k], z_r.at[k], sibling).wait_recv()
        result = result + z_buf[k].astype(f32)
    out_ref[...] = result
    for copy in sent:
        copy.wait_send()


def scatter_dense(parts, n, side):
    rows, width = parts.shape[-2:]
    parts = parts.reshape(2 * side * side, n, rows, width)
    shape = (n, rows, width)
    dma = pltpu.SemaphoreType.DMA
    size = parts.size * 2
    return pl.pallas_call(
        functools.partial(scatter_kernel, n),
        out_shape=jax.ShapeDtypeStruct((rows, width), f32),
        in_specs=[pl.BlockSpec(memory_space=pltpu.VMEM)],
        out_specs=pl.BlockSpec(memory_space=pltpu.VMEM),
        scratch_shapes=[
            pltpu.VMEM((side * side, *shape), b16),
            pltpu.VMEM((side * side, *shape), b16),
            pltpu.VMEM((side * side, *shape), b16),
            pltpu.VMEM((side, *shape), b16),
            pltpu.VMEM((n, rows, width), b16),
            *[dma((side * side,))] * 4,
            *[dma((side,))] * 2,
            *[dma((n,))] * 2,
        ],
        compiler_params=pltpu.CompilerParams(
            collective_id=1, has_side_effects=True, vmem_limit_bytes=3 * size + (8 << 20)
        ),
        cost_estimate=CHEAP,
        name="scatter_dense",
    )(parts)


TILE = 512


def dot(a, b, contract):
    return lax.dot_general(a, b, (contract, ((), ())), preferred_element_type=f32)


NN = ((1,), (0,))
NT = ((1,), (1,))
TN = ((0,), (0,))


def expert_kernel(sources, first, last, part, *refs):
    refs = list(refs)
    weights = [refs.pop(0) for _ in range(sources)]
    x_ref, dout_ref, bias_ref = refs[:3]
    refs = refs[3:]
    sums = [None, None] if first else [refs.pop(0), refs.pop(0)]
    out_ref, grad_x_ref, grad_up_ref, grad_down_ref, w_ref, up_acc, down_acc, bias_acc, sem = refs
    step = pl.program_id(0)

    @pl.when(step == 0)
    def _():
        if sources == 1:
            copy = pltpu.make_async_copy(weights[0], w_ref, sem)
            copy.start()
            copy.wait()
        else:
            me = lax.axis_index("dp")
            inner = (me + 1) // 2 % 2

            @pl.when(inner == 1)
            def _():
                pltpu.make_async_copy(weights[0], w_ref, sem).start()

            @pl.when(inner == 0)
            def _():
                pltpu.make_async_copy(weights[1], w_ref, sem).start()

            pltpu.make_async_copy(weights[0], w_ref, sem).wait()
        up_acc[...] = jnp.zeros_like(up_acc)
        down_acc[...] = jnp.zeros_like(down_acc)
        bias_acc[...] = jnp.zeros_like(bias_acc)

    x = x_ref[...]
    dout = dout_ref[...]
    up = w_ref[:part]
    down = w_ref[part : 2 * part]
    up_bias = w_ref[2 * part :][0:1, :part].astype(f32)
    pre = dot(x, up, NT) + up_bias
    grad_hidden = dot(dout, down, NT)
    square = pre * pre
    inner = jnp.tanh(pre * (GELU_C + GELU_C * GELU_K * square))
    half = 0.5 * pre
    hidden = (half + half * inner).astype(b16)
    slope = 0.5 + 0.5 * inner + half * (1.0 - inner * inner) * (GELU_C + 3.0 * GELU_C * GELU_K * square)
    grad_pre = slope * grad_hidden
    grad_pre_b = grad_pre.astype(b16)
    out = dot(hidden, down, NN)
    grad_x = dot(grad_pre_b, up, NN)
    if not first:
        out = out + sums[0][...]
        grad_x = grad_x + sums[1][...]
    if last:
        out = out + bias_ref[1:2, :]
    out_ref[...] = out.astype(out_ref.dtype)
    grad_x_ref[...] = grad_x.astype(grad_x_ref.dtype)
    down_acc[...] += dot(hidden, dout, TN)
    up_acc[...] += dot(grad_pre_b, x, TN)
    bias_acc[0:1, :] += jnp.sum(grad_pre_b.astype(f32), axis=0, keepdims=True)

    @pl.when(step == pl.num_programs(0) - 1)
    def _():
        grad_up_ref[...] = up_acc[...].astype(grad_up_ref.dtype)
        grad_down_ref[:part] = down_acc[...].astype(grad_down_ref.dtype)
        row = lax.broadcasted_iota(jnp.int32, (BIAS_ROWS, D), 0)
        tail = jnp.where(row == 0, bias_acc[0:1, :], jnp.where(row == 1, bias_ref[0:1, :], 0.0))
        grad_down_ref[part:] = tail.astype(grad_down_ref.dtype)


def expert_part(weights, x, dout, biases, sums, last, grad_type, name):
    first = sums is None
    slots = x.shape[0]
    rows = weights[0].shape[0]
    part = (rows - BIAS_ROWS) // 2
    tile = pl.BlockSpec((TILE, D), lambda i: (i, 0))
    kept = b16 if last else f32
    n = len(weights)
    return pl.pallas_call(
        functools.partial(expert_kernel, n, first, last, part),
        grid=(slots // TILE,),
        in_specs=[
            *[pl.BlockSpec(memory_space=pl.ANY)] * n,
            tile,
            tile,
            pl.BlockSpec((2, D), lambda i: (0, 0)),
            *([] if first else [tile, tile]),
        ],
        out_specs=[
            tile,
            tile,
            pl.BlockSpec((part, D), lambda i: (0, 0)),
            pl.BlockSpec((part + BIAS_ROWS, D), lambda i: (0, 0)),
        ],
        out_shape=[
            jax.ShapeDtypeStruct((slots, D), kept),
            jax.ShapeDtypeStruct((slots, D), kept),
            jax.ShapeDtypeStruct((part, D), grad_type),
            jax.ShapeDtypeStruct((part + BIAS_ROWS, D), grad_type),
        ],
        scratch_shapes=[
            pltpu.VMEM((rows, D), b16),
            pltpu.VMEM((part, D), f32),
            pltpu.VMEM((part, D), f32),
            pltpu.VMEM((8, part), f32),
            pltpu.SemaphoreType.DMA,
        ],
        compiler_params=pltpu.CompilerParams(vmem_limit_bytes=56 << 20, dimension_semantics=("arbitrary",)),
        cost_estimate=pl.CostEstimate(flops=12 * slots * part * D, bytes_accessed=slots * D * 20, transcendentals=0),
        name=name,
    )(*weights, x, dout, biases, *([] if first else sums))


SCALE = HEAD_DIM ** (-0.5)
PAIRS = HEADS // 2
WIDE = 2 * HEAD_DIM
CHEAP = pl.CostEstimate(flops=0, bytes_accessed=1024, transcendentals=0)


def normal(values):
    center = values - jnp.mean(values, axis=-1, keepdims=True)
    rate = lax.rsqrt(jnp.mean(center * center, axis=-1, keepdims=True) + NORM_EPS)
    return center * rate, rate


def lanes_like(values):
    return lax.broadcasted_iota(jnp.int32, values.shape, values.ndim - 1)


def scores_of(part_q, pair_k, length):
    scores = dot(part_q, pair_k, NT) * SCALE
    return jnp.where(lanes_like(scores) < length, scores, NEG_FILL)


def halves(pair):
    low = lanes_like(pair) < HEAD_DIM
    zero = jnp.zeros_like(pair)
    return jnp.where(low, pair, zero), jnp.where(low, zero, pair)


def joined(even, odd):
    return jnp.where(lanes_like(even) < HEAD_DIM, even, odd)


def attention_kernel(
    lengths_ref, tokens_ref, weights_ref, vector_ref, router_ref, routes_ref, places_ref,
    normed_ref, q_ref, k_ref, v_ref, context_ref, lse_ref, resid_ref, normed_two_ref, gates_ref, slots_ref,
):
    length = lengths_ref[pl.program_id(0)]
    rows = tokens_ref[...].astype(f32)
    hat, _ = normal(rows)
    normed = (hat * vector_ref[0:1, :] + vector_ref[1:2, :]).astype(b16)
    normed_ref[...] = normed
    q_ref[...] = (dot(normed, weights_ref[0], NN) + vector_ref[2:3, :]).astype(b16)
    k_ref[...] = dot(normed, weights_ref[1], NN).astype(b16)
    v_ref[...] = (dot(normed, weights_ref[2], NN) + vector_ref[3:4, :]).astype(b16)
    lse = jnp.zeros((LEN, 128), f32)
    for pair in range(PAIRS):
        lanes = slice(pair * WIDE, (pair + 1) * WIDE)
        keys, values = k_ref[:, lanes], v_ref[:, lanes]
        mixed = []
        for half, part in enumerate(halves(q_ref[:, lanes])):
            scores = scores_of(part, keys, length)
            top = jnp.max(scores, axis=-1, keepdims=True)
            total = top + jnp.log(jnp.sum(jnp.exp(scores - top), axis=-1, keepdims=True))
            chance = jnp.exp(scores - total).astype(b16)
            mixed.append(dot(chance, values, NN))
            lse = jnp.where(lanes_like(lse) == 2 * pair + half, total, lse)
        context_ref[:, lanes] = joined(*mixed).astype(b16)
    lse_ref[...] = lse
    resid = rows + (dot(context_ref[...], weights_ref[3], NN) + vector_ref[4:5, :])
    resid_ref[...] = resid
    hat, _ = normal(resid)
    normed_two = (hat * vector_ref[5:6, :] + vector_ref[6:7, :]).astype(b16)
    normed_two_ref[...] = normed_two
    logits = dot(normed_two, router_ref[...], NT)
    names = lanes_like(logits)
    first = jnp.sum(jnp.where(names == routes_ref[:, 0:1], logits, 0.0), axis=-1, keepdims=True)
    second = jnp.sum(jnp.where(names == routes_ref[:, 1:2], logits, 0.0), axis=-1, keepdims=True)
    gate = lanes_like(gates_ref[...])
    gates_ref[...] = jnp.where(gate == 0, jax.nn.sigmoid(first - second), jax.nn.sigmoid(second - first))
    experts, _, capacity, _ = slots_ref.shape
    slots = experts * capacity
    ids = lax.broadcasted_iota(jnp.int32, (slots, ROWS), 0)
    places = places_ref[0]
    chosen = jnp.where((ids == places[0:1, :]) | (ids == places[1:2, :]), 1.0, 0.0).astype(b16)
    sent = dot(chosen, normed_two, NN).astype(b16)
    slots_ref[...] = sent.reshape(experts, 1, capacity, D)


def attention_forward(lengths, tokens, weights, vector, router, routes, places, experts, capacity):
    count = tokens.shape[0]
    rows = pl.BlockSpec((LEN, D), lambda i: (i, 0))
    lanes = pl.BlockSpec((LEN, 128), lambda i: (i, 0))
    once = pl.Buffered(1)
    return pl.pallas_call(
        attention_kernel,
        grid=(count // LEN,),
        in_specs=[
            pl.BlockSpec(memory_space=pltpu.SMEM),
            rows,
            pl.BlockSpec((4, D, D), lambda i: (0, 0, 0), pipeline_mode=once),
            pl.BlockSpec((8, D), lambda i: (0, 0)),
            pl.BlockSpec((128, D), lambda i: (0, 0)),
            pl.BlockSpec((LEN, 2), lambda i: (i, 0)),
            pl.BlockSpec((1, 2, ROWS), lambda i: (i, 0, 0)),
        ],
        out_specs=[
            rows, rows, rows, rows, rows, lanes, rows, rows, lanes,
            pl.BlockSpec((experts, 1, capacity, D), lambda i: (0, i, 0, 0)),
        ],
        out_shape=[
            *[jax.ShapeDtypeStruct((count, D), b16)] * 5,
            jax.ShapeDtypeStruct((count, 128), f32),
            jax.ShapeDtypeStruct((count, D), f32),
            jax.ShapeDtypeStruct((count, D), b16),
            jax.ShapeDtypeStruct((count, 128), f32),
            jax.ShapeDtypeStruct((experts, count // ROWS, capacity, D), b16),
        ],
        compiler_params=pltpu.CompilerParams(vmem_limit_bytes=48 << 20),
        cost_estimate=CHEAP,
        name="attention_forward",
    )(lengths, tokens, weights, vector, router, routes, places)


def norm_back(grad, hat, rate, gain):
    inner = grad * gain
    return rate * (
        inner
        - jnp.mean(inner, axis=-1, keepdims=True)
        - hat * jnp.mean(inner * hat, axis=-1, keepdims=True)
    )


def two_terms(values):
    high = values.astype(b16)
    return high, (values - high.astype(f32)).astype(b16)


def column_sum(values):
    return jnp.sum(values, axis=0, keepdims=True)


def backward_kernel(
    lengths_ref, tokens_ref, grad_ref, weights_ref, vector_ref, router_ref, routes_ref, places_ref,
    normed_ref, q_ref, k_ref, v_ref, context_ref, lse_ref, resid_ref, normed_two_ref, gates_ref, outs_ref, returned_ref,
    output_ref, input_grad_ref, grad_weights_ref, grad_vector_ref, grad_router_ref,
    weights_acc, vector_acc, router_acc, dq_ref, dk_ref, dv_ref,
):
    step = pl.program_id(0)
    length = lengths_ref[step]

    @pl.when(step == 0)
    def _():
        weights_acc[...] = jnp.zeros_like(weights_acc)
        vector_acc[...] = jnp.zeros_like(vector_acc)
        router_acc[...] = jnp.zeros_like(router_acc)

    slots = outs_ref.shape[0] * outs_ref.shape[2]
    ids = lax.broadcasted_iota(jnp.int32, (ROWS, slots), 1)
    outs = outs_ref[...].reshape(slots, D)
    returned = returned_ref[...].reshape(slots, D)
    grad_out = grad_ref[...].astype(f32)
    take = [jnp.where(ids == places_ref[:, k : k + 1], 1.0, 0.0).astype(b16) for k in range(2)]
    out = [dot(t, outs, NN) for t in take]
    gates = [gates_ref[:, k : k + 1] for k in range(2)]
    resid = resid_ref[...]
    output_ref[...] = resid + gates[0] * out[0] + gates[1] * out[1]
    slopes = [
        jnp.sum(grad_out * out[k], axis=-1, keepdims=True) * (gates[k] * (1.0 - gates[k])) for k in range(2)
    ]
    pull = slopes[0] - slopes[1]
    names = lax.broadcasted_iota(jnp.int32, (ROWS, 128), 1)
    grad_logits = jnp.where(names == routes_ref[:, 0:1], pull, jnp.where(names == routes_ref[:, 1:2], -pull, 0.0))
    high, low = two_terms(grad_logits)
    normed_two = normed_two_ref[...]
    router = router_ref[...]
    router_acc[...] += dot(high, normed_two, TN) + dot(low, normed_two, TN)
    grad_two = dot(take[0] + take[1], returned, NN) + (dot(high, router, NN) + dot(low, router, NN))
    hat, rate = normal(resid)
    vector_acc[5:6, :] += column_sum(grad_two * hat)
    vector_acc[6:7, :] += column_sum(grad_two)
    grad_resid = grad_out + norm_back(grad_two, hat, rate, vector_ref[5:6, :])
    input_grad_ref[...] = grad_resid
    branch = grad_resid.astype(b16)
    vector_acc[4:5, :] += column_sum(branch.astype(f32))
    weights_acc[3] += dot(context_ref[...], branch, TN)
    grad_context = dot(branch, weights_ref[3], NT).astype(b16)
    for pair in range(PAIRS):
        lanes = slice(pair * WIDE, (pair + 1) * WIDE)
        queries, keys, values = q_ref[:, lanes], k_ref[:, lanes], v_ref[:, lanes]
        given = grad_context[:, lanes]
        grads = []
        for half, (part, part_given) in enumerate(zip(halves(queries), halves(given))):
            head = 2 * pair + half
            chance = jnp.exp(scores_of(part, keys, length) - lse_ref[:, head : head + 1])
            grad_v = dot(chance.astype(b16), given, TN)
            grad_chance = dot(part_given, values, NT)
            mean = jnp.sum(chance * grad_chance, axis=-1, keepdims=True)
            grad_scores = (chance * (grad_chance - mean)).astype(b16)
            grads.append((dot(grad_scores, keys, NN), dot(grad_scores, queries, TN), grad_v))
        dq_ref[:, lanes] = (joined(grads[0][0], grads[1][0]) * SCALE).astype(b16)
        dk_ref[:, lanes] = (joined(grads[0][1], grads[1][1]) * SCALE).astype(b16)
        dv_ref[:, lanes] = joined(grads[0][2], grads[1][2]).astype(b16)
    normed = normed_ref[...]
    grad_one = jnp.zeros((LEN, D), f32)
    for k, ref in enumerate((dq_ref, dk_ref, dv_ref)):
        weights_acc[k] += dot(normed, ref[...], TN)
        grad_one += dot(ref[...], weights_ref[k], NT)
    vector_acc[2:3, :] += column_sum(dq_ref[...].astype(f32))
    vector_acc[3:4, :] += column_sum(dv_ref[...].astype(f32))
    hat, rate = normal(tokens_ref[...].astype(f32))
    vector_acc[0:1, :] += column_sum(grad_one * hat)
    vector_acc[1:2, :] += column_sum(grad_one)
    input_grad_ref[...] += norm_back(grad_one, hat, rate, vector_ref[0:1, :])

    @pl.when(step == pl.num_programs(0) - 1)
    def _():
        for k in range(4):
            grad_weights_ref[k] = weights_acc[k].astype(b16)
        grad_vector_ref[...] = vector_acc[...]
        grad_router_ref[...] = router_acc[...]


def attention_backward(lengths, tokens, out_grad, weights, vector, router, routes, places, kept, outs, returned):
    count = tokens.shape[0]
    experts, _, capacity, _ = outs.shape
    rows = pl.BlockSpec((LEN, D), lambda i: (i, 0))
    lanes = pl.BlockSpec((LEN, 128), lambda i: (i, 0))
    pairs = pl.BlockSpec((LEN, 2), lambda i: (i, 0))
    slots = pl.BlockSpec((experts, 1, capacity, D), lambda i: (0, i, 0, 0))

    def fixed(*shape):
        return pl.BlockSpec(shape, lambda i: (0,) * len(shape), pipeline_mode=pl.Buffered(1))

    return pl.pallas_call(
        backward_kernel,
        grid=(count // LEN,),
        in_specs=[
            pl.BlockSpec(memory_space=pltpu.SMEM),
            rows, rows, fixed(4, D, D), fixed(8, D), fixed(128, D), pairs, pairs,
            rows, rows, rows, rows, rows, lanes, rows, rows, lanes, slots, slots,
        ],
        out_specs=[rows, rows, fixed(4, D, D), fixed(8, D), fixed(128, D)],
        out_shape=[
            jax.ShapeDtypeStruct((count, D), f32),
            jax.ShapeDtypeStruct((count, D), f32),
            jax.ShapeDtypeStruct((4, D, D), b16),
            jax.ShapeDtypeStruct((8, D), f32),
            jax.ShapeDtypeStruct((128, D), f32),
        ],
        scratch_shapes=[
            pltpu.VMEM((4, D, D), f32),
            pltpu.VMEM((8, D), f32),
            pltpu.VMEM((128, D), f32),
            *[pltpu.VMEM((LEN, D), b16)] * 3,
        ],
        compiler_params=pltpu.CompilerParams(vmem_limit_bytes=58 << 20),
        cost_estimate=CHEAP,
        name="attention_backward",
    )(lengths, tokens, out_grad, weights, vector, router, routes, places, *kept, outs, returned)


def pack_expert(up, down, up_bias, down_bias, dtype):
    part = up.shape[0]
    tail = jnp.zeros((BIAS_ROWS, D), dtype)
    tail = tail.at[0, :part].set(up_bias.astype(dtype))
    tail = tail.at[1, : down_bias.shape[0]].set(down_bias.astype(dtype))
    return jnp.concatenate([up.astype(dtype), down.astype(dtype), tail], axis=0)


def after(x, *others):
    return lax.optimization_barrier((x, *others))[0]


def along(x, *pairs):
    return lax.ppermute(x, "dp", pairs)


def body(
    tokens, out_grad, routes, lengths,
    attention, gain_bias, router, expert_up, up_bias, expert_down, down_bias,
    first_attention, first_gain_bias, first_router, first_expert_up, first_up_bias, first_expert_down, first_down_bias,
    square_attention, square_gain_bias, square_router, square_expert_up, square_up_bias, square_expert_down, square_down_bias,
):
    experts = router.shape[0]
    capacity = 4 * ROWS // experts
    count = tokens.shape[0]
    blocks = count // ROWS
    part = expert_up.shape[1]
    narrow = down_bias.shape[1]
    cols = attention.shape[1]
    devices = D // cols
    n_dp = lax.axis_size("dp")
    assert n_dp == 4 and expert_up.shape[0] == 1
    me = lax.axis_index("dp")
    mine = lax.axis_index("expert")
    both = ("dp", "expert")

    flat_len = (7 + experts) * cols
    extra = -(-(4 * cols + -(-flat_len // D)) // 16) * 16 - 4 * cols
    side = math.isqrt(experts // 2)
    small = jnp.concatenate([gain_bias, router], axis=0).astype(b16).reshape(-1)
    small = jnp.pad(small, (0, extra * D - flat_len)).reshape(extra, D)
    packed = jnp.concatenate([attention.astype(b16).reshape(4 * cols, D), small], axis=0)
    whole = gather_dense(packed, n_dp, side)
    own = after(pack_expert(expert_up[0], expert_down[0], up_bias[0], down_bias[0], b16), whole)

    second = along(own, (0, 1), (1, 0), (2, 3), (3, 2))
    third_inner = along(own, (1, 2), (2, 1))
    third_outer = along(third_inner, (1, 0), (2, 3))
    fourth_inner = along(second, (1, 2), (2, 1))
    fourth_outer = along(fourth_inner, (1, 0), (2, 3))

    weights_b = whole[:, : 4 * cols].reshape(devices, 4, cols, D).transpose(1, 0, 2, 3).reshape(4, D, D)
    small = whole[:, 4 * cols :].reshape(devices, extra * D)[:, :flat_len].reshape(devices, 7 + experts, cols)
    small = small.transpose(1, 0, 2).reshape(7 + experts, D)
    vector = small[:7].astype(f32)
    router_b = small[7:]

    positions = slots_of(routes, experts, capacity)
    slot_ids = jnp.arange(experts * capacity, dtype=jnp.int32)
    hit = positions[:, :, :, None] == slot_ids
    split = jnp.any(hit, axis=2).astype(b16).reshape(blocks, ROWS, experts, capacity)
    other = jnp.flip(routes, axis=1).reshape(blocks, ROWS, 2)
    partner = jnp.sum(jnp.where(hit, other[:, :, :, None], 0), axis=(1, 2)).astype(f32)
    partner = partner.reshape(blocks, experts, capacity).transpose(1, 0, 2)
    partner = lax.all_to_all(partner, "expert", split_axis=0, concat_axis=0, tiled=True)
    grad_rows = out_grad.reshape(blocks, ROWS, D)

    sent = jnp.einsum("btec,btd->ebcd", split, grad_rows, preferred_element_type=f32).astype(b16)
    sent = after(sent, whole)
    grad_slots = lax.all_to_all(sent, "expert", split_axis=0, concat_axis=0, tiled=True)
    grad_slots = grad_slots.reshape(experts * blocks * capacity, D)

    router_all = jnp.pad(router_b, ((0, 128 - experts), (0, 0)))
    vector_all = jnp.pad(vector, ((0, 1), (0, 0)))
    *kept, slots_out = attention_forward(
        lengths, tokens, weights_b, vector_all, router_all, routes, positions.transpose(0, 2, 1), experts, capacity
    )

    def exchange(sent):
        return lax.all_to_all(sent, "expert", split_axis=0, concat_axis=0, tiled=True)

    slots_in = exchange(after(slots_out, grad_slots)).reshape(experts * blocks * capacity, D)

    slot_logits = jnp.einsum("sd,ed->se", slots_in, router_b, preferred_element_type=f32)
    ids = jnp.arange(experts, dtype=jnp.int32)
    rival = partner.reshape(-1).astype(jnp.int32)
    margin = jnp.sum(
        slot_logits * ((ids == mine).astype(f32) - (rival[:, None] == ids).astype(f32)), axis=-1
    )
    dout = (jax.nn.sigmoid(margin)[:, None] * grad_slots.astype(f32)).astype(b16)
    grad_down_bias = jnp.sum(dout.astype(f32), axis=0)

    def pick(*arrays):
        out = arrays[-1]
        for i in range(len(arrays) - 2, -1, -1):
            out = jnp.where(me == i, arrays[i], out)
        return out

    inner = (me == 1) | (me == 2)
    tail = 2 * part + 1
    names = [me, pick(1, 0, 3, 2), pick(2, 2, 1, 1), pick(3, 3, 0, 0)]
    bias_rows = [
        own[tail, :narrow],
        second[tail, :narrow],
        jnp.where(inner, third_inner[tail, :narrow], third_outer[tail, :narrow]),
        jnp.where(inner, fourth_inner[tail, :narrow], fourth_outer[tail, :narrow]),
    ]
    place = jnp.stack(names)
    down_bias_full = jnp.zeros((n_dp, narrow), b16).at[place].set(jnp.stack(bias_rows)).reshape(D)
    weights = [(own,), (second,), (third_inner, third_outer), (fourth_inner, fourth_outer)]
    sums = None
    part_grads = []
    for i in range(4):
        share = lax.dynamic_slice(grad_down_bias, (names[i] * narrow,), (narrow,))
        share = jnp.pad(share, (0, D - narrow))
        biases = jnp.stack([share, down_bias_full.astype(f32) if i == 3 else share])
        *sums, grad_up, grad_down = expert_part(
            weights[i], slots_in, dout, biases, sums, i == 3, b16 if i else f32, f"expert_part_{i}"
        )
        part_grads.append((grad_up, grad_down))
    out_b, grad_b = sums

    back = exchange(out_b.reshape(experts, blocks, capacity, D))
    returned = exchange(grad_b.reshape(experts, blocks, capacity, D))

    def add(a, b):
        return (a.astype(f32) + b.astype(f32)).astype(b16)

    both_halves = range(2)
    nearest, middle, far = ([part_grads[k][i] for i in both_halves] for k in (1, 2, 3))
    near = [along(nearest[i], (0, 1), (3, 2)) for i in both_halves]
    mid = [along(after(middle[i], near[i]), (0, 1), (3, 2)) for i in both_halves]
    end = [along(after(far[i], mid[i]), (0, 1), (3, 2)) for i in both_halves]
    mid = [along(add(middle[i], mid[i]), (1, 2), (2, 1)) for i in both_halves]
    end = [along(add(far[i], end[i]), (1, 2), (2, 1)) for i in both_halves]
    end = [along(add(nearest[i], end[i]), (1, 0), (2, 3)) for i in both_halves]
    totals = [
        part_grads[0][i] + (near[i].astype(f32) + mid[i].astype(f32) + end[i].astype(f32)) for i in both_halves
    ]
    shard_up = totals[0][None]
    shard_down = totals[1][:part][None]
    shard_up_bias = totals[1][part, :part][None]
    shard_down_bias = totals[1][part + 1, :narrow][None]

    output, input_grad, grad_weights, grad_vector, grad_router = attention_backward(
        lengths, tokens, out_grad, weights_b, vector_all, router_all, routes, positions.reshape(count, 2), kept, back, returned
    )

    small = jnp.concatenate([grad_vector[:7], grad_router[:experts]], axis=0).reshape(7 + experts, devices, cols)
    small = jnp.pad(small.transpose(1, 0, 2).reshape(devices, flat_len), ((0, 0), (0, extra * D - flat_len)))
    big = grad_weights.reshape(4, devices, cols, D).transpose(1, 0, 2, 3).reshape(devices, 4 * cols, D)
    packed = jnp.concatenate([big, small.reshape(devices, extra, D).astype(b16)], axis=1)
    packed = packed.reshape(n_dp, side, side, 2, 4 * cols + extra, D).transpose(3, 1, 2, 0, 4, 5)
    packed = scatter_dense(packed, n_dp, side)
    shard_weights = packed[: 4 * cols].reshape(4, cols, D)
    small = packed[4 * cols :].reshape(extra * D)[:flat_len].reshape(7 + experts, cols)
    shard_vector, shard_router = small[:7], small[7:]

    params = (attention, gain_bias, router, expert_up, up_bias, expert_down, down_bias)
    grads = (shard_weights, shard_vector, shard_router, shard_up, shard_up_bias, shard_down, shard_down_bias)
    firsts = (first_attention, first_gain_bias, first_router, first_expert_up, first_up_bias, first_expert_down, first_down_bias)
    squares = (square_attention, square_gain_bias, square_router, square_expert_up, square_up_bias, square_expert_down, square_down_bias)
    hidden_units = n_dp * part
    rates = (1.6 * D ** (-0.5), 0.3, 0.5 * D ** (-0.5), 1.5 * D ** (-0.5), 0.25, 0.5 * hidden_units ** (-0.5), 0.25)
    updated = [adam_step(params[i], grads[i], firsts[i], squares[i], rates[i]) for i in range(7)]
    return (output, input_grad, *grads, *(u[0] for u in updated), *(u[1] for u in updated), *(u[2] for u in updated))


def solution(mesh):
    rows = P(("dp", "expert"), None)
    state = (
        P(None, ("dp", "expert"), None),
        P(None, ("dp", "expert")),
        P(None, ("dp", "expert")),
        P("expert", "dp", None),
        P("expert", "dp"),
        P("expert", "dp", None),
        P("expert", "dp"),
    )
    return jax.shard_map(
        body,
        mesh=mesh,
        in_specs=(rows, rows, rows, P(("dp", "expert")), *state, *state, *state),
        out_specs=(rows, rows, *state, *state, *state, *state),
        check_vma=False,
    )
```

time: 652 us -> 575 us (0.88)
  Pallas kernels: 0 us -> 241 us
  matrix products: 186 us -> 4.07 us
  waiting for transfers between devices: 215 us -> 159 us
  local copies, waits for them, and re-layouts: 98.1 us -> 44.6 us
  other arithmetic: 75.8 us -> 45 us
  starting transfers between devices: 51.2 us -> 67.8 us
  between operations: 16.5 us -> 2.08 us
    pallas_call x0 -> x8, Pallas kernels: none -> 241 us  [the longest x4 96.2 us: expert_part(): pl.pallas_call(functools.partial(expert_kernel, n, first, last, part), gr...]
    dot_general x43 -> x1, matrix products: 185 us -> 0.99 us  [body(): jnp.einsum('btec,btd->ebcd', split, grad_rows, preferred_element_type=f32)]
    reduce_scatter x1 -> x0, waiting for transfers between devices: 34.9 us -> none  [body(): lax.psum_scatter(packed, both, scatter_dimension=0, tiled=False).astype(f32)]
    concatenate x15 -> x0, local copies, waits for them, and re-layouts: 22.8 us -> none  [body(): jnp.concatenate([grad_vector, grad_router], axis=0)]
    ppermute x12 -> x17, waiting for transfers between devices: 136 us -> 118 us  [along(): return lax.ppermute(x, 'dp', pairs)]
    ppermute x12 -> x17, starting transfers between devices: 28.5 us -> 46.2 us  [along(): return lax.ppermute(x, 'dp', pairs)]
    add x5 -> x7, other arithmetic: 3.5 us -> 17.3 us  [adam_step(): return (weight + update, new_first, new_square)]
    convert_element_type x9 -> x2, local copies, waits for them, and re-layouts: 12.5 us -> 0.21 us  [the longest x1 0.13 us: body(): vector = small[:7].astype(f32)]
  transfers between devices with their start and end apart: 19 -> 22, of which waited for: 10 -> 8; matrix products, arithmetic and copies ran while one was open for 42% -> 11% of each run, Pallas kernels for 0% -> 43%
where the time goes in v2:
time: 575 us; the launch traced here: 563 us
  Pallas kernels  241 us (42%)
  waiting for transfers between devices  159 us (28%)
  starting transfers between devices  67.8 us (12%)
  other arithmetic  45 us (8%)
  local copies, waits for them, and re-layouts  44.6 us (8%)
    ppermute x17, waiting for transfers between devices, along(): return lax.ppermute(x, 'dp', pairs)  118 us
    pallas_call x4, Pallas kernels, expert_part(): pl.pallas_call(functools.partial(expert_kernel, n, first, last, part), gr...  96.2 us
    pallas_call x1, Pallas kernels, scatter_dense(): pl.pallas_call(functools.partial(scatter_kernel, n), out_shape=jax.ShapeD...  66.8 us
    ppermute x17, starting transfers between devices, along(): return lax.ppermute(x, 'dp', pairs)  46.2 us
    pallas_call x1, Pallas kernels, gather_dense(): pl.pallas_call(functools.partial(gather_kernel, n), out_shape=jax.ShapeDt...  35 us
    pallas_call x1, Pallas kernels, attention_backward(): pl.pallas_call(backward_kernel, grid=(count // LEN,), in_specs=[pl.BlockS...  30.4 us
    all_to_all x3, waiting for transfers between devices, exchange(): lax.all_to_all(sent, 'expert', split_axis=0, concat_axis=0, tiled=True)  27.2 us
    add x7, other arithmetic, adam_step(): return (weight + update, new_first, new_square)  17.3 us
  transfers between devices with their start and end apart: 22, of which 8 were waited for; matrix products, arithmetic and copies ran while one was open for 11% of the time, Pallas kernels for 43%

profile of v2, /device:TPU:0, one launch (start us, length us, event | category | flops | bytes accessed | tf_op | source)
XLA Modules:
  0.0 563.5 jit_solution(9470519471530013102)
XLA Ops:
  6.1 5.2 all-to-all-start.2
  11.5 35.0 %gather_dense.1 = bf16[32,112,768]{2,1,0:T(8,128)(2,1)S(1)} custom-call(bf16[112,768]{1,0:T(8,128)(2,1)S(1)} %pad_maximum_fusion.1.in_ref), custom_call_target="tpu_custom_call" | custom-call | bytes 1024 | tf_op jit(solution)/shard_map/gather_dense/pallas_call | solution.py:152
  46.6 2.4 copy-done
  49.7 4.9 slice.108
  54.8 5.0 copy.94
  59.8 13.0 %attention_forward.1 = (bf16[512,768]{1,0:T(8,128)(2,1)S(1)}, bf16[512,768]{1,0:T(8,128)(2,1)S(1)}, bf16[512,768]{1,0:T(8,128)(2,1)S(1)}, bf16[512,768]{1,0:T(8,...) custom-call(s32[2]{0:T(128)S(1)} %copy-done.12, ...), custom_call_target="tpu_custom_call" | custom-call | bytes 1024 | tf_op jit(solution)/shard_map/attention_forward/pallas_call | solution.py:459
  79.6 4.6 all-to-all-start.1
  84.5 2.0 convert_bitcast_fusion.1
  86.5 1.5 pad_maximum_fusion.refs_0_
  88.7 2.1 collective-permute-start.3
  92.9 2.0 copy.103
  94.8 27.2 %all-to-all-done.1 = bf16[8,2,128,768]{3,2,1,0:T(8,128)(2,1)} async-done(((bf16[8,2,128,768]{3,2,1,0:T(8,128)(2,1)}), bf16[8,2,128,768]{3,2,1,0:T(8,128)(2,1)}, u32[]{:S(2)}, u32[]{:S(2)}) %all-to-all-start.1) | async-done | bytes 3145760 | tf_op jit(solution)/shard_map/all_to_all | solution.py:706
  122.1 3.6 all-to-all-start
  126.5 15.9 %collective-permute-done.refs_0_ = bf16[1552,768]{1,0:T(8,128)(2,1)} collective-permute-done((bf16[1552,768]{1,0:T(8,128)(2,1)}, bf16[1552,768]{1,0:T(8,128)(2,1)}, u32[]{:S(2)}, u32[]{:S(2)}) %collective-permute-start) | collective-permute-done | bytes 2383904 | tf_op jit(solution)/shard_map/ppermute | solution.py:640
  142.5 2.1 collective-permute-start.1
  145.2 1.7 collective-permute-start.4
  147.0 2.8 fusion.5
  149.8 13.7 %all-to-all-done = bf16[8,2,128,768]{3,2,1,0:T(8,128)(2,1)S(1)} async-done(((bf16[8,2,128,768]{3,2,1,0:T(8,128)(2,1)}), bf16[8,2,128,768]{3,2,1,0:T(8,128)(2,1)S(1)}, u32[]{:S(2)}, u32[]{:S(2)}) %all-to-all-start) | async-done | bytes 3145760 | tf_op jit(solution)/shard_map/all_to_all | solution.py:696
  165.6 2.3 multiply_convert_fusion.1.refs_2_.refs_3_
  167.9 23.6 %expert_part_0.1 = (f32[2048,768]{1,0:T(8,128)}, f32[2048,768]{1,0:T(8,128)}, f32[768,768]{1,0:T(8,128)}, f32[784,768]{1,0:T(8,128)}) custom-call(bf16[1552,768]{1,0:T(8,128)(2,1)} %pad_maximum_fusion.refs_0_, bf16[2048,768]{1,0:T(8,128)(2,1)} %bitcast.18.refs_1_.refs_2_, bf16[2048,768]{1,0:T(8,128)(2,1)} %multiply_convert_fusion.1.refs_2_.refs_3_, ...), custom_call_target="tpu_custom_call" | custom-call | flops 14495514624 | bytes 31457280 | tf_op jit(solution)/shard_map/expert_part_0/pallas_call | solution.py:342
  192.8 24.4 %expert_part_1.1 = (f32[2048,768]{1,0:T(8,128)}, f32[2048,768]{1,0:T(8,128)}, bf16[768,768]{1,0:T(8,128)(2,1)}, bf16[784,768]{1,0:T(8,128)(2,1)}) custom-call(bf16[1552,768]{1,0:T(8,128)(2,1)} %collective-permute-done.refs_0_, bf16[2048,768]{1,0:T(8,128)(2,1)} %bitcast.18.refs_1_.refs_2_, bf16[2048,768]{1,0:T(8,128)(2,1)} %multiply_convert_fusion.1.refs_2_.refs_3_, ...), custom_call_target="tpu_custom_call" | custom-call | flops 14495514624 | bytes 31457280 | tf_op jit(solution)/shard_map/expert_part_1/pallas_call | solution.py:342
  217.2 13.5 %collective-permute-start.5 = (bf16[768,768]{1,0:T(8,128)(2,1)}, bf16[768,768]{1,0:T(8,128)(2,1)}, u32[]{:S(2)}, u32[]{:S(2)}) collective-permute-start(bf16[768,768]{1,0:T(8,128)(2,1)} %get-tuple-element.119), channel_id=1, source_target_pairs={{0,8},{24,16},{1,9},{25,17},{2,10},{26,18},{3,11},{27,19},{4,12},{... | collective-permute-start | bytes 3538952 | tf_op jit(solution)/shard_map/ppermute | solution.py:640
  232.0 24.4 %expert_part_2.1 = (f32[2048,768]{1,0:T(8,128)}, f32[2048,768]{1,0:T(8,128)}, bf16[768,768]{1,0:T(8,128)(2,1)}, bf16[784,768]{1,0:T(8,128)(2,1)}) custom-call(bf16[1552,768]{1,0:T(8,128)(2,1)} %collective-permute-done.3.refs_0_, bf16[1552,768]{1,0:T(8,128)(2,1)} %collective-permute-done.4.refs_1_, bf16[2048,768]{1,0:T(8,128)(2,1)} %bitcast.18.refs_1_.refs_2_, ...), custom_call_target="tpu_custom_call" | custom-call | flops 14495514624 | bytes 31457280 | tf_op jit(solution)/shard_map/expert_part_2/pallas_call | solution.py:342
  258.4 23.8 %expert_part_3.1 = (bf16[2048,768]{1,0:T(8,128)(2,1)}, bf16[2048,768]{1,0:T(8,128)(2,1)}, bf16[768,768]{1,0:T(8,128)(2,1)}, bf16[784,768]{1,0:T(8,128)(2,1)}) custom-call(bf16[1552,768]{1,0:T(8,128)(2,1)} %collective-permute-done.1.refs_0_, bf16[1552,768]{1,0:T(8,128)(2,1)} %copy-done.42, bf16[2048,768]{1,0:T(8,128)(2,1)} %bitcast.18.refs_1_.refs_2_, ...), custom_call_target="tpu_custom_call" | custom-call | flops 14495514624 | bytes 31457280 | tf_op jit(solution)/shard_map/expert_part_3/pallas_call | solution.py:342
  282.2 3.7 all-to-all-start.3
  288.7 25.7 %collective-permute-done.11 = bf16[784,768]{1,0:T(8,128)(2,1)S(1)} collective-permute-done((bf16[784,768]{1,0:T(8,128)(2,1)}, bf16[784,768]{1,0:T(8,128)(2,1)S(1)}, u32[]{:S(2)}, u32[]{:S(2)}) %collective-permute-start.11) | collective-permute-done | bytes 1204256 | tf_op jit(solution)/shard_map/ppermute | solution.py:640
  315.5 4.3 collective-permute-start.12
  319.9 19.8 %collective-permute-done.6 = bf16[768,768]{1,0:T(8,128)(2,1)S(1)} collective-permute-done((bf16[768,768]{1,0:T(8,128)(2,1)}, bf16[768,768]{1,0:T(8,128)(2,1)S(1)}, u32[]{:S(2)}, u32[]{:S(2)}) %collective-permute-start.6) | collective-permute-done | bytes 1179680 | tf_op jit(solution)/shard_map/ppermute | solution.py:640
  339.7 5.3 collective-permute-start.8
  345.0 20.5 %collective-permute-done.12 = bf16[784,768]{1,0:T(8,128)(2,1)S(1)} collective-permute-done((bf16[784,768]{1,0:T(8,128)(2,1)}, bf16[784,768]{1,0:T(8,128)(2,1)S(1)}, u32[]{:S(2)}, u32[]{:S(2)}) %collective-permute-start.12) | collective-permute-done | bytes 1204256 | tf_op jit(solution)/shard_map/ppermute | solution.py:640
  366.5 5.3 collective-permute-start.14
  371.9 1.6 copy-done.13
  373.5 4.5 all-to-all-start.4
  378.0 12.8 %collective-permute-done.8 = bf16[768,768]{1,0:T(8,128)(2,1)} collective-permute-done((bf16[768,768]{1,0:T(8,128)(2,1)}, bf16[768,768]{1,0:T(8,128)(2,1)}, u32[]{:S(2)}, u32[]{:S(2)}) %collective-permute-start.8) | collective-permute-done | bytes 1179680 | tf_op jit(solution)/shard_map/ppermute | solution.py:640
  390.8 1.9 add_convert_fusion.4
  393.6 22.8 %collective-permute-done.14 = bf16[784,768]{1,0:T(8,128)(2,1)} collective-permute-done((bf16[784,768]{1,0:T(8,128)(2,1)}, bf16[784,768]{1,0:T(8,128)(2,1)}, u32[]{:S(2)}, u32[]{:S(2)}) %collective-permute-start.14) | collective-permute-done | bytes 1204256 | tf_op jit(solution)/shard_map/ppermute | solution.py:640
  416.4 1.6 add_convert_fusion.1
  422.6 1.8 collective-permute-start.13
  429.9 30.4 %attention_backward.1 = (f32[512,768]{1,0:T(8,128)}, f32[512,768]{1,0:T(8,128)}, bf16[4,768,768]{2,1,0:T(8,128)(2,1)}, f32[8,768]{1,0:T(8,128)}, f32[128,768]{1,0:T(8,128)}) custom-call(s32[2]{0:T(128)} %lengths_ref.3, bf16[512,768]{1,0:T(8,128)(2,1)} %tokens_ref.3, bf16[512,768]{1,0:T(8,128)(2,1)} %grad_ref.1, bf16[4,768,768]{2,1,0:T(8,128)(2,1)} %bitcast.87, ...), custom_call_target="tpu_custom_call" | custom-call | bytes 1024 | tf_op jit(solution)/shard_map/attention_backward/pallas_call | solution.py:599
  460.3 5.1 copy.107
  466.9 2.7 maximum_bitcast_fusion
  470.0 66.8 %scatter_dense.1 = f32[112,768]{1,0:T(8,128)S(1)} custom-call(bf16[8,4,112,768]{3,2,1,0:T(8,128)(2,1)S(1)} %bitcast.84), custom_call_target="tpu_custom_call" | custom-call | bytes 1024 | tf_op jit(solution)/shard_map/scatter_dense/pallas_call | solution.py:231
  538.2 1.7 slice.124
  542.6 2.3 multiply_add_fusion.2
  544.9 7.0 %multiply_add_fusion.1 = (f32[1,768,768]{2,1,0:T(8,128)}, f32[1,768,768]{2,1,0:T(8,128)}, f32[1,768,768]{2,1,0:T(8,128)}, f32[768,768]{1,0:T(8,128)}) fusion(f32[1,768,768]{2,1,0:T(8,128)S(1)} %copy-done.15, f32[1,768,768]{2,1,0:T(8,128)} %param.43, f32[1,768,768]{2,1,0:T(8,128)} %param.50, f32[768,768]{1,0:T(8,128)} %get-tuple-element.118, ...), kind=kLoop, calls=%fused_computation.23 | loop fusion | flops 12386304 | bytes 22413312 | tf_op jit(solution)/shard_map/add | solution.py:38
  551.9 2.5 add_add_fusion
  554.4 1.6 slice_bitcast_fusion
  557.7 4.1 multiply_add_fusion
  (190 shorter events, 48.6 us)
Async XLA Ops:
  0.7 10.6 %copy-start.32 = (f32[4,24,768]{2,1,0:T(8,128)S(1)}, f32[4,24,768]{2,1,0:T(8,128)}, u32[]{:S(2)}) copy-start(f32[4,24,768]{2,1,0:T(8,128)} %param.33) | copy-start | bytes 884740
  0.7 10.6 %copy-start.34 = (f32[7,24]{1,0:T(8,128)S(1)}, f32[7,24]{1,0:T(8,128)}, u32[]{:S(2)}) copy-start(f32[7,24]{1,0:T(8,128)} %param.34) | copy-start | bytes 2020
  0.7 10.6 %copy-start.33 = (f32[8,24]{1,0:T(8,128)S(1)}, f32[8,24]{1,0:T(8,128)}, u32[]{:S(2)}) copy-start(f32[8,24]{1,0:T(8,128)} %param.35) | copy-start | bytes 2308
  1.6 58.2 %copy-start.1 = (s32[512,2]{1,0:T(8,128)}, s32[512,2]{1,0:T(8,128)S(1)}, u32[]{:S(2)}) copy-start(s32[512,2]{1,0:T(8,128)S(1)} %copy.106.routes_ref) | copy-start | bytes 12292
  6.1 73.5 %all-to-all-start.2 = ((f32[8,2,128]{2,1,0:T(2,128)}), f32[8,2,128]{2,1,0:T(2,128)S(1)}, u32[]{:S(2)}, u32[]{:S(2)}) async-start(f32[8,2,128]{2,1,0:T(2,128)} %convert_bitcast_fusion.3), calls=%async_computation.2 | async-start | bytes 16384 | tf_op jit(solution)/shard_map/all_to_all | solution.py:691
  49.7 10.1 %copy-start.11 = (f32[8,768]{1,0:T(8,128)}, f32[8,768]{1,0:T(8,128)S(1)}, u32[]{:S(2)}) copy-start(f32[8,768]{1,0:T(8,128)S(1)} %pad_convert_fusion.vector_ref) | copy-start | bytes 73732
  54.8 5.0 copy-start.2
  54.8 5.0 copy-start.12
  79.6 4.6 copy-start.35
  79.6 4.7 copy-start.37
  79.6 4.9 copy-start.14
  79.6 42.5 %all-to-all-start.1 = ((bf16[8,2,128,768]{3,2,1,0:T(8,128)(2,1)}), bf16[8,2,128,768]{3,2,1,0:T(8,128)(2,1)}, u32[]{:S(2)}, u32[]{:S(2)}) async-start(bf16[8,2,128,768]{3,2,1,0:T(8,128)(2,1)} %get-tuple-element.104), calls=%async_computation.1 | async-start | bytes 6291456 | tf_op jit(solution)/shard_map/all_to_all | solution.py:706
  86.5 5.3 copy-start.17
  88.1 54.4 %collective-permute-start = (bf16[1552,768]{1,0:T(8,128)(2,1)}, bf16[1552,768]{1,0:T(8,128)(2,1)}, u32[]{:S(2)}, u32[]{:S(2)}) collective-permute-start(bf16[1552,768]{1,0:T(8,128)(2,1)} %pad_maximum_fusion.refs_0_), channel_id=1, source_target_pairs={{0,8},{8,0},{16,24},{24,16},{1,9},{9,1},{17,25},{25,17},{2,10},{10... | collective-permute-start | bytes 7151624 | tf_op jit(solution)/shard_map/ppermute | solution.py:640
  88.7 56.5 %collective-permute-start.3 = (bf16[1552,768]{1,0:T(8,128)(2,1)}, bf16[1552,768]{1,0:T(8,128)(2,1)}, u32[]{:S(2)}, u32[]{:S(2)}) collective-permute-start(bf16[1552,768]{1,0:T(8,128)(2,1)} %pad_maximum_fusion.refs_0_), channel_id=1, source_target_pairs={{8,16},{16,8},{9,17},{17,9},{10,18},{18,10},{11,19},{19,11},{12,20... | collective-permute-start | bytes 7151624 | tf_op jit(solution)/shard_map/ppermute | solution.py:640
  122.1 41.5 %all-to-all-start = ((bf16[8,2,128,768]{3,2,1,0:T(8,128)(2,1)}), bf16[8,2,128,768]{3,2,1,0:T(8,128)(2,1)S(1)}, u32[]{:S(2)}, u32[]{:S(2)}) async-start(bf16[8,2,128,768]{3,2,1,0:T(8,128)(2,1)} %copy.103), calls=%async_computation | async-start | bytes 6291456 | tf_op jit(solution)/shard_map/all_to_all | solution.py:696
  142.5 49.0 %collective-permute-start.1 = (bf16[1552,768]{1,0:T(8,128)(2,1)}, bf16[1552,768]{1,0:T(8,128)(2,1)}, u32[]{:S(2)}, u32[]{:S(2)}) collective-permute-start(bf16[1552,768]{1,0:T(8,128)(2,1)} %collective-permute-done.refs_0_), channel_id=1, source_target_pairs={{8,16},{16,8},{9,17},{17,9},{10,18},{18,10},{11,19},{19,11},{12,20... | collective-permute-start | bytes 7151624 | tf_op jit(solution)/shard_map/ppermute | solution.py:640
  145.2 86.1 %collective-permute-start.4 = (bf16[1552,768]{1,0:T(8,128)(2,1)}, bf16[1552,768]{1,0:T(8,128)(2,1)}, u32[]{:S(2)}, u32[]{:S(2)}) collective-permute-start(bf16[1552,768]{1,0:T(8,128)(2,1)} %collective-permute-done.3.refs_0_), channel_id=1, source_target_pairs={{8,0},{16,24},{9,1},{17,25},{10,2},{18,26},{11,3},{19,27},{12,4},{... | collective-permute-start | bytes 7151624 | tf_op jit(solution)/shard_map/ppermute | solution.py:640
  191.5 64.9 %collective-permute-start.2 = (bf16[1552,768]{1,0:T(8,128)(2,1)}, bf16[1552,768]{1,0:T(8,128)(2,1)S(1)}, u32[]{:S(2)}, u32[]{:S(2)}) collective-permute-start(bf16[1552,768]{1,0:T(8,128)(2,1)} %collective-permute-done.1.refs_0_), channel_id=1, source_target_pairs={{8,0},{16,24},{9,1},{17,25},{10,2},{18,26},{11,3},{19,27},{12,4},{... | collective-permute-start | bytes 7151624 | tf_op jit(solution)/shard_map/ppermute | solution.py:640
  217.2 70.2 %collective-permute-start.5 = (bf16[768,768]{1,0:T(8,128)(2,1)}, bf16[768,768]{1,0:T(8,128)(2,1)}, u32[]{:S(2)}, u32[]{:S(2)}) collective-permute-start(bf16[768,768]{1,0:T(8,128)(2,1)} %get-tuple-element.119), channel_id=1, source_target_pairs={{0,8},{24,16},{1,9},{25,17},{2,10},{26,18},{3,11},{27,19},{4,12},{... | collective-permute-start | bytes 3538952 | tf_op jit(solution)/shard_map/ppermute | solution.py:640
  282.2 89.7 %all-to-all-start.3 = ((bf16[8,2,128,768]{3,2,1,0:T(8,128)(2,1)}), bf16[8,2,128,768]{3,2,1,0:T(8,128)(2,1)S(1)}, u32[]{:S(2)}, u32[]{:S(2)}) async-start(bf16[8,2,128,768]{3,2,1,0:T(8,128)(2,1)} %bitcast.93), calls=%async_computation.3 | async-start | bytes 6291456 | tf_op jit(solution)/shard_map/all_to_all | solution.py:706
  286.0 28.5 %collective-permute-start.11 = (bf16[784,768]{1,0:T(8,128)(2,1)}, bf16[784,768]{1,0:T(8,128)(2,1)S(1)}, u32[]{:S(2)}, u32[]{:S(2)}) collective-permute-start(bf16[784,768]{1,0:T(8,128)(2,1)} %get-tuple-element.125), channel_id=1, source_target_pairs={{0,8},{24,16},{1,9},{25,17},{2,10},{26,18},{3,11},{27,19},{4,12},{... | collective-permute-start | bytes 3612680 | tf_op jit(solution)/shard_map/ppermute | solution.py:640
  287.3 52.4 %collective-permute-start.6 = (bf16[768,768]{1,0:T(8,128)(2,1)}, bf16[768,768]{1,0:T(8,128)(2,1)S(1)}, u32[]{:S(2)}, u32[]{:S(2)}) collective-permute-start(bf16[768,768]{1,0:T(8,128)(2,1)} %get-tuple-element.121), channel_id=1, source_target_pairs={{0,8},{24,16},{1,9},{25,17},{2,10},{26,18},{3,11},{27,19},{4,12},{... | collective-permute-start | bytes 3538952 | tf_op jit(solution)/shard_map/ppermute | solution.py:640
  315.5 50.0 %collective-permute-start.12 = (bf16[784,768]{1,0:T(8,128)(2,1)}, bf16[784,768]{1,0:T(8,128)(2,1)S(1)}, u32[]{:S(2)}, u32[]{:S(2)}) collective-permute-start(bf16[784,768]{1,0:T(8,128)(2,1)} %get-tuple-element.127), channel_id=1, source_target_pairs={{0,8},{24,16},{1,9},{25,17},{2,10},{26,18},{3,11},{27,19},{4,12},{... | collective-permute-start | bytes 3612680 | tf_op jit(solution)/shard_map/ppermute | solution.py:640
  339.7 25.8 %copy-start.30 = (bf16[768,768]{1,0:T(8,128)(2,1)}, bf16[768,768]{1,0:T(8,128)(2,1)S(1)}, u32[]{:S(2)}) copy-start(bf16[768,768]{1,0:T(8,128)(2,1)S(1)} %collective-permute-done.6) | copy-start | bytes 3538948
  339.7 51.1 %collective-permute-start.8 = (bf16[768,768]{1,0:T(8,128)(2,1)}, bf16[768,768]{1,0:T(8,128)(2,1)}, u32[]{:S(2)}, u32[]{:S(2)}) collective-permute-start(bf16[768,768]{1,0:T(8,128)(2,1)} %get-tuple-element.123), channel_id=1, source_target_pairs={{0,8},{24,16},{1,9},{25,17},{2,10},{26,18},{3,11},{27,19},{4,12},{... | collective-permute-start | bytes 3538952 | tf_op jit(solution)/shard_map/ppermute | solution.py:640
  366.5 49.9 %collective-permute-start.14 = (bf16[784,768]{1,0:T(8,128)(2,1)}, bf16[784,768]{1,0:T(8,128)(2,1)}, u32[]{:S(2)}, u32[]{:S(2)}) collective-permute-start(bf16[784,768]{1,0:T(8,128)(2,1)} %get-tuple-element.129), channel_id=1, source_target_pairs={{0,8},{24,16},{1,9},{25,17},{2,10},{26,18},{3,11},{27,19},{4,12},{... | collective-permute-start | bytes 3612680 | tf_op jit(solution)/shard_map/ppermute | solution.py:640
  373.5 56.4 %all-to-all-start.4 = ((bf16[8,2,128,768]{3,2,1,0:T(8,128)(2,1)}), bf16[8,2,128,768]{3,2,1,0:T(8,128)(2,1)}, u32[]{:S(2)}, u32[]{:S(2)}) async-start(bf16[8,2,128,768]{3,2,1,0:T(8,128)(2,1)} %bitcast.92), calls=%async_computation.4 | async-start | bytes 6291456 | tf_op jit(solution)/shard_map/all_to_all | solution.py:706
  378.0 38.4 %copy-start.23 = (bf16[784,768]{1,0:T(8,128)(2,1)S(1)}, bf16[784,768]{1,0:T(8,128)(2,1)}, u32[]{:S(2)}) copy-start(bf16[784,768]{1,0:T(8,128)(2,1)} %get-tuple-element.129) | copy-start | bytes 3612676
  392.7 26.3 %copy-start.29 = (bf16[768,768]{1,0:T(8,128)(2,1)S(1)}, bf16[768,768]{1,0:T(8,128)(2,1)}, u32[]{:S(2)}) copy-start(bf16[768,768]{1,0:T(8,128)(2,1)} %get-tuple-element.121) | copy-start | bytes 3538948
  392.7 26.3 %copy-start.31 = (bf16[768,768]{1,0:T(8,128)(2,1)S(1)}, bf16[768,768]{1,0:T(8,128)(2,1)}, u32[]{:S(2)}) copy-start(bf16[768,768]{1,0:T(8,128)(2,1)} %copy-done.30) | copy-start | bytes 3538948
  392.7 31.7 %collective-permute-start.9 = (bf16[768,768]{1,0:T(8,128)(2,1)S(1)}, bf16[768,768]{1,0:T(8,128)(2,1)S(1)}, u32[]{:S(2)}, u32[]{:S(2)}) collective-permute-start(bf16[768,768]{1,0:T(8,128)(2,1)S(1)} %add_convert_fusion.4), channel_id=1, source_target_pairs={{8,16},{16,8},{9,17},{17,9},{10,18},{18,10},{11,19},{19,11},{12,20... | collective-permute-start | bytes 3538952 | tf_op jit(solution)/shard_map/ppermute | solution.py:640
  418.1 8.9 %collective-permute-start.15 = (bf16[784,768]{1,0:T(8,128)(2,1)S(1)}, bf16[784,768]{1,0:T(8,128)(2,1)S(1)}, u32[]{:S(2)}, u32[]{:S(2)}) collective-permute-start(bf16[784,768]{1,0:T(8,128)(2,1)S(1)} %add_convert_fusion.1), channel_id=1, source_target_pairs={{8,16},{16,8},{9,17},{17,9},{10,18},{18,10},{11,19},{19,11},{12,20... | collective-permute-start | bytes 3612680 | tf_op jit(solution)/shard_map/ppermute | solution.py:640
  420.3 4.1 copy-start.28
  420.3 124.5 %collective-permute-start.7 = (bf16[768,768]{1,0:T(8,128)(2,1)}, bf16[768,768]{1,0:T(8,128)(2,1)S(1)}, u32[]{:S(2)}, u32[]{:S(2)}) collective-permute-start(bf16[768,768]{1,0:T(8,128)(2,1)} %add_convert_fusion.5), channel_id=1, source_target_pairs={{8,16},{16,8},{9,17},{17,9},{10,18},{18,10},{11,19},{19,11},{12,20... | collective-permute-start | bytes 3538952 | tf_op jit(solution)/shard_map/ppermute | solution.py:640
  422.6 4.4 copy-start.21
  422.6 129.3 %collective-permute-start.13 = (bf16[784,768]{1,0:T(8,128)(2,1)}, bf16[784,768]{1,0:T(8,128)(2,1)}, u32[]{:S(2)}, u32[]{:S(2)}) collective-permute-start(bf16[784,768]{1,0:T(8,128)(2,1)} %add_convert_fusion.2), channel_id=1, source_target_pairs={{8,16},{16,8},{9,17},{17,9},{10,18},{18,10},{11,19},{19,11},{12,20... | collective-permute-start | bytes 3612680 | tf_op jit(solution)/shard_map/ppermute | solution.py:640
  425.7 119.1 %collective-permute-start.10 = (bf16[768,768]{1,0:T(8,128)(2,1)}, bf16[768,768]{1,0:T(8,128)(2,1)}, u32[]{:S(2)}, u32[]{:S(2)}) collective-permute-start(bf16[768,768]{1,0:T(8,128)(2,1)} %add_convert_fusion.3), channel_id=1, source_target_pairs={{8,0},{16,24},{9,1},{17,25},{10,2},{18,26},{11,3},{19,27},{12,4},{... | collective-permute-start | bytes 3538952 | tf_op jit(solution)/shard_map/ppermute | solution.py:640
  428.4 123.5 %collective-permute-start.16 = (bf16[784,768]{1,0:T(8,128)(2,1)}, bf16[784,768]{1,0:T(8,128)(2,1)}, u32[]{:S(2)}, u32[]{:S(2)}) collective-permute-start(bf16[784,768]{1,0:T(8,128)(2,1)} %add_convert_fusion), channel_id=1, source_target_pairs={{8,0},{16,24},{9,1},{17,25},{10,2},{18,26},{11,3},{19,27},{12,4},{... | collective-permute-start | bytes 3612680 | tf_op jit(solution)/shard_map/ppermute | solution.py:640
  460.3 5.9 %copy-start.36 = (f32[8,768]{1,0:T(8,128)S(1)}, f32[8,768]{1,0:T(8,128)}, u32[]{:S(2)}) copy-start(f32[8,768]{1,0:T(8,128)} %get-tuple-element.116) | copy-start | bytes 73732
  536.8 8.0 %copy-start.15 = (f32[1,768,768]{2,1,0:T(8,128)S(1)}, f32[1,768,768]{2,1,0:T(8,128)}, u32[]{:S(2)}) copy-start(f32[1,768,768]{2,1,0:T(8,128)} %param.36) | copy-start | bytes 7077892
  544.8 7.0 %copy-start.18 = (f32[784,768]{1,0:T(8,128)S(1)}, f32[784,768]{1,0:T(8,128)}, u32[]{:S(2)}) copy-start(f32[784,768]{1,0:T(8,128)} %get-tuple-element.124) | copy-start | bytes 7225348
  544.9 7.0 %copy-start.27 = (bf16[784,768]{1,0:T(8,128)(2,1)S(1)}, bf16[784,768]{1,0:T(8,128)(2,1)}, u32[]{:S(2)}) copy-start(bf16[784,768]{1,0:T(8,128)(2,1)} %copy-done.26) | copy-start | bytes 3612676
  551.9 4.1 copy-start.20
  557.7 4.2 copy-start.38
  557.7 4.2 copy-start.39
  557.7 4.8 copy-start.40
  557.7 4.8 copy-start.41
  (17 other events, 27.0 us)

commit v3 on v2

--- a/solution.py
+++ b/solution.py
@@ -504,59 +504,55 @@
     return jnp.sum(values, axis=0, keepdims=True)
 
 
-def backward_kernel(
-    lengths_ref, tokens_ref, grad_ref, weights_ref, vector_ref, router_ref, routes_ref, places_ref,
+def sequence_backward(
+    s, lengths_ref, tokens_ref, grad_ref, weights_ref, vector_ref, router_ref, routes_ref, places_ref,
     normed_ref, q_ref, k_ref, v_ref, context_ref, lse_ref, resid_ref, normed_two_ref, gates_ref, outs_ref, returned_ref,
-    output_ref, input_grad_ref, grad_weights_ref, grad_vector_ref, grad_router_ref,
-    weights_acc, vector_acc, router_acc, dq_ref, dk_ref, dv_ref,
+    output_ref, input_grad_ref, weights_acc, vector_acc, router_acc, dq_ref, dk_ref, dv_ref,
 ):
-    step = pl.program_id(0)
-    length = lengths_ref[step]
-
-    @pl.when(step == 0)
-    def _():
-        weights_acc[...] = jnp.zeros_like(weights_acc)
-        vector_acc[...] = jnp.zeros_like(vector_acc)
-        router_acc[...] = jnp.zeros_like(router_acc)
-
-    slots = outs_ref.shape[0] * outs_ref.shape[2]
+    at = pl.ds(s * LEN, LEN)
+    length = lengths_ref[s]
+    experts, _, capacity, _ = outs_ref.shape
+    slots = experts * capacity
     ids = lax.broadcasted_iota(jnp.int32, (ROWS, slots), 1)
-    outs = outs_ref[...].reshape(slots, D)
-    returned = returned_ref[...].reshape(slots, D)
-    grad_out = grad_ref[...].astype(f32)
-    take = [jnp.where(ids == places_ref[:, k : k + 1], 1.0, 0.0).astype(b16) for k in range(2)]
+    outs = outs_ref[:, s].reshape(slots, D)
+    grad_out = grad_ref[at, :].astype(f32)
+    places = places_ref[at, :]
+    take = [jnp.where(ids == places[:, k : k + 1], 1.0, 0.0).astype(b16) for k in range(2)]
     out = [dot(t, outs, NN) for t in take]
-    gates = [gates_ref[:, k : k + 1] for k in range(2)]
-    resid = resid_ref[...]
-    output_ref[...] = resid + gates[0] * out[0] + gates[1] * out[1]
+    both_gates = gates_ref[at, :]
+    gates = [both_gates[:, k : k + 1] for k in range(2)]
+    resid = resid_ref[at, :]
+    output_ref[at, :] = resid + gates[0] * out[0] + gates[1] * out[1]
     slopes = [
         jnp.sum(grad_out * out[k], axis=-1, keepdims=True) * (gates[k] * (1.0 - gates[k])) for k in range(2)
     ]
     pull = slopes[0] - slopes[1]
     names = lax.broadcasted_iota(jnp.int32, (ROWS, 128), 1)
-    grad_logits = jnp.where(names == routes_ref[:, 0:1], pull, jnp.where(names == routes_ref[:, 1:2], -pull, 0.0))
+    routes = routes_ref[at, :]
+    grad_logits = jnp.where(names == routes[:, 0:1], pull, jnp.where(names == routes[:, 1:2], -pull, 0.0))
     high, low = two_terms(grad_logits)
-    normed_two = normed_two_ref[...]
+    normed_two = normed_two_ref[at, :]
     router = router_ref[...]
     router_acc[...] += dot(high, normed_two, TN) + dot(low, normed_two, TN)
+    returned = returned_ref[:, s].reshape(slots, D)
     grad_two = dot(take[0] + take[1], returned, NN) + (dot(high, router, NN) + dot(low, router, NN))
     hat, rate = normal(resid)
     vector_acc[5:6, :] += column_sum(grad_two * hat)
     vector_acc[6:7, :] += column_sum(grad_two)
     grad_resid = grad_out + norm_back(grad_two, hat, rate, vector_ref[5:6, :])
-    input_grad_ref[...] = grad_resid
+    input_grad_ref[at, :] = grad_resid
     branch = grad_resid.astype(b16)
     vector_acc[4:5, :] += column_sum(branch.astype(f32))
-    weights_acc[3] += dot(context_ref[...], branch, TN)
+    weights_acc[3] += dot(context_ref[at, :], branch, TN)
     grad_context = dot(branch, weights_ref[3], NT).astype(b16)
     for pair in range(PAIRS):
         lanes = slice(pair * WIDE, (pair + 1) * WIDE)
-        queries, keys, values = q_ref[:, lanes], k_ref[:, lanes], v_ref[:, lanes]
+        queries, keys, values = q_ref[at, lanes], k_ref[at, lanes], v_ref[at, lanes]
         given = grad_context[:, lanes]
         grads = []
         for half, (part, part_given) in enumerate(zip(halves(queries), halves(given))):
             head = 2 * pair + half
-            chance = jnp.exp(scores_of(part, keys, length) - lse_ref[:, head : head + 1])
+            chance = jnp.exp(scores_of(part, keys, length) - lse_ref[at, head : head + 1])
             grad_v = dot(chance.astype(b16), given, TN)
             grad_chance = dot(part_given, values, NT)
             mean = jnp.sum(chance * grad_chance, axis=-1, keepdims=True)
@@ -565,63 +561,261 @@
         dq_ref[:, lanes] = (joined(grads[0][0], grads[1][0]) * SCALE).astype(b16)
         dk_ref[:, lanes] = (joined(grads[0][1], grads[1][1]) * SCALE).astype(b16)
         dv_ref[:, lanes] = joined(grads[0][2], grads[1][2]).astype(b16)
-    normed = normed_ref[...]
+    normed = normed_ref[at, :]
     grad_one = jnp.zeros((LEN, D), f32)
     for k, ref in enumerate((dq_ref, dk_ref, dv_ref)):
         weights_acc[k] += dot(normed, ref[...], TN)
         grad_one += dot(ref[...], weights_ref[k], NT)
     vector_acc[2:3, :] += column_sum(dq_ref[...].astype(f32))
     vector_acc[3:4, :] += column_sum(dv_ref[...].astype(f32))
-    hat, rate = normal(tokens_ref[...].astype(f32))
+    hat, rate = normal(tokens_ref[at, :].astype(f32))
     vector_acc[0:1, :] += column_sum(grad_one * hat)
     vector_acc[1:2, :] += column_sum(grad_one)
-    input_grad_ref[...] += norm_back(grad_one, hat, rate, vector_ref[0:1, :])
-
-    @pl.when(step == pl.num_programs(0) - 1)
+    input_grad_ref[at, :] += norm_back(grad_one, hat, rate, vector_ref[0:1, :])
+
+
+KINDS = 6
+FAR, MIDDLE, NEAR, FAR_ON, MIDDLE_ON, FAR_LAST = range(KINDS)
+
+
+def finish_kernel(
+    n, cols, extra, seqs,
+    lengths_ref, tokens_ref, grad_ref, weights_ref, vector_ref, router_ref, routes_ref, places_ref,
+    normed_ref, q_ref, k_ref, v_ref, context_ref, lse_ref, resid_ref, normed_two_ref, gates_ref, outs_ref, backs_ref,
+    near_up, near_down, middle_up, middle_down, far_up, far_down,
+    output_ref, input_grad_ref, dense_ref, near_up_in, near_down_in, middle_up_in, middle_down_in, end_up_in, end_down_in,
+    outs_in, backs_in, weights_acc, vector_acc, router_acc, dq_ref, dk_ref, dv_ref,
+    far_up_buf, far_down_buf, middle_up_buf, middle_down_buf, on_up_buf, on_down_buf, load_up, load_down,
+    parts, stage, c_buf, b_buf, a_buf, z_buf,
+    own_s, out_s, out_r, back_s, back_r, chain_s, chain_r, load_s, c_s, c_r, b_s, b_r, a_s, a_r, z_s, z_r,
+):
+    inside = cols % 8 == 0
+    side, z, y, x, core = where_am_i()
+    mine = lax.axis_index("expert")
+    experts = outs_in.shape[0]
+    along_z, first, second, sibling = peers_of(n, side, z, y, x, core)
+    plane = [(z, (mine + k) % experts) for k in range(1, experts)]
+    greet([*along_z, *plane])
+    area = side * side if inside else 0
+    sent = []
+
+    def remote(src, dst, send, recv, peer):
+        return pltpu.make_async_remote_copy(
+            src_ref=src, dst_ref=dst, send_sem=send, recv_sem=recv, device_id=peer, device_id_type=MESH
+        )
+
+    def send(src, dst, send_sem, recv_sem, peer):
+        copy = remote(src, dst, send_sem, recv_sem, peer)
+        copy.start()
+        sent.append(copy)
+
+    for k in range(1, experts):
+        to = (mine + k) % experts
+        send(outs_ref.at[to], outs_in.at[mine], out_s.at[k], out_r.at[k], plane[k - 1])
+    for k in range(1, experts):
+        to = (mine + k) % experts
+        send(backs_ref.at[to], backs_in.at[mine], back_s.at[k], back_r.at[k], plane[k - 1])
+    own = [
+        pltpu.make_async_copy(outs_ref.at[mine], outs_in.at[mine], own_s.at[0]),
+        pltpu.make_async_copy(backs_ref.at[mine], backs_in.at[mine], own_s.at[1]),
+    ]
+    for copy in own:
+        copy.start()
+
+    inner = (z + 1) // 2 % 2 == 1
+    outer = jnp.logical_not(inner)
+    inward = (z - z + 1 + z // 2, mine)
+    across = (3 - z, mine)
+    outward = (3 * (z // 2), mine)
+    near, middle, far = (near_up, near_down), (middle_up, middle_down), (far_up, far_down)
+    near_in, middle_in = (near_up_in, near_down_in), (middle_up_in, middle_down_in)
+    end_in = (end_up_in, end_down_in)
+    far_buf, middle_buf, on_buf = (far_up_buf, far_down_buf), (middle_up_buf, middle_down_buf), (on_up_buf, on_down_buf)
+    loads = (load_up, load_down)
+
+    def hop(kind, half, src, dst, peer):
+        return remote(src, dst, chain_s.at[kind, half], chain_r.at[kind, half], peer)
+
+    from_ends = [(FAR, far, far_buf), (MIDDLE, middle, middle_buf), (NEAR, near, near_in)]
+
+    @pl.when(outer)
     def _():
+        for kind, src, dst in from_ends:
+            for half in range(2):
+                hop(kind, half, src[half], dst[half], inward).start()
+
+    def chain_step(kind, half, buf, term, next_kind, target, peer):
+        @pl.when(inner)
+        def _():
+            load = pltpu.make_async_copy(term[half], loads[half], load_s)
+            load.start()
+            hop(kind, half, buf[half], buf[half], across).wait_recv()
+            load.wait()
+            buf[half][...] = (buf[half][...].astype(f32) + loads[half][...].astype(f32)).astype(b16)
+            hop(next_kind, half, buf[half], target[half], peer).start()
+
+    def step_far(half):
+        chain_step(FAR, half, far_buf, far, FAR_ON, on_buf, across)
+
+    def step_on(half):
+        chain_step(FAR_ON, half, on_buf, near, FAR_LAST, end_in, outward)
+
+    def step_middle(half):
+        chain_step(MIDDLE, half, middle_buf, middle, MIDDLE_ON, middle_in, across)
+
+    weights_acc[...] = jnp.zeros_like(weights_acc)
+    vector_acc[...] = jnp.zeros_like(vector_acc)
+    router_acc[...] = jnp.zeros_like(router_acc)
+    step_far(0)
+    step_far(1)
+    step_on(0)
+    for copy in own:
+        copy.wait()
+    for k in range(1, experts):
+        block = outs_in.at[(mine - k + experts) % experts]
+        remote(block, block, out_s.at[k], out_r.at[k], sibling).wait_recv()
+        block = backs_in.at[(mine - k + experts) % experts]
+        remote(block, block, back_s.at[k], back_r.at[k], sibling).wait_recv()
+    for s in range(seqs):
+        sequence_backward(
+            s, lengths_ref, tokens_ref, grad_ref, weights_ref, vector_ref, router_ref, routes_ref, places_ref,
+            normed_ref, q_ref, k_ref, v_ref, context_ref, lse_ref, resid_ref, normed_two_ref, gates_ref, outs_in, backs_in,
+            output_ref, input_grad_ref, weights_acc, vector_acc, router_acc, dq_ref, dk_ref, dv_ref,
+        )
+        if s == 0:
+            step_on(1)
+            step_middle(0)
+
+    small = jnp.concatenate([vector_acc[...], router_acc[: extra - 8, :]], axis=0).astype(b16)
+    if not inside:
+        dense_ref[:extra, :] = jnp.concatenate([vector_acc[...], router_acc[: extra - 8, :]], axis=0)
         for k in range(4):
-            grad_weights_ref[k] = weights_acc[k].astype(b16)
-        grad_vector_ref[...] = vector_acc[...]
-        grad_router_ref[...] = router_acc[...]
-
-
-def attention_backward(lengths, tokens, out_grad, weights, vector, router, routes, places, kept, outs, returned):
-    count = tokens.shape[0]
-    experts, _, capacity, _ = outs.shape
-    rows = pl.BlockSpec((LEN, D), lambda i: (i, 0))
-    lanes = pl.BlockSpec((LEN, 128), lambda i: (i, 0))
-    pairs = pl.BlockSpec((LEN, 2), lambda i: (i, 0))
-    slots = pl.BlockSpec((experts, 1, capacity, D), lambda i: (0, i, 0, 0))
-
-    def fixed(*shape):
-        return pl.BlockSpec(shape, lambda i: (0,) * len(shape), pipeline_mode=pl.Buffered(1))
-
+            dense_ref[extra + k * D : extra + (k + 1) * D, :] = weights_acc[k]
+        step_middle(1)
+    for core_ in range(2 if inside else 0):
+        for y_ in range(side):
+            for x_ in range(side):
+                for z_ in range(n):
+                    owner = ((z_ * side + y_) * side + x_) * 2 + core_
+                    rows = [weights_acc[k, owner * cols : (owner + 1) * cols, :] for k in range(4)]
+                    place = parts.at[(core_ * side + y_) * side + x_, z_]
+                    place[: 4 * cols, :] = jnp.concatenate(rows, axis=0).astype(b16)
+                    place[4 * cols :, :] = small
+
+    def piece(ka, kb, core_):
+        y_ = (y + core * ka + (1 - core) * kb) % side
+        x_ = (x + (1 - core) * ka + core * kb) % side
+        return (core_ * side + y_) * side + x_
+
+    order = [(ka, kb) for kb in [*range(1, side), 0] for ka in [*range(1, side), 0]][:area]
+    for ka, kb in order:
+        place = ka * side + kb
+        send(parts.at[piece(kb, ka, 1 - core)], c_buf.at[place], c_s.at[place], c_r.at[place], sibling)
+    for ka, kb in order:
+        place = ka * side + kb
+        remote(c_buf.at[place], c_buf.at[place], c_s.at[place], c_r.at[place], sibling).wait_recv()
+        mine_ = piece(ka, kb, core)
+        if kb:
+            stage[place] = (parts[mine_].astype(f32) + c_buf[place].astype(f32)).astype(b16)
+            send(stage.at[place], b_buf.at[place], b_s.at[place], b_r.at[place], second[kb - 1])
+            if ka == 0:
+                step_middle(1)
+        else:
+            total = parts[mine_].astype(f32) + c_buf[place].astype(f32)
+            for k in range(1, side):
+                slot = ka * side + k
+                remote(b_buf.at[slot], b_buf.at[slot], b_s.at[slot], b_r.at[slot], sibling).wait_recv()
+                total = total + b_buf[slot].astype(f32)
+            if ka:
+                stage[place] = total.astype(b16)
+                send(stage.at[place], a_buf.at[ka], a_s.at[ka], a_r.at[ka], first[ka - 1])
+            else:
+                for k in range(1, side):
+                    remote(a_buf.at[k], a_buf.at[k], a_s.at[k], a_r.at[k], sibling).wait_recv()
+                    total = total + a_buf[k].astype(f32)
+                stage[place] = total.astype(b16)
+    if inside:
+        for k in range(1, n):
+            send(stage.at[0, (z + k) % n], z_buf.at[k], z_s.at[k], z_r.at[k], along_z[k - 1])
+        result = stage[0, z].astype(f32)
+        for k in range(1, n):
+            remote(z_buf.at[k], z_buf.at[k], z_s.at[k], z_r.at[k], sibling).wait_recv()
+            result = result + z_buf[k].astype(f32)
+        dense_ref[...] = result
+    for copy in sent:
+        copy.wait_send()
+
+    @pl.when(outer)
+    def _():
+        for half in range(2):
+            for kind, src, dst in from_ends:
+                hop(kind, half, src[half], dst[half], inward).wait_send()
+            hop(FAR_LAST, half, end_in[half], end_in[half], inward).wait_recv()
+
+    @pl.when(inner)
+    def _():
+        for half in range(2):
+            hop(FAR_ON, half, far_buf[half], on_buf[half], across).wait_send()
+            hop(FAR_LAST, half, on_buf[half], end_in[half], outward).wait_send()
+            hop(MIDDLE_ON, half, middle_buf[half], middle_in[half], across).wait_send()
+            hop(MIDDLE_ON, half, middle_in[half], middle_in[half], across).wait_recv()
+            hop(NEAR, half, near_in[half], near_in[half], outward).wait_recv()
+
+
+def finish(n, side, cols, extra, lengths, rows_in, kept, outs, backs, grads):
+    count = rows_in[0].shape[0]
+    slots = outs.shape
+    vmem = pl.BlockSpec(memory_space=pltpu.VMEM)
+    hbm = pl.BlockSpec(memory_space=pl.ANY)
+    shapes = [jax.ShapeDtypeStruct(g.shape, b16) for g in grads[:2]]
+    inside = cols % 8 == 0
+    rows = 4 * cols + extra if inside else 4 * D + extra
+    block = (n, rows, D) if inside else (1, 16, 128)
+    dma = pltpu.SemaphoreType.DMA
+    half = [pltpu.VMEM(g.shape, b16) for g in grads[:2]]
+    area = side * side
     return pl.pallas_call(
-        backward_kernel,
-        grid=(count // LEN,),
+        functools.partial(finish_kernel, n, cols, extra, count // LEN),
         in_specs=[
             pl.BlockSpec(memory_space=pltpu.SMEM),
-            rows, rows, fixed(4, D, D), fixed(8, D), fixed(128, D), pairs, pairs,
-            rows, rows, rows, rows, rows, lanes, rows, rows, lanes, slots, slots,
-        ],
-        out_specs=[rows, rows, fixed(4, D, D), fixed(8, D), fixed(128, D)],
+            *[vmem] * (len(rows_in) + len(kept)),
+            hbm,
+            hbm,
+            *[hbm] * len(grads),
+        ],
+        out_specs=[vmem, vmem, vmem, *[hbm] * 6],
         out_shape=[
             jax.ShapeDtypeStruct((count, D), f32),
             jax.ShapeDtypeStruct((count, D), f32),
-            jax.ShapeDtypeStruct((4, D, D), b16),
-            jax.ShapeDtypeStruct((8, D), f32),
-            jax.ShapeDtypeStruct((128, D), f32),
+            jax.ShapeDtypeStruct((rows, D), f32),
+            *shapes * 3,
         ],
         scratch_shapes=[
+            pltpu.VMEM(slots, b16),
+            pltpu.VMEM(slots, b16),
             pltpu.VMEM((4, D, D), f32),
             pltpu.VMEM((8, D), f32),
             pltpu.VMEM((128, D), f32),
             *[pltpu.VMEM((LEN, D), b16)] * 3,
-        ],
-        compiler_params=pltpu.CompilerParams(vmem_limit_bytes=58 << 20),
+            *half * 4,
+            pltpu.VMEM((2 * area, *block), b16),
+            pltpu.VMEM((area, *block), b16),
+            pltpu.VMEM((area, *block), b16),
+            pltpu.VMEM((area, *block), b16),
+            pltpu.VMEM((side, *block), b16),
+            pltpu.VMEM(block, b16),
+            dma((2,)),
+            *[dma((slots[0],))] * 4,
+            *[dma((KINDS, 2))] * 2,
+            dma,
+            *[dma((area,))] * 4,
+            *[dma((side,))] * 2,
+            *[dma((n,))] * 2,
+        ],
+        compiler_params=pltpu.CompilerParams(collective_id=1, has_side_effects=True, vmem_limit_bytes=63 << 20),
         cost_estimate=CHEAP,
-        name="attention_backward",
-    )(lengths, tokens, out_grad, weights, vector, router, routes, places, *kept, outs, returned)
+        name="finish",
+    )(lengths, *rows_in, *kept, outs, backs, *grads)
 
 
 def pack_expert(up, down, up_bias, down_bias, dtype):
@@ -746,41 +940,32 @@
         part_grads.append((grad_up, grad_down))
     out_b, grad_b = sums
 
-    back = exchange(out_b.reshape(experts, blocks, capacity, D))
-    returned = exchange(grad_b.reshape(experts, blocks, capacity, D))
-
-    def add(a, b):
-        return (a.astype(f32) + b.astype(f32)).astype(b16)
-
-    both_halves = range(2)
-    nearest, middle, far = ([part_grads[k][i] for i in both_halves] for k in (1, 2, 3))
-    near = [along(nearest[i], (0, 1), (3, 2)) for i in both_halves]
-    mid = [along(after(middle[i], near[i]), (0, 1), (3, 2)) for i in both_halves]
-    end = [along(after(far[i], mid[i]), (0, 1), (3, 2)) for i in both_halves]
-    mid = [along(add(middle[i], mid[i]), (1, 2), (2, 1)) for i in both_halves]
-    end = [along(add(far[i], end[i]), (1, 2), (2, 1)) for i in both_halves]
-    end = [along(add(nearest[i], end[i]), (1, 0), (2, 3)) for i in both_halves]
+    small_rows = -(-(8 + experts) // 16) * 16
+    slots_shape = (experts, blocks, capacity, D)
+    output, input_grad, dense, *came = finish(
+        n_dp, side, cols, small_rows, lengths,
+        (tokens, out_grad, weights_b, vector_all, router_all, routes, positions.reshape(count, 2)),
+        kept, out_b.reshape(slots_shape), grad_b.reshape(slots_shape), [g for i in (1, 2, 3) for g in part_grads[i]],
+    )
     totals = [
-        part_grads[0][i] + (near[i].astype(f32) + mid[i].astype(f32) + end[i].astype(f32)) for i in both_halves
+        part_grads[0][i]
+        + jnp.where(inner, came[i].astype(f32) + came[2 + i].astype(f32), came[4 + i].astype(f32))
+        for i in range(2)
     ]
     shard_up = totals[0][None]
     shard_down = totals[1][:part][None]
     shard_up_bias = totals[1][part, :part][None]
     shard_down_bias = totals[1][part + 1, :narrow][None]
-
-    output, input_grad, grad_weights, grad_vector, grad_router = attention_backward(
-        lengths, tokens, out_grad, weights_b, vector_all, router_all, routes, positions.reshape(count, 2), kept, back, returned
+    if cols % 8:
+        small = lax.psum(dense[:small_rows], both)
+        big = dense[small_rows:].reshape(4, D, D).astype(b16)
+        big = lax.psum_scatter(big, both, scatter_dimension=1, tiled=True).astype(f32)
+        dense = jnp.concatenate([big.reshape(4 * cols, D), small], axis=0)
+    shard_weights = dense[: 4 * cols].reshape(4, cols, D)
+    small = lax.dynamic_slice(
+        dense[4 * cols :], (0, (me * experts + mine) * cols), (small_rows, cols)
     )
-
-    small = jnp.concatenate([grad_vector[:7], grad_router[:experts]], axis=0).reshape(7 + experts, devices, cols)
-    small = jnp.pad(small.transpose(1, 0, 2).reshape(devices, flat_len), ((0, 0), (0, extra * D - flat_len)))
-    big = grad_weights.reshape(4, devices, cols, D).transpose(1, 0, 2, 3).reshape(devices, 4 * cols, D)
-    packed = jnp.concatenate([big, small.reshape(devices, extra, D).astype(b16)], axis=1)
-    packed = packed.reshape(n_dp, side, side, 2, 4 * cols + extra, D).transpose(3, 1, 2, 0, 4, 5)
-    packed = scatter_dense(packed, n_dp, side)
-    shard_weights = packed[: 4 * cols].reshape(4, cols, D)
-    small = packed[4 * cols :].reshape(extra * D)[:flat_len].reshape(7 + experts, cols)
-    shard_vector, shard_router = small[:7], small[7:]
+    shard_vector, shard_router = small[:7], small[8 : 8 + experts]
 
     params = (attention, gain_bias, router, expert_up, up_bias, expert_down, down_bias)
     grads = (shard_weights, shard_vector, shard_router, shard_up, shard_up_bias, shard_down, shard_down_bias)

time: 575 us -> 489 us (0.85)
  waiting for transfers between devices: 159 us -> 67 us
  Pallas kernels: 241 us -> 319 us
  starting transfers between devices: 67.8 us -> 20.4 us
  other arithmetic: 45 us -> 30 us
  local copies, waits for them, and re-layouts: 44.6 us -> 37.4 us
    ppermute x17 -> x5, waiting for transfers between devices: 118 us -> 25.5 us  [along(): return lax.ppermute(x, 'dp', pairs)]
    pallas_call x2 -> x1, Pallas kernels: 97.2 us -> 175 us  [finish(): pl.pallas_call(functools.partial(finish_kernel, n, cols, extra, count //...]
    ppermute x17 -> x5, starting transfers between devices: 46.2 us -> 7.78 us  [along(): return lax.ppermute(x, 'dp', pairs)]
    all_to_all x3 -> x1, starting transfers between devices: 12.8 us -> 3.78 us  [exchange(): lax.all_to_all(sent, 'expert', split_axis=0, concat_axis=0, tiled=True)]
    convert_element_type x6 -> x0, other arithmetic: 8.97 us -> none  [add(): return (a.astype(f32) + b.astype(f32)).astype(b16)]
    unnamed x89 -> x92, local copies, waits for them, and re-layouts: 16 us -> 16.8 us
    all_to_all x3 -> x1, waiting for transfers between devices: 27.2 us -> 26.6 us  [exchange(): lax.all_to_all(sent, 'expert', split_axis=0, concat_axis=0, tiled=True)]
  transfers between devices with their start and end apart: 22 -> 8, of which waited for: 8 -> 4; matrix products, arithmetic and copies ran while one was open for 11% -> 6% of each run, Pallas kernels for 43% -> 25%
where the time goes in v3:
time: 489 us; the launch traced here: 480 us
  Pallas kernels  319 us (65%)
  waiting for transfers between devices  67 us (14%)
  local copies, waits for them, and re-layouts  37.4 us (8%)
  other arithmetic  30 us (6%)
  starting transfers between devices  20.4 us (4%)
    pallas_call x1, Pallas kernels, finish(): pl.pallas_call(functools.partial(finish_kernel, n, cols, extra, count //...  175 us
    pallas_call x4, Pallas kernels, expert_part(): pl.pallas_call(functools.partial(expert_kernel, n, first, last, part), gr...  96.1 us
    pallas_call x1, Pallas kernels, gather_dense(): pl.pallas_call(functools.partial(gather_kernel, n), out_shape=jax.ShapeDt...  35 us
    all_to_all x1, waiting for transfers between devices, exchange(): lax.all_to_all(sent, 'expert', split_axis=0, concat_axis=0, tiled=True)  26.6 us
    ppermute x5, waiting for transfers between devices, along(): return lax.ppermute(x, 'dp', pairs)  25.5 us
    unnamed x92, local copies, waits for them, and re-layouts  16.8 us
    all_to_all x1, waiting for transfers between devices, body(): lax.all_to_all(sent, 'expert', split_axis=0, concat_axis=0, tiled=True)  14.9 us
    pallas_call x1, Pallas kernels, attention_forward(): pl.pallas_call(attention_kernel, grid=(count // LEN,), in_specs=[pl.Block...  13 us
  transfers between devices with their start and end apart: 8, of which 4 were waited for; matrix products, arithmetic and copies ran while one was open for 6% of the time, Pallas kernels for 25%

profile of v3, /device:TPU:0, one launch (start us, length us, event | category | flops | bytes accessed | tf_op | source)
XLA Modules:
  0.0 480.1 jit_solution(4155309620161015135)
XLA Ops:
  0.7 0.9 copy.100.routes_ref
  2.5 1.4 rev.4
  6.1 5.2 %all-to-all-start.2 = ((f32[8,2,128]{2,1,0:T(2,128)}), f32[8,2,128]{2,1,0:T(2,128)S(1)}, u32[]{:S(2)}, u32[]{:S(2)}) async-start(f32[8,2,128]{2,1,0:T(2,128)} %convert_bitcast_fusion.3), calls=%async_computation.2 | async-start | bytes 16384 | tf_op jit(solution)/shard_map/all_to_all | solution.py:885
  11.5 35.0 %gather_dense.1 = bf16[32,112,768]{2,1,0:T(8,128)(2,1)S(1)} custom-call(bf16[112,768]{1,0:T(8,128)(2,1)S(1)} %pad_maximum_fusion.1.in_ref), custom_call_target="tpu_custom_call" | custom-call | bytes 1024 | tf_op jit(solution)/shard_map/gather_dense/pallas_call | solution.py:152
  46.6 2.4 copy-done
  49.7 4.9 %slice.91 = bf16[32,96,768]{2,1,0:T(8,128)(2,1)} slice(bf16[32,112,768]{2,1,0:T(8,128)(2,1)} %copy-done), slice={[0:32], [0:96], [0:768]} | slice | bytes 9437184 | tf_op jit(solution)/shard_map/slice | solution.py:872
  54.8 5.0 %copy.88 = bf16[32,4,24,768]{3,2,0,1:T(8,128)(2,1)} copy(bf16[32,4,24,768]{3,2,1,0:T(8,128)(2,1)} %bitcast.81) | data formatting | bytes 9437184 | tf_op jit(solution)/shard_map/reshape | solution.py:872
  59.8 13.0 %attention_forward.1 = (bf16[512,768]{1,0:T(8,128)(2,1)S(1)}, bf16[512,768]{1,0:T(8,128)(2,1)S(1)}, bf16[512,768]{1,0:T(8,128)(2,1)S(1)}, bf16[512,768]{1,0:T(8,...) custom-call(s32[2]{0:T(128)S(1)} %copy-done.12, ...), custom_call_target="tpu_custom_call" | custom-call | bytes 1024 | tf_op jit(solution)/shard_map/attention_forward/pallas_call | solution.py:459
  72.8 0.9 copy-done.3
  73.7 0.9 copy-done.4
  74.6 0.9 copy-done.5
  75.4 0.9 copy-done.6
  76.3 0.9 copy-done.7
  77.2 0.9 copy-done.8
  79.5 3.8 all-to-all-start.1
  83.6 2.6 convert_bitcast_fusion.1
  86.3 1.5 pad_maximum_fusion.refs_0_
  88.4 2.1 collective-permute-start.3
  91.6 1.0 convert_bitcast_fusion
  92.6 2.0 copy.97
  94.6 26.6 %all-to-all-done.1 = bf16[8,2,128,768]{3,2,1,0:T(8,128)(2,1)S(1)} async-done(((bf16[8,2,128,768]{3,2,1,0:T(8,128)(2,1)}), bf16[8,2,128,768]{3,2,1,0:T(8,128)(2,1)S(1)}, u32[]{:S(2)}, u32[]{:S(2)}) %all-to-all-start.1) | async-done | bytes 3145760 | tf_op jit(solution)/shard_map/all_to_all | solution.py:900
  121.1 1.6 copy-done.13
  122.7 3.6 all-to-all-start
  127.2 15.0 %collective-permute-done.refs_0_ = bf16[1552,768]{1,0:T(8,128)(2,1)} collective-permute-done((bf16[1552,768]{1,0:T(8,128)(2,1)}, bf16[1552,768]{1,0:T(8,128)(2,1)}, u32[]{:S(2)}, u32[]{:S(2)}) %collective-permute-start) | collective-permute-done | bytes 2383904 | tf_op jit(solution)/shard_map/ppermute | solution.py:834
  142.2 2.0 collective-permute-start.1
  144.9 1.5 collective-permute-start.4
  146.4 2.8 fusion.5
  149.3 14.9 %all-to-all-done = bf16[8,2,128,768]{3,2,1,0:T(8,128)(2,1)S(1)} async-done(((bf16[8,2,128,768]{3,2,1,0:T(8,128)(2,1)}), bf16[8,2,128,768]{3,2,1,0:T(8,128)(2,1)S(1)}, u32[]{:S(2)}, u32[]{:S(2)}) %all-to-all-start) | async-done | bytes 3145760 | tf_op jit(solution)/shard_map/all_to_all | solution.py:890
  166.9 2.2 multiply_convert_fusion.1.refs_2_.refs_3_
  169.1 23.6 %expert_part_0.1 = (f32[2048,768]{1,0:T(8,128)}, f32[2048,768]{1,0:T(8,128)}, f32[768,768]{1,0:T(8,128)}, f32[784,768]{1,0:T(8,128)}) custom-call(bf16[1552,768]{1,0:T(8,128)(2,1)} %pad_maximum_fusion.refs_0_, bf16[2048,768]{1,0:T(8,128)(2,1)} %bitcast.77, bf16[2048,768]{1,0:T(8,128)(2,1)} %multiply_convert_fusion.1.refs_2_.refs_3_, ...), custom_call_target="tpu_custom_call" | custom-call | flops 14495514624 | bytes 31457280 | tf_op jit(solution)/shard_map/expert_part_0/pallas_call | solution.py:342
  192.7 1.5 collective-permute-start.2
  194.3 24.4 %expert_part_1.1 = (f32[2048,768]{1,0:T(8,128)}, f32[2048,768]{1,0:T(8,128)}, bf16[768,768]{1,0:T(8,128)(2,1)}, bf16[784,768]{1,0:T(8,128)(2,1)}) custom-call(bf16[1552,768]{1,0:T(8,128)(2,1)} %collective-permute-done.refs_0_, bf16[2048,768]{1,0:T(8,128)(2,1)} %bitcast.78, bf16[2048,768]{1,0:T(8,128)(2,1)} %multiply_convert_fusion.1.refs_2_.refs_3_, ...), custom_call_target="tpu_custom_call" | custom-call | flops 14495514624 | bytes 31457280 | tf_op jit(solution)/shard_map/expert_part_1/pallas_call | solution.py:342
  219.4 24.4 %expert_part_2.1 = (f32[2048,768]{1,0:T(8,128)}, f32[2048,768]{1,0:T(8,128)}, bf16[768,768]{1,0:T(8,128)(2,1)}, bf16[784,768]{1,0:T(8,128)(2,1)}) custom-call(bf16[1552,768]{1,0:T(8,128)(2,1)} %collective-permute-done.3.refs_0_, bf16[1552,768]{1,0:T(8,128)(2,1)} %collective-permute-done.4.refs_1_, bf16[2048,768]{1,0:T(8,128)(2,1)} %bitcast.79, ...), custom_call_target="tpu_custom_call" | custom-call | flops 14495514624 | bytes 31457280 | tf_op jit(solution)/shard_map/expert_part_2/pallas_call | solution.py:342
  243.7 10.5 %collective-permute-done.2.refs_1_ = bf16[1552,768]{1,0:T(8,128)(2,1)S(1)} collective-permute-done((bf16[1552,768]{1,0:T(8,128)(2,1)}, bf16[1552,768]{1,0:T(8,128)(2,1)S(1)}, u32[]{:S(2)}, u32[]{:S(2)}) %collective-permute-start.2) | collective-permute-done | bytes 2383904 | tf_op jit(solution)/shard_map/ppermute | solution.py:834
  254.9 1.1 scatter_custom_fusion
  256.7 23.8 %expert_part_3.1 = (bf16[2048,768]{1,0:T(8,128)(2,1)}, bf16[2048,768]{1,0:T(8,128)(2,1)}, bf16[768,768]{1,0:T(8,128)(2,1)}, bf16[784,768]{1,0:T(8,128)(2,1)}) custom-call(bf16[1552,768]{1,0:T(8,128)(2,1)} %collective-permute-done.1.refs_0_, bf16[1552,768]{1,0:T(8,128)(2,1)} %copy-done.43, bf16[2048,768]{1,0:T(8,128)(2,1)} %bitcast.80, ...), custom_call_target="tpu_custom_call" | custom-call | flops 14495514624 | bytes 31457280 | tf_op jit(solution)/shard_map/expert_part_3/pallas_call | solution.py:342
  280.5 175.2 %finish.1 = (f32[512,768]{1,0:T(8,128)}, f32[512,768]{1,0:T(8,128)}, f32[112,768]{1,0:T(8,128)}, bf16[768,768]{1,0:T(8,128)(2,1)}, bf16[784,768]{1,0:T(8,128)(2,...) custom-call(s32[2]{0:T(128)} %lengths_ref.3, ...), custom_call_target="tpu_custom_call" | custom-call | bytes 1024 | tf_op jit(solution)/shard_map/finish/pallas_call | solution.py:777
  455.7 1.0 slice.103
  456.7 0.9 slice.104
  457.5 3.3 select_add_fusion
  460.9 1.6 slice_bitcast_fusion
  462.5 1.0 copy-done.15
  464.3 4.4 multiply_add_fusion
  469.9 1.1 multiply_add_fusion.2
  472.4 4.1 multiply_add_fusion.1
  476.5 1.1 copy.108
  477.7 0.8 copy-done.22
  478.5 1.1 copy.109
  (147 shorter events, 17.0 us)
Async XLA Ops:
  0.7 10.6 %copy-start.27 = (f32[4,24,768]{2,1,0:T(8,128)S(1)}, f32[4,24,768]{2,1,0:T(8,128)}, u32[]{:S(2)}) copy-start(f32[4,24,768]{2,1,0:T(8,128)} %param.33) | copy-start | bytes 884740
  0.7 10.6 %copy-start.32 = (f32[7,24]{1,0:T(8,128)S(1)}, f32[7,24]{1,0:T(8,128)}, u32[]{:S(2)}) copy-start(f32[7,24]{1,0:T(8,128)} %param.34) | copy-start | bytes 2020
  0.7 10.6 %copy-start.31 = (f32[8,24]{1,0:T(8,128)S(1)}, f32[8,24]{1,0:T(8,128)}, u32[]{:S(2)}) copy-start(f32[8,24]{1,0:T(8,128)} %param.35) | copy-start | bytes 2308
  1.6 58.2 %copy-start.1 = (s32[512,2]{1,0:T(8,128)}, s32[512,2]{1,0:T(8,128)S(1)}, u32[]{:S(2)}) copy-start(s32[512,2]{1,0:T(8,128)S(1)} %copy.100.routes_ref) | copy-start | bytes 12292
  6.1 73.4 %all-to-all-start.2 = ((f32[8,2,128]{2,1,0:T(2,128)}), f32[8,2,128]{2,1,0:T(2,128)S(1)}, u32[]{:S(2)}, u32[]{:S(2)}) async-start(f32[8,2,128]{2,1,0:T(2,128)} %convert_bitcast_fusion.3), calls=%async_computation.2 | async-start | bytes 16384 | tf_op jit(solution)/shard_map/all_to_all | solution.py:885
  46.5 2.4 copy-start
  49.7 10.1 %copy-start.11 = (f32[8,768]{1,0:T(8,128)}, f32[8,768]{1,0:T(8,128)S(1)}, u32[]{:S(2)}) copy-start(f32[8,768]{1,0:T(8,128)S(1)} %pad_convert_fusion.vector_ref) | copy-start | bytes 73732
  54.8 5.0 %copy-start.2 = (bf16[128,768]{1,0:T(8,128)(2,1)}, bf16[128,768]{1,0:T(8,128)(2,1)S(1)}, u32[]{:S(2)}) copy-start(bf16[128,768]{1,0:T(8,128)(2,1)S(1)} %pad.36.router_ref) | copy-start | bytes 589828
  54.8 5.0 %copy-start.12 = (s32[2]{0:T(128)S(1)}, s32[2]{0:T(128)}, u32[]{:S(2)}) copy-start(s32[2]{0:T(128)} %lengths_ref.3) | copy-start | bytes 28
  72.8 0.9 copy-start.3
  75.4 0.9 copy-start.6
  76.3 0.9 copy-start.7
  77.2 0.9 copy-start.8
  79.5 3.8 copy-start.33
  79.5 3.8 copy-start.36
  79.5 41.6 %all-to-all-start.1 = ((bf16[8,2,128,768]{3,2,1,0:T(8,128)(2,1)}), bf16[8,2,128,768]{3,2,1,0:T(8,128)(2,1)S(1)}, u32[]{:S(2)}, u32[]{:S(2)}) async-start(bf16[8,2,128,768]{3,2,1,0:T(8,128)(2,1)} %get-tuple-element.104), calls=%async_computation.1 | async-start | bytes 6291456 | tf_op jit(solution)/shard_map/all_to_all | solution.py:900
  86.2 5.4 %copy-start.16 = (bf16[512,768]{1,0:T(8,128)(2,1)S(1)}, bf16[512,768]{1,0:T(8,128)(2,1)}, u32[]{:S(2)}) copy-start(bf16[512,768]{1,0:T(8,128)(2,1)} %grad_ref.1) | copy-start | bytes 2359300
  87.8 54.4 %collective-permute-start = (bf16[1552,768]{1,0:T(8,128)(2,1)}, bf16[1552,768]{1,0:T(8,128)(2,1)}, u32[]{:S(2)}, u32[]{:S(2)}) collective-permute-start(bf16[1552,768]{1,0:T(8,128)(2,1)} %pad_maximum_fusion.refs_0_), channel_id=1, source_target_pairs={{0,8},{8,0},{16,24},{24,16},{1,9},{9,1},{17,25},{25,17},{2,10},{10... | collective-permute-start | bytes 7151624 | tf_op jit(solution)/shard_map/ppermute | solution.py:834
  88.4 56.5 %collective-permute-start.3 = (bf16[1552,768]{1,0:T(8,128)(2,1)}, bf16[1552,768]{1,0:T(8,128)(2,1)}, u32[]{:S(2)}, u32[]{:S(2)}) collective-permute-start(bf16[1552,768]{1,0:T(8,128)(2,1)} %pad_maximum_fusion.refs_0_), channel_id=1, source_target_pairs={{8,16},{16,8},{9,17},{17,9},{10,18},{18,10},{11,19},{19,11},{12,20... | collective-permute-start | bytes 7151624 | tf_op jit(solution)/shard_map/ppermute | solution.py:834
  121.1 1.6 copy-start.13
  122.7 41.5 %all-to-all-start = ((bf16[8,2,128,768]{3,2,1,0:T(8,128)(2,1)}), bf16[8,2,128,768]{3,2,1,0:T(8,128)(2,1)S(1)}, u32[]{:S(2)}, u32[]{:S(2)}) async-start(bf16[8,2,128,768]{3,2,1,0:T(8,128)(2,1)} %copy.97), calls=%async_computation | async-start | bytes 6291456 | tf_op jit(solution)/shard_map/all_to_all | solution.py:890
  142.2 50.5 %collective-permute-start.1 = (bf16[1552,768]{1,0:T(8,128)(2,1)}, bf16[1552,768]{1,0:T(8,128)(2,1)}, u32[]{:S(2)}, u32[]{:S(2)}) collective-permute-start(bf16[1552,768]{1,0:T(8,128)(2,1)} %collective-permute-done.refs_0_), channel_id=1, source_target_pairs={{8,16},{16,8},{9,17},{17,9},{10,18},{18,10},{11,19},{19,11},{12,20... | collective-permute-start | bytes 7151624 | tf_op jit(solution)/shard_map/ppermute | solution.py:834
  144.9 73.7 %collective-permute-start.4 = (bf16[1552,768]{1,0:T(8,128)(2,1)}, bf16[1552,768]{1,0:T(8,128)(2,1)}, u32[]{:S(2)}, u32[]{:S(2)}) collective-permute-start(bf16[1552,768]{1,0:T(8,128)(2,1)} %collective-permute-done.3.refs_0_), channel_id=1, source_target_pairs={{8,0},{16,24},{9,1},{17,25},{10,2},{18,26},{11,3},{19,27},{12,4},{... | collective-permute-start | bytes 7151624 | tf_op jit(solution)/shard_map/ppermute | solution.py:834
  192.7 61.5 %collective-permute-start.2 = (bf16[1552,768]{1,0:T(8,128)(2,1)}, bf16[1552,768]{1,0:T(8,128)(2,1)S(1)}, u32[]{:S(2)}, u32[]{:S(2)}) collective-permute-start(bf16[1552,768]{1,0:T(8,128)(2,1)} %collective-permute-done.1.refs_0_), channel_id=1, source_target_pairs={{8,0},{16,24},{9,1},{17,25},{10,2},{18,26},{11,3},{19,27},{12,4},{... | collective-permute-start | bytes 7151624 | tf_op jit(solution)/shard_map/ppermute | solution.py:834
  254.2 2.4 copy-start.43
  456.7 13.2 %copy-start.28 = (f32[96,768]{1,0:T(8,128)}, f32[96,768]{1,0:T(8,128)S(1)}, u32[]{:S(2)}) copy-start(f32[96,768]{1,0:T(8,128)S(1)} %slice.103) | copy-start | bytes 884740
  457.5 4.9 %copy-start.21 = (f32[1,768,768]{2,1,0:T(8,128)S(1)}, f32[1,768,768]{2,1,0:T(8,128)}, u32[]{:S(2)}) copy-start(f32[1,768,768]{2,1,0:T(8,128)} %param.52) | copy-start | bytes 7077892
  460.9 2.5 copy-start.15
  460.9 3.2 copy-start.20
  464.1 4.5 copy-start.39
  464.1 4.5 copy-start.40
  464.2 5.1 %copy-start.41 = (f32[1,192]{1,0:T(1,128)S(1)}, f32[1,192]{1,0:T(1,128)}, u32[]{:S(2)}) copy-start(f32[1,192]{1,0:T(1,128)} %param.46) | copy-start | bytes 2308
  464.2 5.1 %copy-start.42 = (f32[1,192]{1,0:T(1,128)S(1)}, f32[1,192]{1,0:T(1,128)}, u32[]{:S(2)}) copy-start(f32[1,192]{1,0:T(1,128)} %param.53) | copy-start | bytes 2308
  464.2 5.7 %copy-start.29 = (f32[4,24,768]{2,1,0:T(8,128)S(1)}, f32[4,24,768]{2,1,0:T(8,128)}, u32[]{:S(2)}) copy-start(f32[4,24,768]{2,1,0:T(8,128)} %param.40) | copy-start | bytes 884740
  464.2 5.7 %copy-start.30 = (f32[4,24,768]{2,1,0:T(8,128)S(1)}, f32[4,24,768]{2,1,0:T(8,128)}, u32[]{:S(2)}) copy-start(f32[4,24,768]{2,1,0:T(8,128)} %param.47) | copy-start | bytes 884740
  464.2 6.8 %copy-start.37 = (f32[7,24]{1,0:T(8,128)S(1)}, f32[7,24]{1,0:T(8,128)}, u32[]{:S(2)}) copy-start(f32[7,24]{1,0:T(8,128)} %param.41) | copy-start | bytes 2020
  464.2 6.8 %copy-start.38 = (f32[7,24]{1,0:T(8,128)S(1)}, f32[7,24]{1,0:T(8,128)}, u32[]{:S(2)}) copy-start(f32[7,24]{1,0:T(8,128)} %param.48) | copy-start | bytes 2020
  464.2 7.4 %copy-start.34 = (f32[8,24]{1,0:T(8,128)S(1)}, f32[8,24]{1,0:T(8,128)}, u32[]{:S(2)}) copy-start(f32[8,24]{1,0:T(8,128)} %param.42) | copy-start | bytes 2308
  464.2 7.4 %copy-start.35 = (f32[8,24]{1,0:T(8,128)S(1)}, f32[8,24]{1,0:T(8,128)}, u32[]{:S(2)}) copy-start(f32[8,24]{1,0:T(8,128)} %param.49) | copy-start | bytes 2308
  464.2 8.1 %copy-start.14 = (f32[1,768,768]{2,1,0:T(8,128)S(1)}, f32[1,768,768]{2,1,0:T(8,128)}, u32[]{:S(2)}) copy-start(f32[1,768,768]{2,1,0:T(8,128)} %param.36) | copy-start | bytes 7077892
  464.2 8.1 %copy-start.17 = (f32[1,768,768]{2,1,0:T(8,128)S(1)}, f32[1,768,768]{2,1,0:T(8,128)}, u32[]{:S(2)}) copy-start(f32[1,768,768]{2,1,0:T(8,128)} %param.43) | copy-start | bytes 7077892
  464.3 8.1 %copy-start.18 = (f32[1,768,768]{2,1,0:T(8,128)S(1)}, f32[1,768,768]{2,1,0:T(8,128)}, u32[]{:S(2)}) copy-start(f32[1,768,768]{2,1,0:T(8,128)} %param.50) | copy-start | bytes 7077892
  464.3 8.1 %copy-start.19 = (f32[768,768]{1,0:T(8,128)S(1)}, f32[768,768]{1,0:T(8,128)}, u32[]{:S(2)}) copy-start(f32[768,768]{1,0:T(8,128)} %get-tuple-element.122) | copy-start | bytes 7077892
  464.3 8.1 %copy-start.25 = (bf16[768,768]{1,0:T(8,128)(2,1)S(1)}, bf16[768,768]{1,0:T(8,128)(2,1)}, u32[]{:S(2)}) copy-start(bf16[768,768]{1,0:T(8,128)(2,1)} %get-tuple-element.124) | copy-start | bytes 3538948
  464.3 8.1 %copy-start.26 = (bf16[768,768]{1,0:T(8,128)(2,1)S(1)}, bf16[768,768]{1,0:T(8,128)(2,1)}, u32[]{:S(2)}) copy-start(bf16[768,768]{1,0:T(8,128)(2,1)} %get-tuple-element.125) | copy-start | bytes 3538948
  468.7 3.7 copy-start.24
  472.4 4.1 copy-start.23
  476.5 2.0 copy-start.22
  (4 other events, 3.2 us)

commit v4 on v3

--- a/solution.py
+++ b/solution.py
@@ -72,46 +72,42 @@
     return along_z, first, second, at(z, y, x, 1 - core)
 
 
-def gather_kernel(n, in_ref, out_ref, local_sem, z_s, z_r, a_s, a_r, b_s, b_r, c_s, c_r):
+def remote(src, dst, send, recv, peer):
+    return pltpu.make_async_remote_copy(
+        src_ref=src, dst_ref=dst, send_sem=send, recv_sem=recv, device_id=peer, device_id_type=MESH
+    )
+
+
+def spread_blocks(n, in_ref, block_at, sems, meanwhile, at_last):
+    z_s, z_r, a_s, a_r, b_s, b_r, c_s, c_r = sems
     side, z, y, x, core = where_am_i()
     along_z, first, second, sibling = peers_of(n, side, z, y, x, core)
-    greet([*along_z, *first, *second, sibling])
+    sent = []
 
     def block(j, ka, kb, core_):
         y_ = (y - core * ka - (1 - core) * kb + 2 * side) % side
         x_ = (x - (1 - core) * ka - core * kb + 2 * side) % side
-        return out_ref.at[((((z - j + n) % n) * side + y_) * side + x_) * 2 + core_]
-
-    def remote(src, dst, send, recv, peer):
-        return pltpu.make_async_remote_copy(
-            src_ref=src, dst_ref=dst, send_sem=send, recv_sem=recv, device_id=peer, device_id_type=MESH
-        )
-
-    own = pltpu.make_async_copy(in_ref, block(0, 0, 0, core), local_sem)
-    own.start()
-    sent = []
+        return block_at(((((z - j + n) % n) * side + y_) * side + x_) * 2 + core_)
+
+    def send(src, dst, send_sem, recv_sem, peer):
+        copy = remote(src, dst, send_sem, recv_sem, peer)
+        copy.start()
+        sent.append(copy)
 
     def pass_on(src, dst, j, ka, kb):
         if kb == 0:
             if ka == 0:
                 for k in range(1, side):
-                    copy = remote(src, dst, a_s.at[j * side + k], a_r.at[j * side + k], first[k - 1])
-                    copy.start()
-                    sent.append(copy)
+                    send(src, dst, a_s.at[j * side + k], a_r.at[j * side + k], first[k - 1])
             for k in range(1, side):
                 place = (j * side + ka) * side + k
-                copy = remote(src, dst, b_s.at[place], b_r.at[place], second[k - 1])
-                copy.start()
-                sent.append(copy)
+                send(src, dst, b_s.at[place], b_r.at[place], second[k - 1])
         place = (j * side + kb) * side + ka
-        copy = remote(src, dst, c_s.at[place], c_r.at[place], sibling)
-        copy.start()
-        sent.append(copy)
+        send(src, dst, c_s.at[place], c_r.at[place], sibling)
 
     for k in range(1, n):
-        copy = remote(in_ref, block(0, 0, 0, core), z_s.at[k], z_r.at[k], along_z[k - 1])
-        copy.start()
-        sent.append(copy)
+        send(in_ref, block(0, 0, 0, core), z_s.at[k], z_r.at[k], along_z[k - 1])
+    meanwhile()
     pass_on(in_ref, block(0, 0, 0, core), 0, 0, 0)
     for j in range(1, n):
         here = block(j, 0, 0, core)
@@ -129,126 +125,103 @@
                 place = (j * side + ka) * side + kb
                 remote(here, here, b_s.at[place], b_r.at[place], sibling).wait_recv()
                 pass_on(here, here, j, ka, kb)
+    at_last()
     for j in range(n):
         for ka in range(side):
             for kb in range(side):
                 here = block(j, ka, kb, 1 - core)
                 place = (j * side + ka) * side + kb
                 remote(here, here, c_s.at[place], c_r.at[place], sibling).wait_recv()
-    for copy in sent:
+    return sent
+
+
+def spread_sems(n, side):
+    dma = pltpu.SemaphoreType.DMA
+    return [*[dma((n,))] * 2, *[dma((n * side,))] * 2, *[dma((n * side * side,))] * 4]
+
+
+def exchange_all(pairs, sent):
+    z, mine = lax.axis_index("dp"), lax.axis_index("expert")
+    experts = lax.axis_size("expert")
+    for k in range(1, experts):
+        to = (mine + k) % experts
+        for src, dst, send, recv in pairs:
+            copy = remote(src(to), dst(mine), send.at[k], recv.at[k], (z, to))
+            copy.start()
+            sent.append(copy)
+
+
+def wait_all(pairs):
+    z, mine = lax.axis_index("dp"), lax.axis_index("expert")
+    experts = lax.axis_size("expert")
+    for k in range(1, experts):
+        came = (mine - k + experts) % experts
+        for _, dst, send, recv in pairs:
+            remote(dst(came), dst(came), send.at[k], recv.at[k], (z, came)).wait_recv()
+
+
+def gather_kernel(
+    n, in_ref, own_ref, slots_ref, marks_ref, out_ref, second_ref, third_ref, slots_in, marks_in,
+    local_sem, part_s, part_r, slot_s, slot_r, mark_s, mark_r, *sems,
+):
+    side, z, y, x, core = where_am_i()
+    mine = lax.axis_index("expert")
+    experts = slots_ref.shape[0]
+    greet([*peers_of(n, side, z, y, x, core)[0], *[(z, (mine + k) % experts) for k in range(1, experts)]])
+    me = ((z * side + y) * side + x) * 2 + core
+    stays = [
+        pltpu.make_async_copy(in_ref, out_ref.at[me], local_sem.at[0]),
+        pltpu.make_async_copy(slots_ref.at[mine], slots_in.at[mine], local_sem.at[1]),
+        pltpu.make_async_copy(marks_ref.at[mine], marks_in.at[mine], local_sem.at[2]),
+    ]
+    for copy in stays:
+        copy.start()
+    beside = remote(own_ref, second_ref, part_s.at[0], part_r.at[0], (z + 1 - 2 * (z % 2), mine))
+    across = remote(own_ref, third_ref, part_s.at[1], part_r.at[1], ((n - 1 - z) % n, mine))
+    inner = (z + 1) // 2 % 2 == 1
+    pairs = [
+        (lambda e: slots_ref.at[e], lambda e: slots_in.at[e], slot_s, slot_r),
+        (lambda e: marks_ref.at[e], lambda e: marks_in.at[e], mark_s, mark_r),
+    ]
+    more = []
+
+    def weights_on():
+        beside.start()
+
+        @pl.when(inner)
+        def _():
+            across.start()
+
+    sent = spread_blocks(n, in_ref, lambda d: out_ref.at[d], sems, weights_on, lambda: exchange_all(pairs, more))
+    wait_all(pairs)
+    for copy in [*sent, *more]:
         copy.wait_send()
-    own.wait()
-
-
-def gather_dense(packed, n, side):
+    for copy in stays:
+        copy.wait()
+    beside.wait()
+
+    @pl.when(inner)
+    def _():
+        across.wait()
+
+
+def gather_dense(packed, own, slots, marks, n, side):
     devices = n * side * side * 2
-    sems = [
-        pltpu.SemaphoreType.DMA,
-        *[pltpu.SemaphoreType.DMA((n,))] * 2,
-        *[pltpu.SemaphoreType.DMA((n * side,))] * 2,
-        *[pltpu.SemaphoreType.DMA((n * side * side,))] * 4,
-    ]
-    size = devices * packed.size * 2
+    experts = slots.shape[0]
+    dma = pltpu.SemaphoreType.DMA
+    sems = [dma((3,)), *[dma((2,))] * 2, *[dma((experts,))] * 4, *spread_sems(n, side)]
+    vmem, hbm = pl.BlockSpec(memory_space=pltpu.VMEM), pl.BlockSpec(memory_space=pl.ANY)
+    gathered = jax.ShapeDtypeStruct((devices, *packed.shape), packed.dtype)
     return pl.pallas_call(
         functools.partial(gather_kernel, n),
-        out_shape=jax.ShapeDtypeStruct((devices, *packed.shape), packed.dtype),
-        in_specs=[pl.BlockSpec(memory_space=pltpu.VMEM)],
-        out_specs=pl.BlockSpec(memory_space=pltpu.VMEM),
+        out_shape=[gathered, *[jax.ShapeDtypeStruct(v.shape, v.dtype) for v in (own, own, slots, marks)]],
+        in_specs=[vmem, hbm, hbm, hbm],
+        out_specs=[vmem, *[hbm] * 4],
         scratch_shapes=sems,
-        compiler_params=pltpu.CompilerParams(
-            collective_id=0, has_side_effects=True, vmem_limit_bytes=size + (4 << 20)
-        ),
+        compiler_params=pltpu.CompilerParams(collective_id=0, has_side_effects=True, vmem_limit_bytes=60 << 20),
         cost_estimate=CHEAP,
         name="gather_dense",
-    )(packed)
-
-
-def scatter_kernel(n, in_ref, out_ref, stage, c_buf, b_buf, a_buf, z_buf, c_s, c_r, b_s, b_r, a_s, a_r, z_s, z_r):
-    side, z, y, x, core = where_am_i()
-    along_z, first, second, sibling = peers_of(n, side, z, y, x, core)
-    greet([*along_z, *first, *second, sibling])
-
-    def piece(ka, kb, core_):
-        y_ = (y + core * ka + (1 - core) * kb) % side
-        x_ = (x + (1 - core) * ka + core * kb) % side
-        return (core_ * side + y_) * side + x_
-
-    def remote(src, dst, send, recv, peer):
-        return pltpu.make_async_remote_copy(
-            src_ref=src, dst_ref=dst, send_sem=send, recv_sem=recv, device_id=peer, device_id_type=MESH
-        )
-
-    sent = []
-
-    def send(src, dst, send_sem, recv_sem, peer):
-        copy = remote(src, dst, send_sem, recv_sem, peer)
-        copy.start()
-        sent.append(copy)
-
-    order = [(ka, kb) for kb in [*range(1, side), 0] for ka in [*range(1, side), 0]]
-    for ka, kb in order:
-        place = ka * side + kb
-        send(in_ref.at[piece(kb, ka, 1 - core)], c_buf.at[place], c_s.at[place], c_r.at[place], sibling)
-    for ka, kb in order:
-        place = ka * side + kb
-        remote(c_buf.at[place], c_buf.at[place], c_s.at[place], c_r.at[place], sibling).wait_recv()
-        mine = piece(ka, kb, core)
-        if kb:
-            stage[place] = (in_ref[mine].astype(f32) + c_buf[place].astype(f32)).astype(b16)
-            slot = ka * side + kb
-            send(stage.at[place], b_buf.at[slot], b_s.at[slot], b_r.at[slot], second[kb - 1])
-        else:
-            total = in_ref[mine].astype(f32) + c_buf[place].astype(f32)
-            for k in range(1, side):
-                slot = ka * side + k
-                remote(b_buf.at[slot], b_buf.at[slot], b_s.at[slot], b_r.at[slot], sibling).wait_recv()
-                total = total + b_buf[slot].astype(f32)
-            if ka:
-                stage[place] = total.astype(b16)
-                send(stage.at[place], a_buf.at[ka], a_s.at[ka], a_r.at[ka], first[ka - 1])
-            else:
-                for k in range(1, side):
-                    remote(a_buf.at[k], a_buf.at[k], a_s.at[k], a_r.at[k], sibling).wait_recv()
-                    total = total + a_buf[k].astype(f32)
-                stage[place] = total.astype(b16)
-    for k in range(1, n):
-        send(stage.at[0, (z + k) % n], z_buf.at[k], z_s.at[k], z_r.at[k], along_z[k - 1])
-    result = stage[0, z].astype(f32)
-    for k in range(1, n):
-        remote(z_buf.at[k], z_buf.at[k], z_s.at[k], z_r.at[k], sibling).wait_recv()
-        result = result + z_buf[k].astype(f32)
-    out_ref[...] = result
-    for copy in sent:
-        copy.wait_send()
-
-
-def scatter_dense(parts, n, side):
-    rows, width = parts.shape[-2:]
-    parts = parts.reshape(2 * side * side, n, rows, width)
-    shape = (n, rows, width)
-    dma = pltpu.SemaphoreType.DMA
-    size = parts.size * 2
-    return pl.pallas_call(
-        functools.partial(scatter_kernel, n),
-        out_shape=jax.ShapeDtypeStruct((rows, width), f32),
-        in_specs=[pl.BlockSpec(memory_space=pltpu.VMEM)],
-        out_specs=pl.BlockSpec(memory_space=pltpu.VMEM),
-        scratch_shapes=[
-            pltpu.VMEM((side * side, *shape), b16),
-            pltpu.VMEM((side * side, *shape), b16),
-            pltpu.VMEM((side * side, *shape), b16),
-            pltpu.VMEM((side, *shape), b16),
-            pltpu.VMEM((n, rows, width), b16),
-            *[dma((side * side,))] * 4,
-            *[dma((side,))] * 2,
-            *[dma((n,))] * 2,
-        ],
-        compiler_params=pltpu.CompilerParams(
-            collective_id=1, has_side_effects=True, vmem_limit_bytes=3 * size + (8 << 20)
-        ),
-        cost_estimate=CHEAP,
-        name="scatter_dense",
-    )(parts)
+    )(packed, own, slots, marks)
 
 
 TILE = 512
@@ -261,6 +234,23 @@
 NN = ((1,), (0,))
 NT = ((1,), (1,))
 TN = ((0,), (0,))
+
+
+def expert_tile(x, dout, up, up_bias, down):
+    pre = dot(x, up, NT) + up_bias
+    grad_hidden = dot(dout, down, NT)
+    square = pre * pre
+    inner = jnp.tanh(pre * (GELU_C + GELU_C * GELU_K * square))
+    half = 0.5 * pre
+    hidden = (half + half * inner).astype(b16)
+    slope = 0.5 + 0.5 * inner + half * (1.0 - inner * inner) * (GELU_C + 3.0 * GELU_C * GELU_K * square)
+    grad_pre = (slope * grad_hidden).astype(b16)
+    return hidden, grad_pre, dot(hidden, down, NN), dot(grad_pre, up, NN)
+
+
+def bias_rows(first, second):
+    row = lax.broadcasted_iota(jnp.int32, (BIAS_ROWS, D), 0)
+    return jnp.where(row == 0, first, jnp.where(row == 1, second, 0.0))
 
 
 def expert_kernel(sources, first, last, part, *refs):
@@ -300,17 +290,7 @@
     up = w_ref[:part]
     down = w_ref[part : 2 * part]
     up_bias = w_ref[2 * part :][0:1, :part].astype(f32)
-    pre = dot(x, up, NT) + up_bias
-    grad_hidden = dot(dout, down, NT)
-    square = pre * pre
-    inner = jnp.tanh(pre * (GELU_C + GELU_C * GELU_K * square))
-    half = 0.5 * pre
-    hidden = (half + half * inner).astype(b16)
-    slope = 0.5 + 0.5 * inner + half * (1.0 - inner * inner) * (GELU_C + 3.0 * GELU_C * GELU_K * square)
-    grad_pre = slope * grad_hidden
-    grad_pre_b = grad_pre.astype(b16)
-    out = dot(hidden, down, NN)
-    grad_x = dot(grad_pre_b, up, NN)
+    hidden, grad_pre_b, out, grad_x = expert_tile(x, dout, up, up_bias, down)
     if not first:
         out = out + sums[0][...]
         grad_x = grad_x + sums[1][...]
@@ -326,8 +306,7 @@
     def _():
         grad_up_ref[...] = up_acc[...].astype(grad_up_ref.dtype)
         grad_down_ref[:part] = down_acc[...].astype(grad_down_ref.dtype)
-        row = lax.broadcasted_iota(jnp.int32, (BIAS_ROWS, D), 0)
-        tail = jnp.where(row == 0, bias_acc[0:1, :], jnp.where(row == 1, bias_ref[0:1, :], 0.0))
+        tail = bias_rows(bias_acc[0:1, :], bias_ref[0:1, :])
         grad_down_ref[part:] = tail.astype(grad_down_ref.dtype)
 
 
@@ -369,7 +348,7 @@
             pltpu.SemaphoreType.DMA,
         ],
         compiler_params=pltpu.CompilerParams(vmem_limit_bytes=56 << 20, dimension_semantics=("arbitrary",)),
-        cost_estimate=pl.CostEstimate(flops=12 * slots * part * D, bytes_accessed=slots * D * 20, transcendentals=0),
+        cost_estimate=pl.CostEstimate(flops=48 * slots * part * D, bytes_accessed=slots * D * 20, transcendentals=0),
         name=name,
     )(*weights, x, dout, biases, *([] if first else sums))
 
@@ -405,81 +384,77 @@
     return jnp.where(lanes_like(even) < HEAD_DIM, even, odd)
 
 
-def attention_kernel(
-    lengths_ref, tokens_ref, weights_ref, vector_ref, router_ref, routes_ref, places_ref,
+def sequence_forward(
+    s, lengths_ref, tokens_ref, weights_ref, vector_ref, router_ref, routes_ref, places_ref,
     normed_ref, q_ref, k_ref, v_ref, context_ref, lse_ref, resid_ref, normed_two_ref, gates_ref, slots_ref,
 ):
-    length = lengths_ref[pl.program_id(0)]
-    rows = tokens_ref[...].astype(f32)
+    at = pl.ds(s * LEN, LEN)
+    length = lengths_ref[s]
+    rows = tokens_ref[at, :].astype(f32)
     hat, _ = normal(rows)
     normed = (hat * vector_ref[0:1, :] + vector_ref[1:2, :]).astype(b16)
-    normed_ref[...] = normed
-    q_ref[...] = (dot(normed, weights_ref[0], NN) + vector_ref[2:3, :]).astype(b16)
-    k_ref[...] = dot(normed, weights_ref[1], NN).astype(b16)
-    v_ref[...] = (dot(normed, weights_ref[2], NN) + vector_ref[3:4, :]).astype(b16)
+    normed_ref[at, :] = normed
+    q_ref[at, :] = (dot(normed, weights_ref[0], NN) + vector_ref[2:3, :]).astype(b16)
+    k_ref[at, :] = dot(normed, weights_ref[1], NN).astype(b16)
+    v_ref[at, :] = (dot(normed, weights_ref[2], NN) + vector_ref[3:4, :]).astype(b16)
     lse = jnp.zeros((LEN, 128), f32)
     for pair in range(PAIRS):
         lanes = slice(pair * WIDE, (pair + 1) * WIDE)
-        keys, values = k_ref[:, lanes], v_ref[:, lanes]
+        keys, values = k_ref[at, lanes], v_ref[at, lanes]
         mixed = []
-        for half, part in enumerate(halves(q_ref[:, lanes])):
+        for half, part in enumerate(halves(q_ref[at, lanes])):
             scores = scores_of(part, keys, length)
             top = jnp.max(scores, axis=-1, keepdims=True)
             total = top + jnp.log(jnp.sum(jnp.exp(scores - top), axis=-1, keepdims=True))
             chance = jnp.exp(scores - total).astype(b16)
             mixed.append(dot(chance, values, NN))
             lse = jnp.where(lanes_like(lse) == 2 * pair + half, total, lse)
-        context_ref[:, lanes] = joined(*mixed).astype(b16)
-    lse_ref[...] = lse
-    resid = rows + (dot(context_ref[...], weights_ref[3], NN) + vector_ref[4:5, :])
-    resid_ref[...] = resid
+        context_ref[at, lanes] = joined(*mixed).astype(b16)
+    lse_ref[at, :] = lse
+    resid = rows + (dot(context_ref[at, :], weights_ref[3], NN) + vector_ref[4:5, :])
+    resid_ref[at, :] = resid
     hat, _ = normal(resid)
     normed_two = (hat * vector_ref[5:6, :] + vector_ref[6:7, :]).astype(b16)
-    normed_two_ref[...] = normed_two
+    normed_two_ref[at, :] = normed_two
     logits = dot(normed_two, router_ref[...], NT)
     names = lanes_like(logits)
-    first = jnp.sum(jnp.where(names == routes_ref[:, 0:1], logits, 0.0), axis=-1, keepdims=True)
-    second = jnp.sum(jnp.where(names == routes_ref[:, 1:2], logits, 0.0), axis=-1, keepdims=True)
-    gate = lanes_like(gates_ref[...])
-    gates_ref[...] = jnp.where(gate == 0, jax.nn.sigmoid(first - second), jax.nn.sigmoid(second - first))
+    routes = routes_ref[at, :]
+    first = jnp.sum(jnp.where(names == routes[:, 0:1], logits, 0.0), axis=-1, keepdims=True)
+    second = jnp.sum(jnp.where(names == routes[:, 1:2], logits, 0.0), axis=-1, keepdims=True)
+    gates_ref[at, :] = jnp.where(names == 0, jax.nn.sigmoid(first - second), jax.nn.sigmoid(second - first))
     experts, _, capacity, _ = slots_ref.shape
     slots = experts * capacity
     ids = lax.broadcasted_iota(jnp.int32, (slots, ROWS), 0)
-    places = places_ref[0]
+    places = places_ref[s]
     chosen = jnp.where((ids == places[0:1, :]) | (ids == places[1:2, :]), 1.0, 0.0).astype(b16)
     sent = dot(chosen, normed_two, NN).astype(b16)
-    slots_ref[...] = sent.reshape(experts, 1, capacity, D)
+    slots_ref[:, s] = sent.reshape(experts, capacity, D)
+
+
+def kept_shapes(count, experts, capacity):
+    return [
+        *[jax.ShapeDtypeStruct((count, D), b16)] * 5,
+        jax.ShapeDtypeStruct((count, 128), f32),
+        jax.ShapeDtypeStruct((count, D), f32),
+        jax.ShapeDtypeStruct((count, D), b16),
+        jax.ShapeDtypeStruct((count, 128), f32),
+        jax.ShapeDtypeStruct((experts, count // ROWS, capacity, D), b16),
+    ]
 
 
 def attention_forward(lengths, tokens, weights, vector, router, routes, places, experts, capacity):
     count = tokens.shape[0]
-    rows = pl.BlockSpec((LEN, D), lambda i: (i, 0))
-    lanes = pl.BlockSpec((LEN, 128), lambda i: (i, 0))
-    once = pl.Buffered(1)
+    vmem = pl.BlockSpec(memory_space=pltpu.VMEM)
+
+    def kernel(*refs):
+        for s in range(count // LEN):
+            sequence_forward(s, *refs)
+
     return pl.pallas_call(
-        attention_kernel,
-        grid=(count // LEN,),
-        in_specs=[
-            pl.BlockSpec(memory_space=pltpu.SMEM),
-            rows,
-            pl.BlockSpec((4, D, D), lambda i: (0, 0, 0), pipeline_mode=once),
-            pl.BlockSpec((8, D), lambda i: (0, 0)),
-            pl.BlockSpec((128, D), lambda i: (0, 0)),
-            pl.BlockSpec((LEN, 2), lambda i: (i, 0)),
-            pl.BlockSpec((1, 2, ROWS), lambda i: (i, 0, 0)),
-        ],
-        out_specs=[
-            rows, rows, rows, rows, rows, lanes, rows, rows, lanes,
-            pl.BlockSpec((experts, 1, capacity, D), lambda i: (0, i, 0, 0)),
-        ],
-        out_shape=[
-            *[jax.ShapeDtypeStruct((count, D), b16)] * 5,
-            jax.ShapeDtypeStruct((count, 128), f32),
-            jax.ShapeDtypeStruct((count, D), f32),
-            jax.ShapeDtypeStruct((count, D), b16),
-            jax.ShapeDtypeStruct((count, 128), f32),
-            jax.ShapeDtypeStruct((experts, count // ROWS, capacity, D), b16),
-        ],
+        kernel,
+        in_specs=[pl.BlockSpec(memory_space=pltpu.SMEM), *[vmem] * 6],
+        out_specs=[vmem] * 10,
+        out_shape=kept_shapes(count, experts, capacity),
         compiler_params=pltpu.CompilerParams(vmem_limit_bytes=48 << 20),
         cost_estimate=CHEAP,
         name="attention_forward",
@@ -574,8 +549,277 @@
     input_grad_ref[at, :] += norm_back(grad_one, hat, rate, vector_ref[0:1, :])
 
 
-KINDS = 6
-FAR, MIDDLE, NEAR, FAR_ON, MIDDLE_ON, FAR_LAST = range(KINDS)
+def begin_kernel(
+    n, cols, seqs, part, lengths_ref, in_ref, own_ref, slots_ref, marks_ref, tokens_ref, routes_ref, places_ref,
+    weights_ref, vector_ref, router_ref, normed_ref, q_ref, k_ref, v_ref, context_ref, lse_ref, resid_ref, normed_two_ref,
+    gates_ref, out_ref, back_ref, mine_up, mine_down, near_up, near_down, middle_up, middle_down, far_up, far_down,
+    near_up_in, near_down_in,
+    pool, acc, second_ref, third_ref, fourth_ref, going, x_in, dout_in, marks_in, out_acc, back_acc, bias_acc, tail_ref,
+    local_sem, part_s, part_r, slot_s, slot_r, mark_s, mark_r, x_s, x_r, near_s, near_r, store_s, *sems,
+):
+    side, z, y, x, core = where_am_i()
+    mine = lax.axis_index("expert")
+    experts, _, capacity, _ = slots_ref.shape
+    slots = experts * seqs * capacity
+    greet([*peers_of(n, side, z, y, x, core)[0], *[(z, (mine + k) % experts) for k in range(1, experts)]])
+    me = ((z * side + y) * side + x) * 2 + core
+    block_rows = in_ref.shape[0]
+    stage_rows = 2 * part + BIAS_ROWS
+
+    def block_at(device):
+        return pool.at[pl.ds(pl.multiple_of(device * block_rows, 16), block_rows), :]
+
+    def sender(ref, e, b=0, blocks=seqs):
+        return ref.at[pl.ds(pl.multiple_of((e * seqs + b) * capacity, 16), blocks * capacity), :]
+
+    flat_slots = slots_ref.reshape(slots, D)
+    flat_marks = marks_ref.reshape(slots, 128)
+    stays = [
+        pltpu.make_async_copy(in_ref, block_at(me), local_sem.at[0]),
+        pltpu.make_async_copy(sender(flat_slots, mine), sender(dout_in, mine), local_sem.at[1]),
+        pltpu.make_async_copy(sender(flat_marks, mine), sender(marks_in, mine), local_sem.at[2]),
+    ]
+    for copy in stays:
+        copy.start()
+    inner = (z + 1) // 2 % 2 == 1
+    outer = jnp.logical_not(inner)
+    inward, across, outward = (1 + z // 2, mine), (3 - z, mine), (3 * (z // 2), mine)
+
+    def hop(k, src, dst, peer):
+        return remote(src, dst, part_s.at[k], part_r.at[k], peer)
+
+    beside = hop(0, own_ref, second_ref, (z + 1 - 2 * (z % 2), mine))
+    own_across = hop(1, own_ref, third_ref, across)
+    third_on = hop(2, third_ref, third_ref, outward)
+    second_across = hop(3, second_ref, fourth_ref, across)
+    fourth_on = hop(4, fourth_ref, fourth_ref, outward)
+
+    def weights_on():
+        beside.start()
+
+        @pl.when(inner)
+        def _():
+            own_across.start()
+
+    early = [
+        (lambda e: sender(flat_slots, e), lambda e: sender(dout_in, e), slot_s, slot_r),
+        (lambda e: sender(flat_marks, e), lambda e: sender(marks_in, e), mark_s, mark_r),
+    ]
+    more = []
+    sent = spread_blocks(n, in_ref, block_at, sems, weights_on, lambda: exchange_all(early, more))
+    stays[0].wait()
+
+    for pair in range(2):
+        def spread(device, carry):
+            rows = block_at(device)[2 * pair * cols : 2 * (pair + 1) * cols, :].astype(f32)
+            place = pl.ds(pl.multiple_of(device * cols, 8), cols)
+            acc[0, place, :] = rows[:cols]
+            acc[1, place, :] = rows[cols:]
+            return carry
+
+        lax.fori_loop(0, n * experts, spread, 0)
+        weights_ref[2 * pair] = acc[0].astype(b16)
+        weights_ref[2 * pair + 1] = acc[1].astype(b16)
+
+    def gather_small(device, total):
+        return total + block_at(device)[4 * cols :, :].astype(f32)
+
+    small = lax.fori_loop(0, n * experts, gather_small, jnp.zeros((block_rows - 4 * cols, D), f32))
+    vector_ref[...] = small[:8]
+    router_ref[...] = jnp.zeros_like(router_ref)
+    router_ref[: block_rows - 4 * cols - 8, :] = small[8:].astype(b16)
+
+    late = []
+    for s in range(seqs):
+        sequence_forward(
+            s, lengths_ref, tokens_ref, weights_ref, vector_ref, router_ref, routes_ref, places_ref,
+            normed_ref, q_ref, k_ref, v_ref, context_ref, lse_ref, resid_ref, normed_two_ref, gates_ref, going,
+        )
+        dst = functools.partial(sender, x_in, b=s, blocks=1)
+        late.append((functools.partial(lambda e, s: going.at[e, s], s=s), dst, x_s.at[s], x_r.at[s]))
+        exchange_all(late[-1:], more)
+        stays.append(pltpu.make_async_copy(going.at[mine, s], dst(mine), local_sem.at[3 + s]))
+        stays[-1].start()
+    beside.wait()
+
+    @pl.when(inner)
+    def _():
+        second_across.start()
+        own_across.wait()
+        third_on.start()
+
+    wait_all(early)
+    wait_all(late)
+    for copy in [*sent, *more]:
+        copy.wait_send()
+    for copy in stays[1:]:
+        copy.wait()
+
+    up_acc, down_acc = acc.at[0], acc.at[1]
+    tiles = slots // TILE
+    down_bias = jnp.zeros((1, D), f32)
+    stores = []
+    outs = [(mine_up, mine_down), (near_up, near_down), (middle_up, middle_down), (far_up, far_down)]
+    near_in = (near_up_in, near_down_in)
+    bias_acc[...] = jnp.zeros_like(bias_acc)
+    for p, w_ref in enumerate((own_ref, second_ref, third_ref, fourth_ref)):
+        if p == 1:
+
+            @pl.when(inner)
+            def _():
+                second_across.wait()
+                fourth_on.start()
+
+        if p == 2:
+
+            @pl.when(outer)
+            def _():
+                third_on.wait_recv()
+
+        if p == 3:
+
+            @pl.when(outer)
+            def _():
+                fourth_on.wait_recv()
+
+        down_bias = down_bias + w_ref[2 * part :, :].astype(f32)[1:2, :]
+        up_acc[...] = jnp.zeros_like(up_acc)
+        down_acc[...] = jnp.zeros_like(down_acc)
+        bias_acc[0:1, :] = jnp.zeros((1, D), f32)
+
+        def tile(t, carry):
+            rows = pl.ds(pl.multiple_of(t * TILE, TILE), TILE)
+            x = x_in[rows, :]
+            if p == 0:
+                logits = dot(x, router_ref[...], NT)
+                signs = jnp.where(lanes_like(logits) == mine, 1.0, -marks_in[rows, :].astype(f32))
+                margin = jnp.sum(logits * signs, axis=-1, keepdims=True)
+                dout = (jax.nn.sigmoid(margin) * dout_in[rows, :].astype(f32)).astype(b16)
+                dout_in[rows, :] = dout
+                bias_acc[1:2, :] += column_sum(dout.astype(f32))
+            else:
+                dout = dout_in[rows, :]
+            up_bias = w_ref[2 * part :, :].astype(f32)[0:1, :part]
+            hidden, grad_pre, out, back = expert_tile(x, dout, w_ref[:part, :], up_bias, w_ref[part : 2 * part, :])
+            down_acc[...] += dot(hidden, dout, TN)
+            up_acc[...] += dot(grad_pre, x, TN)
+            bias_acc[0:1, :] += column_sum(grad_pre.astype(f32))
+            if p == 0:
+                out_acc[rows, :] = out
+                back_acc[rows, :] = back
+            elif p < 3:
+                out_acc[rows, :] += out
+                back_acc[rows, :] += back
+            else:
+                x_in[rows, :] = (out_acc[rows, :] + out + down_bias).astype(b16)
+                dout_in[rows, :] = (back_acc[rows, :] + back).astype(b16)
+            return carry
+
+        lax.fori_loop(0, tiles, tile, 0)
+        tail = bias_rows(bias_acc[0:1, :], bias_acc[1:2, :])
+        base = stage_rows if p > 1 else 0
+        if p == 0:
+            tail_ref[...] = tail
+            now = [
+                pltpu.make_async_copy(up_acc, mine_up, store_s.at[0]),
+                pltpu.make_async_copy(down_acc, mine_down.at[pl.ds(0, part), :], store_s.at[1]),
+                pltpu.make_async_copy(tail_ref, mine_down.at[pl.ds(part, BIAS_ROWS), :], store_s.at[2]),
+            ]
+            for copy in now:
+                copy.start()
+            for copy in now:
+                copy.wait()
+        else:
+            if p == 3:
+                for copy in stores[2:]:
+                    copy.wait()
+                del stores[2:]
+            pool[base : base + part, :] = up_acc[...].astype(b16)
+            pool[base + part : base + 2 * part, :] = down_acc[...].astype(b16)
+            pool[base + 2 * part : base + stage_rows, :] = tail.astype(b16)
+            halves_of = [pool.at[pl.ds(base, part), :], pool.at[pl.ds(base + part, part + BIAS_ROWS), :]]
+            for h in range(2):
+                stores.append(pltpu.make_async_copy(halves_of[h], outs[p][h], store_s.at[1 + 2 * p + h]))
+                stores[-1].start()
+            if p == 1:
+                nears = [remote(halves_of[h], near_in[h], near_s.at[h], near_r.at[h], inward) for h in range(2)]
+
+                @pl.when(outer)
+                def _():
+                    for copy in nears:
+                        copy.start()
+
+    for src, dst, k in ((x_in, out_ref, 9), (dout_in, back_ref, 10)):
+        stores.append(pltpu.make_async_copy(src, dst, store_s.at[k]))
+        stores[-1].start()
+    for copy in stores:
+        copy.wait()
+
+    @pl.when(inner)
+    def _():
+        third_on.wait_send()
+        fourth_on.wait_send()
+        for copy in nears:
+            copy.wait_recv()
+
+    @pl.when(outer)
+    def _():
+        for copy in nears:
+            copy.wait_send()
+
+
+def begin(n, side, cols, lengths, packed, own, slots, marks, tokens, routes, places):
+    devices = n * side * side * 2
+    experts, blocks, capacity, _ = slots.shape
+    count = tokens.shape[0]
+    total = experts * blocks * capacity
+    part = (own.shape[0] - BIAS_ROWS) // 2
+    dma = pltpu.SemaphoreType.DMA
+    vmem, hbm = pl.BlockSpec(memory_space=pltpu.VMEM), pl.BlockSpec(memory_space=pl.ANY)
+    *kept, going = kept_shapes(count, experts, capacity)
+
+    def halves_in(dtype):
+        return [jax.ShapeDtypeStruct((part, D), dtype), jax.ShapeDtypeStruct((part + BIAS_ROWS, D), dtype)]
+
+    return pl.pallas_call(
+        functools.partial(begin_kernel, n, cols, blocks, part),
+        out_shape=[
+            jax.ShapeDtypeStruct((4, D, D), b16),
+            jax.ShapeDtypeStruct((8, D), f32),
+            jax.ShapeDtypeStruct((128, D), b16),
+            *kept,
+            *[jax.ShapeDtypeStruct((total, D), b16)] * 2,
+            *halves_in(f32),
+            *halves_in(b16) * 4,
+        ],
+        in_specs=[pl.BlockSpec(memory_space=pltpu.SMEM), vmem, vmem, hbm, hbm, vmem, vmem, vmem],
+        out_specs=[*[vmem] * 12, *[hbm] * 12],
+        scratch_shapes=[
+            pltpu.VMEM((max(devices * packed.shape[0], 2 * own.shape[0]), D), b16),
+            pltpu.VMEM((2, D, D), f32),
+            *[pltpu.VMEM(own.shape, b16)] * 3,
+            pltpu.VMEM(going.shape, b16),
+            *[pltpu.VMEM((total, D), b16)] * 2,
+            pltpu.VMEM((total, 128), b16),
+            *[pltpu.VMEM((total, D), f32)] * 2,
+            pltpu.VMEM((8, D), f32),
+            pltpu.VMEM((BIAS_ROWS, D), f32),
+            dma((3 + blocks,)),
+            *[dma((5,))] * 2,
+            *[dma((experts,))] * 4,
+            *[dma((blocks, experts))] * 2,
+            *[dma((2,))] * 2,
+            dma((11,)),
+            *spread_sems(n, side),
+        ],
+        compiler_params=pltpu.CompilerParams(collective_id=0, has_side_effects=True, vmem_limit_bytes=63 << 20),
+        cost_estimate=CHEAP,
+        name="begin",
+    )(lengths, packed, own, slots, marks, tokens, routes, places)
+
+
+KINDS = 5
+FAR, MIDDLE, FAR_ON, MIDDLE_ON, FAR_LAST = range(KINDS)
 
 
 def finish_kernel(
@@ -583,7 +827,7 @@
     lengths_ref, tokens_ref, grad_ref, weights_ref, vector_ref, router_ref, routes_ref, places_ref,
     normed_ref, q_ref, k_ref, v_ref, context_ref, lse_ref, resid_ref, normed_two_ref, gates_ref, outs_ref, backs_ref,
     near_up, near_down, middle_up, middle_down, far_up, far_down,
-    output_ref, input_grad_ref, dense_ref, near_up_in, near_down_in, middle_up_in, middle_down_in, end_up_in, end_down_in,
+    output_ref, input_grad_ref, dense_ref, middle_up_in, middle_down_in, end_up_in, end_down_in,
     outs_in, backs_in, weights_acc, vector_acc, router_acc, dq_ref, dk_ref, dv_ref,
     far_up_buf, far_down_buf, middle_up_buf, middle_down_buf, on_up_buf, on_down_buf, load_up, load_down,
     parts, stage, c_buf, b_buf, a_buf, z_buf,
@@ -599,11 +843,6 @@
     area = side * side if inside else 0
     sent = []
 
-    def remote(src, dst, send, recv, peer):
-        return pltpu.make_async_remote_copy(
-            src_ref=src, dst_ref=dst, send_sem=send, recv_sem=recv, device_id=peer, device_id_type=MESH
-        )
-
     def send(src, dst, send_sem, recv_sem, peer):
         copy = remote(src, dst, send_sem, recv_sem, peer)
         copy.start()
@@ -628,7 +867,7 @@
     across = (3 - z, mine)
     outward = (3 * (z // 2), mine)
     near, middle, far = (near_up, near_down), (middle_up, middle_down), (far_up, far_down)
-    near_in, middle_in = (near_up_in, near_down_in), (middle_up_in, middle_down_in)
+    middle_in = (middle_up_in, middle_down_in)
     end_in = (end_up_in, end_down_in)
     far_buf, middle_buf, on_buf = (far_up_buf, far_down_buf), (middle_up_buf, middle_down_buf), (on_up_buf, on_down_buf)
     loads = (load_up, load_down)
@@ -636,7 +875,7 @@
     def hop(kind, half, src, dst, peer):
         return remote(src, dst, chain_s.at[kind, half], chain_r.at[kind, half], peer)
 
-    from_ends = [(FAR, far, far_buf), (MIDDLE, middle, middle_buf), (NEAR, near, near_in)]
+    from_ends = [(FAR, far, far_buf), (MIDDLE, middle, middle_buf)]
 
     @pl.when(outer)
     def _():
@@ -759,7 +998,6 @@
             hop(FAR_LAST, half, on_buf[half], end_in[half], outward).wait_send()
             hop(MIDDLE_ON, half, middle_buf[half], middle_in[half], across).wait_send()
             hop(MIDDLE_ON, half, middle_in[half], middle_in[half], across).wait_recv()
-            hop(NEAR, half, near_in[half], near_in[half], outward).wait_recv()
 
 
 def finish(n, side, cols, extra, lengths, rows_in, kept, outs, backs, grads):
@@ -783,12 +1021,12 @@
             hbm,
             *[hbm] * len(grads),
         ],
-        out_specs=[vmem, vmem, vmem, *[hbm] * 6],
+        out_specs=[vmem, vmem, vmem, *[hbm] * 4],
         out_shape=[
             jax.ShapeDtypeStruct((count, D), f32),
             jax.ShapeDtypeStruct((count, D), f32),
             jax.ShapeDtypeStruct((rows, D), f32),
-            *shapes * 3,
+            *shapes * 2,
         ],
         scratch_shapes=[
             pltpu.VMEM(slots, b16),
@@ -818,16 +1056,12 @@
     )(lengths, *rows_in, *kept, outs, backs, *grads)
 
 
-def pack_expert(up, down, up_bias, down_bias, dtype):
+def pack_expert(up, down, up_bias, down_bias, start, dtype):
     part = up.shape[0]
     tail = jnp.zeros((BIAS_ROWS, D), dtype)
     tail = tail.at[0, :part].set(up_bias.astype(dtype))
-    tail = tail.at[1, : down_bias.shape[0]].set(down_bias.astype(dtype))
+    tail = lax.dynamic_update_slice(tail, down_bias.astype(dtype)[None], (1, start))
     return jnp.concatenate([up.astype(dtype), down.astype(dtype), tail], axis=0)
-
-
-def after(x, *others):
-    return lax.optimization_barrier((x, *others))[0]
 
 
 def along(x, *pairs):
@@ -854,108 +1088,94 @@
     mine = lax.axis_index("expert")
     both = ("dp", "expert")
 
+    side = math.isqrt(experts // 2)
+    inside = cols if cols % 8 == 0 else 0
+    small_rows = -(-(8 + experts) // 16) * 16
     flat_len = (7 + experts) * cols
-    extra = -(-(4 * cols + -(-flat_len // D)) // 16) * 16 - 4 * cols
-    side = math.isqrt(experts // 2)
-    small = jnp.concatenate([gain_bias, router], axis=0).astype(b16).reshape(-1)
-    small = jnp.pad(small, (0, extra * D - flat_len)).reshape(extra, D)
+    if inside:
+        small = jnp.zeros((small_rows, D), b16)
+        column = (me * experts + mine) * cols
+        small = lax.dynamic_update_slice(small, gain_bias.astype(b16), (0, column))
+        small = lax.dynamic_update_slice(small, router.astype(b16), (8, column))
+    else:
+        extra = -(-(4 * cols + -(-flat_len // D)) // 16) * 16 - 4 * cols
+        small = jnp.concatenate([gain_bias, router], axis=0).astype(b16).reshape(-1)
+        small = jnp.pad(small, (0, extra * D - flat_len)).reshape(extra, D)
     packed = jnp.concatenate([attention.astype(b16).reshape(4 * cols, D), small], axis=0)
-    whole = gather_dense(packed, n_dp, side)
-    own = after(pack_expert(expert_up[0], expert_down[0], up_bias[0], down_bias[0], b16), whole)
-
-    second = along(own, (0, 1), (1, 0), (2, 3), (3, 2))
-    third_inner = along(own, (1, 2), (2, 1))
-    third_outer = along(third_inner, (1, 0), (2, 3))
-    fourth_inner = along(second, (1, 2), (2, 1))
-    fourth_outer = along(fourth_inner, (1, 0), (2, 3))
-
-    weights_b = whole[:, : 4 * cols].reshape(devices, 4, cols, D).transpose(1, 0, 2, 3).reshape(4, D, D)
-    small = whole[:, 4 * cols :].reshape(devices, extra * D)[:, :flat_len].reshape(devices, 7 + experts, cols)
-    small = small.transpose(1, 0, 2).reshape(7 + experts, D)
-    vector = small[:7].astype(f32)
-    router_b = small[7:]
+    own = pack_expert(expert_up[0], expert_down[0], up_bias[0], down_bias[0], me * narrow, b16)
 
     positions = slots_of(routes, experts, capacity)
     slot_ids = jnp.arange(experts * capacity, dtype=jnp.int32)
     hit = positions[:, :, :, None] == slot_ids
     split = jnp.any(hit, axis=2).astype(b16).reshape(blocks, ROWS, experts, capacity)
-    other = jnp.flip(routes, axis=1).reshape(blocks, ROWS, 2)
-    partner = jnp.sum(jnp.where(hit, other[:, :, :, None], 0), axis=(1, 2)).astype(f32)
-    partner = partner.reshape(blocks, experts, capacity).transpose(1, 0, 2)
-    partner = lax.all_to_all(partner, "expert", split_axis=0, concat_axis=0, tiled=True)
-    grad_rows = out_grad.reshape(blocks, ROWS, D)
-
-    sent = jnp.einsum("btec,btd->ebcd", split, grad_rows, preferred_element_type=f32).astype(b16)
-    sent = after(sent, whole)
-    grad_slots = lax.all_to_all(sent, "expert", split_axis=0, concat_axis=0, tiled=True)
-    grad_slots = grad_slots.reshape(experts * blocks * capacity, D)
-
-    router_all = jnp.pad(router_b, ((0, 128 - experts), (0, 0)))
-    vector_all = jnp.pad(vector, ((0, 1), (0, 0)))
-    *kept, slots_out = attention_forward(
-        lengths, tokens, weights_b, vector_all, router_all, routes, positions.transpose(0, 2, 1), experts, capacity
-    )
-
-    def exchange(sent):
-        return lax.all_to_all(sent, "expert", split_axis=0, concat_axis=0, tiled=True)
-
-    slots_in = exchange(after(slots_out, grad_slots)).reshape(experts * blocks * capacity, D)
-
-    slot_logits = jnp.einsum("sd,ed->se", slots_in, router_b, preferred_element_type=f32)
-    ids = jnp.arange(experts, dtype=jnp.int32)
-    rival = partner.reshape(-1).astype(jnp.int32)
-    margin = jnp.sum(
-        slot_logits * ((ids == mine).astype(f32) - (rival[:, None] == ids).astype(f32)), axis=-1
-    )
-    dout = (jax.nn.sigmoid(margin)[:, None] * grad_slots.astype(f32)).astype(b16)
-    grad_down_bias = jnp.sum(dout.astype(f32), axis=0)
-
-    def pick(*arrays):
-        out = arrays[-1]
-        for i in range(len(arrays) - 2, -1, -1):
-            out = jnp.where(me == i, arrays[i], out)
-        return out
-
+    marked = jnp.any(routes[:, :, None] == jnp.arange(128, dtype=jnp.int32), axis=1).astype(b16)
+
+    def by_slot(rows):
+        sent = jnp.einsum("btec,btd->ebcd", split, rows.reshape(blocks, ROWS, -1), preferred_element_type=f32)
+        return sent.astype(b16)
+
+    places = positions.transpose(0, 2, 1)
     inner = (me == 1) | (me == 2)
-    tail = 2 * part + 1
-    names = [me, pick(1, 0, 3, 2), pick(2, 2, 1, 1), pick(3, 3, 0, 0)]
-    bias_rows = [
-        own[tail, :narrow],
-        second[tail, :narrow],
-        jnp.where(inner, third_inner[tail, :narrow], third_outer[tail, :narrow]),
-        jnp.where(inner, fourth_inner[tail, :narrow], fourth_outer[tail, :narrow]),
-    ]
-    place = jnp.stack(names)
-    down_bias_full = jnp.zeros((n_dp, narrow), b16).at[place].set(jnp.stack(bias_rows)).reshape(D)
-    weights = [(own,), (second,), (third_inner, third_outer), (fourth_inner, fourth_outer)]
-    sums = None
-    part_grads = []
-    for i in range(4):
-        share = lax.dynamic_slice(grad_down_bias, (names[i] * narrow,), (narrow,))
-        share = jnp.pad(share, (0, D - narrow))
-        biases = jnp.stack([share, down_bias_full.astype(f32) if i == 3 else share])
-        *sums, grad_up, grad_down = expert_part(
-            weights[i], slots_in, dout, biases, sums, i == 3, b16 if i else f32, f"expert_part_{i}"
+    if inside:
+        weights_b, vector_all, router_all, *got = begin(
+            n_dp, side, cols, lengths, packed, own, by_slot(out_grad), by_slot(marked), tokens, routes, places
         )
-        part_grads.append((grad_up, grad_down))
-    out_b, grad_b = sums
-
-    small_rows = -(-(8 + experts) // 16) * 16
+        kept, out_b, back_b, grads, near_in = got[:9], got[9], got[10], got[11:19], got[19:]
+    else:
+        whole, second, third_inner, grad_slots, marks = gather_dense(
+            packed, own, by_slot(out_grad), by_slot(marked), n_dp, side
+        )
+        weights_b = whole[:, : 4 * cols].reshape(devices, 4, cols, D).transpose(1, 0, 2, 3).reshape(4, D, D)
+        small = whole[:, 4 * cols :].reshape(devices, extra * D)[:, :flat_len].reshape(devices, 7 + experts, cols)
+        small = small.transpose(1, 0, 2).reshape(7 + experts, D)
+        vector_all = jnp.pad(small[:7].astype(f32), ((0, 1), (0, 0)))
+        router_all = jnp.pad(small[7:], ((0, 128 - experts), (0, 0)))
+        *kept, slots_out = attention_forward(
+            lengths, tokens, weights_b, vector_all, router_all, routes, places, experts, capacity
+        )
+        slots_in = lax.all_to_all(slots_out, "expert", split_axis=0, concat_axis=0, tiled=True)
+        slots_in = slots_in.reshape(experts * blocks * capacity, D)
+        grad_slots = grad_slots.reshape(experts * blocks * capacity, D)
+        marks = marks.reshape(experts * blocks * capacity, 128)
+        third_outer = along(third_inner, (1, 0), (2, 3))
+        fourth_inner = along(second, (1, 2), (2, 1))
+        fourth_outer = along(fourth_inner, (1, 0), (2, 3))
+        slot_logits = jnp.einsum("sd,ed->se", slots_in, router_all, preferred_element_type=f32)
+        this = jnp.arange(128, dtype=jnp.int32) == mine
+        margin = jnp.sum(slot_logits * jnp.where(this, 1.0, -marks.astype(f32)), axis=-1)
+        dout = (jax.nn.sigmoid(margin)[:, None] * grad_slots.astype(f32)).astype(b16)
+        grad_down_bias = jnp.sum(dout.astype(f32), axis=0)
+        row = 2 * part + 1
+        down_bias_full = own[row].astype(f32) + second[row].astype(f32)
+        down_bias_full += jnp.where(inner, third_inner[row], third_outer[row]).astype(f32)
+        down_bias_full += jnp.where(inner, fourth_inner[row], fourth_outer[row]).astype(f32)
+        biases = jnp.stack([grad_down_bias, down_bias_full])
+        weights = [(own,), (second,), (third_inner, third_outer), (fourth_inner, fourth_outer)]
+        sums = None
+        grads = []
+        for i in range(4):
+            *sums, grad_up, grad_down = expert_part(
+                weights[i], slots_in, dout, biases, sums, i == 3, b16 if i else f32, f"expert_part_{i}"
+            )
+            grads += [grad_up, grad_down]
+        out_b, back_b = sums
+        near_in = [along(g, (0, 1), (3, 2)) for g in grads[2:4]]
+
     slots_shape = (experts, blocks, capacity, D)
     output, input_grad, dense, *came = finish(
         n_dp, side, cols, small_rows, lengths,
         (tokens, out_grad, weights_b, vector_all, router_all, routes, positions.reshape(count, 2)),
-        kept, out_b.reshape(slots_shape), grad_b.reshape(slots_shape), [g for i in (1, 2, 3) for g in part_grads[i]],
+        kept, out_b.reshape(slots_shape), back_b.reshape(slots_shape), grads[2:],
     )
     totals = [
-        part_grads[0][i]
-        + jnp.where(inner, came[i].astype(f32) + came[2 + i].astype(f32), came[4 + i].astype(f32))
+        grads[i]
+        + jnp.where(inner, near_in[i].astype(f32) + came[i].astype(f32), came[2 + i].astype(f32))
         for i in range(2)
     ]
     shard_up = totals[0][None]
     shard_down = totals[1][:part][None]
     shard_up_bias = totals[1][part, :part][None]
-    shard_down_bias = totals[1][part + 1, :narrow][None]
+    shard_down_bias = lax.dynamic_slice(totals[1], (part + 1, me * narrow), (1, narrow))
     if cols % 8:
         small = lax.psum(dense[:small_rows], both)
         big = dense[small_rows:].reshape(4, D, D).astype(b16)

time: 489 us -> 418 us (0.85)
  waiting for transfers between devices: 67 us -> 0 us
  Pallas kernels: 319 us -> 370 us
  local copies, waits for them, and re-layouts: 37.4 us -> 8.76 us
  starting transfers between devices: 20.4 us -> 0 us
    pallas_call x6 -> x1, Pallas kernels: 144 us -> 210 us  [begin(): pl.pallas_call(functools.partial(begin_kernel, n, cols, blocks, part), ou...]
    all_to_all x3 -> x0, waiting for transfers between devices: 41.5 us -> none  [the longest x1 26.6 us: exchange(): lax.all_to_all(sent, 'expert', split_axis=0, concat_axis=0, tiled=True)]
    ppermute x5 -> x0, waiting for transfers between devices: 25.5 us -> none  [along(): return lax.ppermute(x, 'dp', pairs)]
    pallas_call x1, Pallas kernels: 175 us -> 160 us  [finish(): pl.pallas_call(functools.partial(finish_kernel, n, cols, extra, count //...]
    all_to_all x3 -> x0, starting transfers between devices: 12.6 us -> none  [the longest x1 5.17 us: body(): lax.all_to_all(partner, 'expert', split_axis=0, concat_axis=0, tiled=True)]
    unnamed x92 -> x69, local copies, waits for them, and re-layouts: 16.8 us -> 5.16 us
    ppermute x5 -> x0, starting transfers between devices: 7.78 us -> none  [along(): return lax.ppermute(x, 'dp', pairs)]
    slice x10 -> x0, local copies, waits for them, and re-layouts: 6.51 us -> none  [the longest x1 4.89 us: body(): whole[:, :4 * cols].reshape(devices, 4, cols, D).transpose(1, 0, 2, 3)]
  transfers between devices with their start and end apart: 8 -> 0, of which waited for: 4 -> 0; matrix products, arithmetic and copies ran while one was open for 6% -> 0% of each run, Pallas kernels for 25% -> 0%
where the time goes in v4:
time: 418 us; the launch traced here: 410 us
  Pallas kernels  370 us (89%)
  other arithmetic  25.6 us (6%)
  local copies, waits for them, and re-layouts  8.76 us (2%)
  matrix products  4.18 us (1%)
    pallas_call x1, Pallas kernels, begin(): pl.pallas_call(functools.partial(begin_kernel, n, cols, blocks, part), ou...  210 us
    pallas_call x1, Pallas kernels, finish(): pl.pallas_call(functools.partial(finish_kernel, n, cols, extra, count //...  160 us
    add x7, other arithmetic, adam_step(): return (weight + update, new_first, new_square)  12.2 us

profile of v4, /device:TPU:0, one launch (start us, length us, event | category | flops | bytes accessed | tf_op | source)
XLA Modules:
  0.0 410.3 jit_solution(8769742414672328563)
XLA Ops:
  0.7 0.7 convert_element_type.82
  1.4 0.2 dynamic_update_slice.9
  1.6 0.7 convert_element_type.83
  2.3 0.2 dynamic_update_slice.10
  2.5 1.0 convert_element_type.81
  3.5 0.7 pad_maximum_fusion.1.in_ref
  4.2 0.7 convert_element_type.88
  4.9 0.7 convert_element_type.89
  5.6 0.1 dynamic_update_slice.11
  5.7 2.6 convert_bitcast_fusion.1
  8.3 0.0 copy-start.20
  8.3 1.6 pad_maximum_fusion.own_ref
  9.9 0.1 copy.76.routes_ref
  10.1 0.0 copy-start.2
  10.1 0.2 eq.47
  10.3 0.3 fusion.15
  10.6 0.2 convert_element_type.98
  10.8 0.7 fusion.26
  11.5 0.1 copy.78
  11.6 0.2 convert_element_type.93
  11.8 0.1 copy.79
  12.0 0.5 fusion
  12.4 0.6 copy.80
  13.1 2.6 convert_bitcast_fusion.slots_ref
  15.7 0.2 fusion.18
  15.9 1.3 fusion.11.marks_ref
  17.2 210.4 %begin.1 = (bf16[4,768,768]{2,1,0:T(8,128)(2,1)}, f32[8,768]{1,0:T(8,128)}, bf16[128,768]{1,0:T(8,128)(2,1)}, bf16[512,768]{1,0:T(8,128)(2,1)}, bf16[512,768]{1,...) custom-call(s32[2]{0:T(128)} %lengths_ref.3, ...), custom_call_target="tpu_custom_call" | custom-call | bytes 1024 | tf_op jit(solution)/shard_map/begin/pallas_call | solution.py:784
  227.6 159.9 %finish.1 = (f32[512,768]{1,0:T(8,128)}, f32[512,768]{1,0:T(8,128)}, f32[112,768]{1,0:T(8,128)}, bf16[768,768]{1,0:T(8,128)(2,1)}, bf16[784,768]{1,0:T(8,128)(2,...) custom-call(s32[2]{0:T(128)} %lengths_ref.3, bf16[512,768]{1,0:T(8,128)(2,1)} %tokens_ref.3, ...), custom_call_target="tpu_custom_call" | custom-call | bytes 1024 | tf_op jit(solution)/shard_map/finish/pallas_call | solution.py:1015
  387.5 0.0 copy-start.1
  387.5 0.0 copy-start.7
  387.6 3.4 select_add_fusion
  390.9 0.1 copy-done.1
  391.0 0.7 copy-done.7
  391.7 0.7 copy-done.8
  392.5 4.4 %multiply_add_fusion = (f32[1,768,768]{2,1,0:T(8,128)}, f32[1,768,768]{2,1,0:T(8,128)}, f32[1,768,768]{2,1,0:T(8,128)}) fusion(f32[1,768,768]{2,1,0:T(8,128)S(1)} %copy-done.1, f32[784,768]{1,0:T(8,128)S(1)} %select_add_fusion, f32[1,768,768]{2,1,0:T(8,128)S(1)} %copy-done.7, f32[1,768,768]{2,1,0:T(8,128)S(1)} %copy-done.8), kind=kLoop, calls=%fused_computation.13 | loop fusion | flops 8847360 | bytes 16515072 | tf_op jit(solution)/shard_map/add | solution.py:38
  396.8 0.0 copy-start.4
  396.9 1.6 slice_bitcast_fusion
  398.4 0.7 multiply_add_fusion.10
  399.1 0.6 multiply_add_fusion.8
  399.7 0.4 copy-done
  400.1 0.7 copy-done.4
  400.8 4.1 %multiply_add_fusion.1 = (f32[1,768,768]{2,1,0:T(8,128)}, f32[1,768,768]{2,1,0:T(8,128)}, f32[1,768,768]{2,1,0:T(8,128)}, f32[768,768]{1,0:T(8,128)}) fusion(f32[1,768,768]{2,1,0:T(8,128)S(1)} %copy-done, f32[1,768,768]{2,1,0:T(8,128)S(1)} %copy-done.4, f32[1,768,768]{2,1,0:T(8,128)S(1)} %copy-done.5, f32[768,768]{1,0:T(8,128)S(1)} %copy-done.6, ...), kind=kLoop, calls=%fused_computation.14 | loop fusion | flops 12386304 | bytes 22413312 | tf_op jit(solution)/shard_map/add | solution.py:38
  405.0 0.0 copy-start.15
  405.1 1.0 multiply_add_fusion.2
  406.2 0.7 multiply_add_fusion.4
  406.9 0.7 multiply_add_fusion.6
  407.6 1.1 copy.107
  408.7 1.1 copy.108
  (61 shorter events, 0.2 us)
Async XLA Ops:
  8.3 1.6 copy-start.20
  9.9 3.1 copy-start.3
  10.1 5.6 %copy-start.2 = (s32[512,2]{1,0:T(8,128)}, s32[512,2]{1,0:T(8,128)S(1)}, u32[]{:S(2)}) copy-start(s32[512,2]{1,0:T(8,128)S(1)} %copy.76.routes_ref) | copy-start | bytes 12292
  12.0 3.7 copy-start.19
  387.5 3.5 copy-start.1
  387.5 4.2 %copy-start.7 = (f32[1,768,768]{2,1,0:T(8,128)S(1)}, f32[1,768,768]{2,1,0:T(8,128)}, u32[]{:S(2)}) copy-start(f32[1,768,768]{2,1,0:T(8,128)} %param.43) | copy-start | bytes 7077892
  387.5 4.9 %copy-start.8 = (f32[1,768,768]{2,1,0:T(8,128)S(1)}, f32[1,768,768]{2,1,0:T(8,128)}, u32[]{:S(2)}) copy-start(f32[1,768,768]{2,1,0:T(8,128)} %param.50) | copy-start | bytes 7077892
  392.4 6.0 %copy-start.26 = (f32[1,192]{1,0:T(1,128)S(1)}, f32[1,192]{1,0:T(1,128)}, u32[]{:S(2)}) copy-start(f32[1,192]{1,0:T(1,128)} %param.37) | copy-start | bytes 2308
  392.4 6.0 %copy-start.31 = (f32[1,192]{1,0:T(1,128)S(1)}, f32[1,192]{1,0:T(1,128)}, u32[]{:S(2)}) copy-start(f32[1,192]{1,0:T(1,128)} %param.44) | copy-start | bytes 2308
  392.4 6.0 %copy-start.32 = (f32[1,192]{1,0:T(1,128)S(1)}, f32[1,192]{1,0:T(1,128)}, u32[]{:S(2)}) copy-start(f32[1,192]{1,0:T(1,128)} %param.51) | copy-start | bytes 2308
  392.4 7.3 %copy-start.5 = (f32[1,768,768]{2,1,0:T(8,128)S(1)}, f32[1,768,768]{2,1,0:T(8,128)}, u32[]{:S(2)}) copy-start(f32[1,768,768]{2,1,0:T(8,128)} %param.48) | copy-start | bytes 7077892
  392.4 7.3 %copy-start.6 = (f32[768,768]{1,0:T(8,128)S(1)}, f32[768,768]{1,0:T(8,128)}, u32[]{:S(2)}) copy-start(f32[768,768]{1,0:T(8,128)} %get-tuple-element.96) | copy-start | bytes 7077892
  392.4 7.3 %copy-start.11 = (bf16[768,768]{1,0:T(8,128)(2,1)S(1)}, bf16[768,768]{1,0:T(8,128)(2,1)}, u32[]{:S(2)}) copy-start(bf16[768,768]{1,0:T(8,128)(2,1)} %get-tuple-element.97) | copy-start | bytes 3538948
  392.4 7.3 %copy-start.12 = (bf16[768,768]{1,0:T(8,128)(2,1)S(1)}, bf16[768,768]{1,0:T(8,128)(2,1)}, u32[]{:S(2)}) copy-start(bf16[768,768]{1,0:T(8,128)(2,1)} %get-tuple-element.98) | copy-start | bytes 3538948
  392.5 7.3 %copy-start.13 = (bf16[768,768]{1,0:T(8,128)(2,1)S(1)}, bf16[768,768]{1,0:T(8,128)(2,1)}, u32[]{:S(2)}) copy-start(bf16[768,768]{1,0:T(8,128)(2,1)} %get-tuple-element.99) | copy-start | bytes 3538948
  396.8 2.3 copy-start.23
  396.8 2.3 copy-start.29
  396.8 2.3 copy-start.30
  396.8 3.3 copy-start
  396.8 4.0 copy-start.4
  400.8 4.2 %copy-start.16 = (f32[112,768]{1,0:T(8,128)S(1)}, f32[112,768]{1,0:T(8,128)}, u32[]{:S(2)}) copy-start(f32[112,768]{1,0:T(8,128)} %get-tuple-element.95) | copy-start | bytes 1032196
  400.8 4.2 %copy-start.14 = (f32[4,24,768]{2,1,0:T(8,128)S(1)}, f32[4,24,768]{2,1,0:T(8,128)}, u32[]{:S(2)}) copy-start(f32[4,24,768]{2,1,0:T(8,128)} %param.31) | copy-start | bytes 884740
  400.8 4.2 %copy-start.17 = (f32[4,24,768]{2,1,0:T(8,128)S(1)}, f32[4,24,768]{2,1,0:T(8,128)}, u32[]{:S(2)}) copy-start(f32[4,24,768]{2,1,0:T(8,128)} %param.38) | copy-start | bytes 884740
  400.8 4.2 %copy-start.18 = (f32[4,24,768]{2,1,0:T(8,128)S(1)}, f32[4,24,768]{2,1,0:T(8,128)}, u32[]{:S(2)}) copy-start(f32[4,24,768]{2,1,0:T(8,128)} %param.45) | copy-start | bytes 884740
  404.9 1.2 copy-start.21
  405.0 1.2 copy-start.24
  405.0 1.2 copy-start.25
  405.0 1.9 copy-start.22
  405.0 1.9 copy-start.27
  405.0 1.9 copy-start.28
  405.0 2.6 copy-start.10
  405.0 3.7 copy-start.15
  405.1 3.6 copy-start.9

commit v5 on v4

--- a/solution.py
+++ b/solution.py
@@ -551,12 +551,17 @@
 
 def begin_kernel(
     n, cols, seqs, part, lengths_ref, in_ref, own_ref, slots_ref, marks_ref, tokens_ref, routes_ref, places_ref,
-    weights_ref, vector_ref, router_ref, normed_ref, q_ref, k_ref, v_ref, context_ref, lse_ref, resid_ref, normed_two_ref,
-    gates_ref, out_ref, back_ref, mine_up, mine_down, near_up, near_down, middle_up, middle_down, far_up, far_down,
-    near_up_in, near_down_in,
+    *refs,
+):
+    kept_out, refs = refs[:12], refs[12:]
+    here, refs = refs[-12:], refs[:-12]
+    weights_ref, vector_ref, router_ref, *attention_refs = here
+    (
+        out_ref, back_ref, mine_up, mine_down, near_up, near_down, middle_up, middle_down, far_up, far_down,
+    near_up_in, near_down_in, middle_in,
     pool, acc, second_ref, third_ref, fourth_ref, going, x_in, dout_in, marks_in, out_acc, back_acc, bias_acc, tail_ref,
     local_sem, part_s, part_r, slot_s, slot_r, mark_s, mark_r, x_s, x_r, near_s, near_r, store_s, *sems,
-):
+    ) = refs
     side, z, y, x, core = where_am_i()
     mine = lax.axis_index("expert")
     experts, _, capacity, _ = slots_ref.shape
@@ -592,7 +597,12 @@
     own_across = hop(1, own_ref, third_ref, across)
     third_on = hop(2, third_ref, third_ref, outward)
     second_across = hop(3, second_ref, fourth_ref, across)
-    fourth_on = hop(4, fourth_ref, fourth_ref, outward)
+    cut = part // 3 * 2
+    spans = [(0, cut), (part, cut), (2 * part, BIAS_ROWS), (cut, part - cut), (part + cut, part - cut)]
+    fourth_on = [
+        hop(4 + i, fourth_ref.at[pl.ds(at, length), :], fourth_ref.at[pl.ds(at, length), :], outward)
+        for i, (at, length) in enumerate(spans)
+    ]
 
     def weights_on():
         beside.start()
@@ -632,14 +642,16 @@
     late = []
     for s in range(seqs):
         sequence_forward(
-            s, lengths_ref, tokens_ref, weights_ref, vector_ref, router_ref, routes_ref, places_ref,
-            normed_ref, q_ref, k_ref, v_ref, context_ref, lse_ref, resid_ref, normed_two_ref, gates_ref, going,
+            s, lengths_ref, tokens_ref, weights_ref, vector_ref, router_ref, routes_ref, places_ref, *attention_refs, going
         )
         dst = functools.partial(sender, x_in, b=s, blocks=1)
         late.append((functools.partial(lambda e, s: going.at[e, s], s=s), dst, x_s.at[s], x_r.at[s]))
         exchange_all(late[-1:], more)
         stays.append(pltpu.make_async_copy(going.at[mine, s], dst(mine), local_sem.at[3 + s]))
         stays[-1].start()
+    stores = [pltpu.make_async_copy(src, dst, store_s.at[11 + k]) for k, (src, dst) in enumerate(zip(here, kept_out))]
+    for copy in stores:
+        copy.start()
     beside.wait()
 
     @pl.when(inner)
@@ -658,17 +670,21 @@
     up_acc, down_acc = acc.at[0], acc.at[1]
     tiles = slots // TILE
     down_bias = jnp.zeros((1, D), f32)
-    stores = []
     outs = [(mine_up, mine_down), (near_up, near_down), (middle_up, middle_down), (far_up, far_down)]
     near_in = (near_up_in, near_down_in)
     bias_acc[...] = jnp.zeros_like(bias_acc)
-    for p, w_ref in enumerate((own_ref, second_ref, third_ref, fourth_ref)):
-        if p == 1:
+    pieces = [(1, 0, part), (0, 0, part), (2, 0, part), (3, 0, cut), (3, cut, part)]
+    for p, low, high in pieces:
+        begins = p == 1
+        w_ref = (own_ref, second_ref, third_ref, fourth_ref)[p]
+        last = p == 3 and high == part
+        if p == 0:
 
             @pl.when(inner)
             def _():
                 second_across.wait()
-                fourth_on.start()
+                for copy in fourth_on:
+                    copy.start()
 
         if p == 2:
 
@@ -680,17 +696,23 @@
 
             @pl.when(outer)
             def _():
-                fourth_on.wait_recv()
-
-        down_bias = down_bias + w_ref[2 * part :, :].astype(f32)[1:2, :]
-        up_acc[...] = jnp.zeros_like(up_acc)
-        down_acc[...] = jnp.zeros_like(down_acc)
-        bias_acc[0:1, :] = jnp.zeros((1, D), f32)
+                for copy in fourth_on[3:] if low else fourth_on[:3]:
+                    copy.wait_recv()
+
+        if low == 0:
+            up_acc[...] = jnp.zeros_like(up_acc)
+            down_acc[...] = jnp.zeros_like(down_acc)
+            bias_acc[0:1, :] = jnp.zeros((1, D), f32)
+
+        biases = w_ref[2 * part :, :].astype(f32)
+        up_bias = biases[0:1, low:high]
+        if low == 0:
+            down_bias = down_bias + biases[1:2, :]
 
         def tile(t, carry):
             rows = pl.ds(pl.multiple_of(t * TILE, TILE), TILE)
             x = x_in[rows, :]
-            if p == 0:
+            if begins:
                 logits = dot(x, router_ref[...], NT)
                 signs = jnp.where(lanes_like(logits) == mine, 1.0, -marks_in[rows, :].astype(f32))
                 margin = jnp.sum(logits * signs, axis=-1, keepdims=True)
@@ -699,15 +721,16 @@
                 bias_acc[1:2, :] += column_sum(dout.astype(f32))
             else:
                 dout = dout_in[rows, :]
-            up_bias = w_ref[2 * part :, :].astype(f32)[0:1, :part]
-            hidden, grad_pre, out, back = expert_tile(x, dout, w_ref[:part, :], up_bias, w_ref[part : 2 * part, :])
-            down_acc[...] += dot(hidden, dout, TN)
-            up_acc[...] += dot(grad_pre, x, TN)
-            bias_acc[0:1, :] += column_sum(grad_pre.astype(f32))
-            if p == 0:
+            hidden, grad_pre, out, back = expert_tile(
+                x, dout, w_ref[low:high, :], up_bias, w_ref[part + low : part + high, :]
+            )
+            down_acc[low:high, :] += dot(hidden, dout, TN)
+            up_acc[low:high, :] += dot(grad_pre, x, TN)
+            bias_acc[0:1, low:high] += column_sum(grad_pre.astype(f32))
+            if begins:
                 out_acc[rows, :] = out
                 back_acc[rows, :] = back
-            elif p < 3:
+            elif not last:
                 out_acc[rows, :] += out
                 back_acc[rows, :] += back
             else:
@@ -716,8 +739,10 @@
             return carry
 
         lax.fori_loop(0, tiles, tile, 0)
+        if high < part:
+            continue
         tail = bias_rows(bias_acc[0:1, :], bias_acc[1:2, :])
-        base = stage_rows if p > 1 else 0
+        base = stage_rows if p == 2 else 0
         if p == 0:
             tail_ref[...] = tail
             now = [
@@ -731,9 +756,15 @@
                 copy.wait()
         else:
             if p == 3:
-                for copy in stores[2:]:
+                for copy in stores[12:14]:
                     copy.wait()
-                del stores[2:]
+                del stores[12:14]
+
+                @pl.when(outer)
+                def _():
+                    for copy in nears[:2]:
+                        copy.wait_send()
+
             pool[base : base + part, :] = up_acc[...].astype(b16)
             pool[base + part : base + 2 * part, :] = down_acc[...].astype(b16)
             pool[base + 2 * part : base + stage_rows, :] = tail.astype(b16)
@@ -749,6 +780,14 @@
                     for copy in nears:
                         copy.start()
 
+            if p == 2:
+                middle = remote(halves_of[0], middle_in, near_s.at[2], near_r.at[2], inward)
+                nears.append(middle)
+
+                @pl.when(outer)
+                def _():
+                    middle.start()
+
     for src, dst, k in ((x_in, out_ref, 9), (dout_in, back_ref, 10)):
         stores.append(pltpu.make_async_copy(src, dst, store_s.at[k]))
         stores[-1].start()
@@ -757,15 +796,14 @@
 
     @pl.when(inner)
     def _():
-        third_on.wait_send()
-        fourth_on.wait_send()
+        for copy in [third_on, *fourth_on]:
+            copy.wait_send()
         for copy in nears:
             copy.wait_recv()
 
     @pl.when(outer)
     def _():
-        for copy in nears:
-            copy.wait_send()
+        nears[2].wait_send()
 
 
 def begin(n, side, cols, lengths, packed, own, slots, marks, tokens, routes, places):
@@ -777,6 +815,12 @@
     dma = pltpu.SemaphoreType.DMA
     vmem, hbm = pl.BlockSpec(memory_space=pltpu.VMEM), pl.BlockSpec(memory_space=pl.ANY)
     *kept, going = kept_shapes(count, experts, capacity)
+    held = [
+        jax.ShapeDtypeStruct((4, D, D), b16),
+        jax.ShapeDtypeStruct((8, D), f32),
+        jax.ShapeDtypeStruct((128, D), b16),
+        *kept,
+    ]
 
     def halves_in(dtype):
         return [jax.ShapeDtypeStruct((part, D), dtype), jax.ShapeDtypeStruct((part + BIAS_ROWS, D), dtype)]
@@ -784,16 +828,14 @@
     return pl.pallas_call(
         functools.partial(begin_kernel, n, cols, blocks, part),
         out_shape=[
-            jax.ShapeDtypeStruct((4, D, D), b16),
-            jax.ShapeDtypeStruct((8, D), f32),
-            jax.ShapeDtypeStruct((128, D), b16),
-            *kept,
+            *held,
             *[jax.ShapeDtypeStruct((total, D), b16)] * 2,
             *halves_in(f32),
             *halves_in(b16) * 4,
+            halves_in(b16)[0],
         ],
         in_specs=[pl.BlockSpec(memory_space=pltpu.SMEM), vmem, vmem, hbm, hbm, vmem, vmem, vmem],
-        out_specs=[*[vmem] * 12, *[hbm] * 12],
+        out_specs=[hbm] * 25,
         scratch_shapes=[
             pltpu.VMEM((max(devices * packed.shape[0], 2 * own.shape[0]), D), b16),
             pltpu.VMEM((2, D, D), f32),
@@ -805,12 +847,13 @@
             pltpu.VMEM((8, D), f32),
             pltpu.VMEM((BIAS_ROWS, D), f32),
             dma((3 + blocks,)),
-            *[dma((5,))] * 2,
+            *[dma((9,))] * 2,
             *[dma((experts,))] * 4,
             *[dma((blocks, experts))] * 2,
-            *[dma((2,))] * 2,
-            dma((11,)),
+            *[dma((3,))] * 2,
+            dma((23,)),
             *spread_sems(n, side),
+            *[pltpu.VMEM(v.shape, v.dtype) for v in held],
         ],
         compiler_params=pltpu.CompilerParams(collective_id=0, has_side_effects=True, vmem_limit_bytes=63 << 20),
         cost_estimate=CHEAP,
@@ -823,16 +866,20 @@
 
 
 def finish_kernel(
-    n, cols, extra, seqs,
-    lengths_ref, tokens_ref, grad_ref, weights_ref, vector_ref, router_ref, routes_ref, places_ref,
-    normed_ref, q_ref, k_ref, v_ref, context_ref, lse_ref, resid_ref, normed_two_ref, gates_ref, outs_ref, backs_ref,
-    near_up, near_down, middle_up, middle_down, far_up, far_down,
-    output_ref, input_grad_ref, dense_ref, middle_up_in, middle_down_in, end_up_in, end_down_in,
-    outs_in, backs_in, weights_acc, vector_acc, router_acc, dq_ref, dk_ref, dv_ref,
-    far_up_buf, far_down_buf, middle_up_buf, middle_down_buf, on_up_buf, on_down_buf, load_up, load_down,
-    parts, stage, c_buf, b_buf, a_buf, z_buf,
-    own_s, out_s, out_r, back_s, back_r, chain_s, chain_r, load_s, c_s, c_r, b_s, b_r, a_s, a_r, z_s, z_r,
+    n, cols, extra, seqs, lengths_ref, vector_ref, router_ref, routes_ref, places_ref, *refs,
 ):
+    brought, refs = refs[:12], refs[12:]
+    here, refs = refs[-12:], refs[:-12]
+    tokens_ref, grad_ref, weights_ref, *attention_refs = here
+    (
+        outs_ref, backs_ref,
+        near_up, near_down, middle_up, middle_down, far_up, far_down, middle_came,
+        output_ref, input_grad_ref, dense_ref, middle_up_in, middle_down_in, end_up_in, end_down_in,
+        outs_in, backs_in, weights_acc, vector_acc, router_acc, dq_ref, dk_ref, dv_ref,
+        far_up_buf, far_down_buf, middle_up_buf, middle_down_buf, on_up_buf, on_down_buf, load_up, load_down,
+        parts, stage, c_buf, b_buf, a_buf, z_buf,
+        own_s, out_s, out_r, back_s, back_r, chain_s, chain_r, load_s, came_s, c_s, c_r, b_s, b_r, a_s, a_r, z_s, z_r,
+    ) = refs
     inside = cols % 8 == 0
     side, z, y, x, core = where_am_i()
     mine = lax.axis_index("expert")
@@ -848,16 +895,19 @@
         copy.start()
         sent.append(copy)
 
-    for k in range(1, experts):
-        to = (mine + k) % experts
-        send(outs_ref.at[to], outs_in.at[mine], out_s.at[k], out_r.at[k], plane[k - 1])
-    for k in range(1, experts):
-        to = (mine + k) % experts
-        send(backs_ref.at[to], backs_in.at[mine], back_s.at[k], back_r.at[k], plane[k - 1])
+    def by_sequence(s):
+        return [
+            (lambda e: outs_ref.at[e, s], lambda e: outs_in.at[e, s], out_s.at[s], out_r.at[s]),
+            (lambda e: backs_ref.at[e, s], lambda e: backs_in.at[e, s], back_s.at[s], back_r.at[s]),
+        ]
+
+    for s in range(seqs):
+        exchange_all(by_sequence(s), sent)
     own = [
         pltpu.make_async_copy(outs_ref.at[mine], outs_in.at[mine], own_s.at[0]),
         pltpu.make_async_copy(backs_ref.at[mine], backs_in.at[mine], own_s.at[1]),
     ]
+    own += [pltpu.make_async_copy(src, dst, own_s.at[2 + k]) for k, (src, dst) in enumerate(zip(brought, here))]
     for copy in own:
         copy.start()
 
@@ -872,65 +922,77 @@
     far_buf, middle_buf, on_buf = (far_up_buf, far_down_buf), (middle_up_buf, middle_down_buf), (on_up_buf, on_down_buf)
     loads = (load_up, load_down)
 
-    def hop(kind, half, src, dst, peer):
-        return remote(src, dst, chain_s.at[kind, half], chain_r.at[kind, half], peer)
-
-    from_ends = [(FAR, far, far_buf), (MIDDLE, middle, middle_buf)]
+    whole = [(h, 0, far[h].shape[0]) for h in range(2)]
+    split = far[0].shape[0] // 32 * 16
+    quarters = [(h, at, split if at == 0 else far[h].shape[0] - split) for h in range(2) for at in (0, split)]
+
+    def hop(kind, k, piece, src, dst, peer):
+        h, at, length = piece
+        rows = pl.ds(at, length)
+        return remote(src[h].at[rows, :], dst[h].at[rows, :], chain_s.at[kind, k], chain_r.at[kind, k], peer)
+
+    from_ends = [(FAR, whole, far, far_buf), (MIDDLE, quarters, middle, middle_buf)]
 
     @pl.when(outer)
     def _():
-        for kind, src, dst in from_ends:
-            for half in range(2):
-                hop(kind, half, src[half], dst[half], inward).start()
-
-    def chain_step(kind, half, buf, term, next_kind, target, peer):
+        for kind, cuts, src, dst in from_ends:
+            for k, piece_ in enumerate(cuts):
+                if kind == FAR or piece_[0]:
+                    hop(kind, k, piece_, src, dst, inward).start()
+
+    def chain_step(kind, k, piece_, buf, term, next_kind, target, peer):
         @pl.when(inner)
         def _():
-            load = pltpu.make_async_copy(term[half], loads[half], load_s)
+            h, at, length = piece_
+            rows = pl.ds(at, length)
+            load = pltpu.make_async_copy(term[h].at[rows, :], loads[h].at[rows, :], load_s)
             load.start()
-            hop(kind, half, buf[half], buf[half], across).wait_recv()
+            if kind == MIDDLE and h == 0:
+                came = pltpu.make_async_copy(middle_came.at[rows, :], buf[h].at[rows, :], came_s)
+                came.start()
+                came.wait()
+            else:
+                hop(kind, k, piece_, buf, buf, across).wait_recv()
             load.wait()
-            buf[half][...] = (buf[half][...].astype(f32) + loads[half][...].astype(f32)).astype(b16)
-            hop(next_kind, half, buf[half], target[half], peer).start()
-
-    def step_far(half):
-        chain_step(FAR, half, far_buf, far, FAR_ON, on_buf, across)
-
-    def step_on(half):
-        chain_step(FAR_ON, half, on_buf, near, FAR_LAST, end_in, outward)
-
-    def step_middle(half):
-        chain_step(MIDDLE, half, middle_buf, middle, MIDDLE_ON, middle_in, across)
+            buf[h][rows, :] = (buf[h][rows, :].astype(f32) + loads[h][rows, :].astype(f32)).astype(b16)
+            hop(next_kind, k, piece_, buf, target, peer).start()
+
+    def step_far(k):
+        chain_step(FAR, k, whole[k], far_buf, far, FAR_ON, on_buf, across)
+
+    def step_on(k):
+        chain_step(FAR_ON, k, whole[k], on_buf, near, FAR_LAST, end_in, outward)
+
+    def step_middle(k):
+        chain_step(MIDDLE, k, quarters[k], middle_buf, middle, MIDDLE_ON, middle_in, across)
 
     weights_acc[...] = jnp.zeros_like(weights_acc)
     vector_acc[...] = jnp.zeros_like(vector_acc)
     router_acc[...] = jnp.zeros_like(router_acc)
+    step_middle(0)
+    step_middle(1)
     step_far(0)
-    step_far(1)
-    step_on(0)
     for copy in own:
         copy.wait()
-    for k in range(1, experts):
-        block = outs_in.at[(mine - k + experts) % experts]
-        remote(block, block, out_s.at[k], out_r.at[k], sibling).wait_recv()
-        block = backs_in.at[(mine - k + experts) % experts]
-        remote(block, block, back_s.at[k], back_r.at[k], sibling).wait_recv()
     for s in range(seqs):
+        wait_all(by_sequence(s))
         sequence_backward(
             s, lengths_ref, tokens_ref, grad_ref, weights_ref, vector_ref, router_ref, routes_ref, places_ref,
-            normed_ref, q_ref, k_ref, v_ref, context_ref, lse_ref, resid_ref, normed_two_ref, gates_ref, outs_in, backs_in,
+            *attention_refs, outs_in, backs_in,
             output_ref, input_grad_ref, weights_acc, vector_acc, router_acc, dq_ref, dk_ref, dv_ref,
         )
         if s == 0:
-            step_on(1)
-            step_middle(0)
+            step_far(1)
+            step_on(0)
+    step_on(1)
 
     small = jnp.concatenate([vector_acc[...], router_acc[: extra - 8, :]], axis=0).astype(b16)
     if not inside:
         dense_ref[:extra, :] = jnp.concatenate([vector_acc[...], router_acc[: extra - 8, :]], axis=0)
         for k in range(4):
             dense_ref[extra + k * D : extra + (k + 1) * D, :] = weights_acc[k]
-        step_middle(1)
+        step_middle(2)
+        step_middle(3)
     for core_ in range(2 if inside else 0):
         for y_ in range(side):
             for x_ in range(side):
@@ -957,10 +1019,10 @@
         if kb:
             stage[place] = (parts[mine_].astype(f32) + c_buf[place].astype(f32)).astype(b16)
             send(stage.at[place], b_buf.at[place], b_s.at[place], b_r.at[place], second[kb - 1])
-            if ka == 0:
-                step_middle(1)
         else:
             total = parts[mine_].astype(f32) + c_buf[place].astype(f32)
+            if ka:
+                step_middle(2)
             for k in range(1, side):
                 slot = ka * side + k
                 remote(b_buf.at[slot], b_buf.at[slot], b_s.at[slot], b_r.at[slot], sibling).wait_recv()
@@ -969,6 +1031,7 @@
                 stage[place] = total.astype(b16)
                 send(stage.at[place], a_buf.at[ka], a_s.at[ka], a_r.at[ka], first[ka - 1])
             else:
+                step_middle(3)
                 for k in range(1, side):
                     remote(a_buf.at[k], a_buf.at[k], a_s.at[k], a_r.at[k], sibling).wait_recv()
                     total = total + a_buf[k].astype(f32)
@@ -986,22 +1049,25 @@
 
     @pl.when(outer)
     def _():
-        for half in range(2):
-            for kind, src, dst in from_ends:
-                hop(kind, half, src[half], dst[half], inward).wait_send()
-            hop(FAR_LAST, half, end_in[half], end_in[half], inward).wait_recv()
+        for kind, cuts, src, dst in from_ends:
+            for k, piece_ in enumerate(cuts):
+                if kind == FAR or piece_[0]:
+                    hop(kind, k, piece_, src, dst, inward).wait_send()
+        for k, piece_ in enumerate(whole):
+            hop(FAR_LAST, k, piece_, end_in, end_in, inward).wait_recv()
 
     @pl.when(inner)
     def _():
-        for half in range(2):
-            hop(FAR_ON, half, far_buf[half], on_buf[half], across).wait_send()
-            hop(FAR_LAST, half, on_buf[half], end_in[half], outward).wait_send()
-            hop(MIDDLE_ON, half, middle_buf[half], middle_in[half], across).wait_send()
-            hop(MIDDLE_ON, half, middle_in[half], middle_in[half], across).wait_recv()
-
-
-def finish(n, side, cols, extra, lengths, rows_in, kept, outs, backs, grads):
+        for k, piece_ in enumerate(whole):
+            hop(FAR_ON, k, piece_, far_buf, on_buf, across).wait_send()
+            hop(FAR_LAST, k, piece_, on_buf, end_in, outward).wait_send()
+        for k, piece_ in enumerate(quarters):
+            hop(MIDDLE_ON, k, piece_, middle_buf, middle_in, across).wait()
+
+
+def finish(n, side, cols, extra, lengths, small, rows_in, kept, outs, backs, grads):
     count = rows_in[0].shape[0]
+    held = (*rows_in, *kept)
     slots = outs.shape
     vmem = pl.BlockSpec(memory_space=pltpu.VMEM)
     hbm = pl.BlockSpec(memory_space=pl.ANY)
@@ -1016,10 +1082,8 @@
         functools.partial(finish_kernel, n, cols, extra, count // LEN),
         in_specs=[
             pl.BlockSpec(memory_space=pltpu.SMEM),
-            *[vmem] * (len(rows_in) + len(kept)),
-            hbm,
-            hbm,
-            *[hbm] * len(grads),
+            *[vmem] * len(small),
+            *[hbm] * (len(held) + 2 + len(grads)),
         ],
         out_specs=[vmem, vmem, vmem, *[hbm] * 4],
         out_shape=[
@@ -1042,18 +1106,20 @@
             pltpu.VMEM((area, *block), b16),
             pltpu.VMEM((side, *block), b16),
             pltpu.VMEM(block, b16),
-            dma((2,)),
-            *[dma((slots[0],))] * 4,
-            *[dma((KINDS, 2))] * 2,
+            dma((2 + len(held),)),
+            *[dma((slots[1], slots[0]))] * 4,
+            *[dma((KINDS, 4))] * 2,
+            dma,
             dma,
             *[dma((area,))] * 4,
             *[dma((side,))] * 2,
             *[dma((n,))] * 2,
+            *[pltpu.VMEM(v.shape, v.dtype) for v in held],
         ],
         compiler_params=pltpu.CompilerParams(collective_id=1, has_side_effects=True, vmem_limit_bytes=63 << 20),
         cost_estimate=CHEAP,
         name="finish",
-    )(lengths, *rows_in, *kept, outs, backs, *grads)
+    )(lengths, *small, *held, outs, backs, *grads)
 
 
 def pack_expert(up, down, up_bias, down_bias, start, dtype):
@@ -1120,7 +1186,7 @@
         weights_b, vector_all, router_all, *got = begin(
             n_dp, side, cols, lengths, packed, own, by_slot(out_grad), by_slot(marked), tokens, routes, places
         )
-        kept, out_b, back_b, grads, near_in = got[:9], got[9], got[10], got[11:19], got[19:]
+        kept, out_b, back_b, grads, near_in, middle_in = got[:9], got[9], got[10], got[11:19], got[19:21], got[21]
     else:
         whole, second, third_inner, grad_slots, marks = gather_dense(
             packed, own, by_slot(out_grad), by_slot(marked), n_dp, side
@@ -1160,12 +1226,13 @@
             grads += [grad_up, grad_down]
         out_b, back_b = sums
         near_in = [along(g, (0, 1), (3, 2)) for g in grads[2:4]]
+        middle_in = along(grads[4], (0, 1), (3, 2))
 
     slots_shape = (experts, blocks, capacity, D)
     output, input_grad, dense, *came = finish(
         n_dp, side, cols, small_rows, lengths,
-        (tokens, out_grad, weights_b, vector_all, router_all, routes, positions.reshape(count, 2)),
-        kept, out_b.reshape(slots_shape), back_b.reshape(slots_shape), grads[2:],
+        (vector_all, router_all, routes, positions.reshape(count, 2)), (tokens, out_grad, weights_b),
+        kept, out_b.reshape(slots_shape), back_b.reshape(slots_shape), [*grads[2:], middle_in],
     )
     totals = [
         grads[i]

time: 418 us -> 405 us (0.969)
  the two profiles are of different devices: /device:TPU:0 before, /device:TPU:24 now
where the time goes in v5:
time: 405 us; the launch traced here: 397 us
  Pallas kernels  356 us (88%)
  other arithmetic  25.5 us (6%)
  local copies, waits for them, and re-layouts  9.36 us (2%)
  matrix products  4.22 us (1%)
    pallas_call x1, Pallas kernels, begin(): pl.pallas_call(functools.partial(begin_kernel, n, cols, blocks, part), ou...  206 us
    pallas_call x1, Pallas kernels, finish(): pl.pallas_call(functools.partial(finish_kernel, n, cols, extra, count //...  150 us
    add x7, other arithmetic, adam_step(): return (weight + update, new_first, new_square)  12.2 us

profile of v5, /device:TPU:24, one launch (start us, length us, event | category | flops | bytes accessed | tf_op | source)
XLA Modules:
  0.0 396.8 jit_solution(7976709458081221635)
XLA Ops:
  0.7 0.7 convert_element_type.82
  1.4 0.5 dynamic_update_slice.9
  1.9 0.7 convert_element_type.83
  2.6 0.4 dynamic_update_slice.10
  3.0 1.0 convert_element_type.81
  4.0 0.7 pad_maximum_fusion.1.in_ref
  4.7 0.7 convert_element_type.88
  5.4 0.7 convert_element_type.89
  6.1 0.2 dynamic_update_slice.11
  6.3 2.6 convert_bitcast_fusion.1
  8.9 1.5 pad_maximum_fusion.own_ref
  10.5 0.1 copy.76.routes_ref
  10.7 0.2 eq.47
  10.8 0.3 fusion.15
  11.1 0.2 convert_element_type.98
  11.3 0.7 fusion.26
  12.1 0.1 copy.78
  12.2 0.2 convert_element_type.93
  12.4 0.1 copy.79
  12.5 0.5 fusion
  13.0 0.6 copy.80
  13.6 2.7 convert_bitcast_fusion.slots_ref
  16.3 0.2 fusion.18
  16.5 1.3 fusion.11.marks_ref
  17.8 206.5 %begin.1 = (bf16[4,768,768]{2,1,0:T(8,128)(2,1)}, f32[8,768]{1,0:T(8,128)}, bf16[128,768]{1,0:T(8,128)(2,1)}, bf16[512,768]{1,0:T(8,128)(2,1)}, bf16[512,768]{1,...) custom-call(s32[2]{0:T(128)} %lengths_ref.3, ...), custom_call_target="tpu_custom_call" | custom-call | bytes 1024 | tf_op jit(solution)/shard_map/begin/pallas_call | solution.py:828
  224.3 149.7 %finish.1 = (f32[512,768]{1,0:T(8,128)}, f32[512,768]{1,0:T(8,128)}, f32[112,768]{1,0:T(8,128)}, bf16[768,768]{1,0:T(8,128)(2,1)}, bf16[784,768]{1,0:T(8,128)(2,...) custom-call(s32[2]{0:T(128)} %lengths_ref.3, f32[8,768]{1,0:T(8,128)} %get-tuple-element.74.vector_ref, ...), custom_call_target="tpu_custom_call" | custom-call | bytes 1024 | tf_op jit(solution)/shard_map/finish/pallas_call | solution.py:1081
  374.1 0.0 copy-start.7
  374.1 0.0 copy-start.8
  374.1 3.4 select_add_fusion
  377.4 0.1 copy-done.1
  377.5 0.7 copy-done.7
  378.2 0.7 copy-done.8
  379.0 4.4 %multiply_add_fusion = (f32[1,768,768]{2,1,0:T(8,128)}, f32[1,768,768]{2,1,0:T(8,128)}, f32[1,768,768]{2,1,0:T(8,128)}) fusion(f32[1,768,768]{2,1,0:T(8,128)S(1)} %copy-done.1, f32[784,768]{1,0:T(8,128)S(1)} %select_add_fusion, f32[1,768,768]{2,1,0:T(8,128)S(1)} %copy-done.7, f32[1,768,768]{2,1,0:T(8,128)S(1)} %copy-done.8), kind=kLoop, calls=%fused_computation.13 | loop fusion | flops 8847360 | bytes 16515072 | tf_op jit(solution)/shard_map/add | solution.py:38
  383.4 0.0 copy-start.4
  383.4 1.6 slice_bitcast_fusion
  385.0 0.7 multiply_add_fusion.10
  385.6 0.6 multiply_add_fusion.8
  386.3 0.4 copy-done
  386.7 0.7 copy-done.4
  387.4 4.1 %multiply_add_fusion.1 = (f32[1,768,768]{2,1,0:T(8,128)}, f32[1,768,768]{2,1,0:T(8,128)}, f32[1,768,768]{2,1,0:T(8,128)}, f32[768,768]{1,0:T(8,128)}) fusion(f32[1,768,768]{2,1,0:T(8,128)S(1)} %copy-done, f32[1,768,768]{2,1,0:T(8,128)S(1)} %copy-done.4, f32[1,768,768]{2,1,0:T(8,128)S(1)} %copy-done.5, f32[768,768]{1,0:T(8,128)S(1)} %copy-done.6, ...), kind=kLoop, calls=%fused_computation.14 | loop fusion | flops 12386304 | bytes 22413312 | tf_op jit(solution)/shard_map/add | solution.py:38
  391.5 0.0 copy-start.27
  391.5 0.0 copy-start.28
  391.6 0.0 copy-start.15
  391.6 1.0 multiply_add_fusion.2
  392.7 0.7 multiply_add_fusion.4
  393.4 0.7 multiply_add_fusion.6
  394.1 1.1 copy.107
  395.3 1.1 copy.108
  (61 shorter events, 0.2 us)
Async XLA Ops:
  8.9 1.6 copy-start.20
  10.5 3.1 copy-start.3
  10.6 5.6 %copy-start.2 = (s32[512,2]{1,0:T(8,128)}, s32[512,2]{1,0:T(8,128)S(1)}, u32[]{:S(2)}) copy-start(s32[512,2]{1,0:T(8,128)S(1)} %copy.76.routes_ref) | copy-start | bytes 12292
  12.5 3.8 copy-start.19
  374.1 3.5 copy-start.1
  374.1 4.2 %copy-start.7 = (f32[1,768,768]{2,1,0:T(8,128)S(1)}, f32[1,768,768]{2,1,0:T(8,128)}, u32[]{:S(2)}) copy-start(f32[1,768,768]{2,1,0:T(8,128)} %param.43) | copy-start | bytes 7077892
  374.1 4.9 %copy-start.8 = (f32[1,768,768]{2,1,0:T(8,128)S(1)}, f32[1,768,768]{2,1,0:T(8,128)}, u32[]{:S(2)}) copy-start(f32[1,768,768]{2,1,0:T(8,128)} %param.50) | copy-start | bytes 7077892
  379.0 6.0 %copy-start.26 = (f32[1,192]{1,0:T(1,128)S(1)}, f32[1,192]{1,0:T(1,128)}, u32[]{:S(2)}) copy-start(f32[1,192]{1,0:T(1,128)} %param.37) | copy-start | bytes 2308
  379.0 6.0 %copy-start.31 = (f32[1,192]{1,0:T(1,128)S(1)}, f32[1,192]{1,0:T(1,128)}, u32[]{:S(2)}) copy-start(f32[1,192]{1,0:T(1,128)} %param.44) | copy-start | bytes 2308
  379.0 6.0 %copy-start.32 = (f32[1,192]{1,0:T(1,128)S(1)}, f32[1,192]{1,0:T(1,128)}, u32[]{:S(2)}) copy-start(f32[1,192]{1,0:T(1,128)} %param.51) | copy-start | bytes 2308
  379.0 7.3 %copy-start.5 = (f32[1,768,768]{2,1,0:T(8,128)S(1)}, f32[1,768,768]{2,1,0:T(8,128)}, u32[]{:S(2)}) copy-start(f32[1,768,768]{2,1,0:T(8,128)} %param.48) | copy-start | bytes 7077892
  379.0 7.3 %copy-start.6 = (f32[768,768]{1,0:T(8,128)S(1)}, f32[768,768]{1,0:T(8,128)}, u32[]{:S(2)}) copy-start(f32[768,768]{1,0:T(8,128)} %get-tuple-element.98) | copy-start | bytes 7077892
  379.0 7.3 %copy-start.11 = (bf16[768,768]{1,0:T(8,128)(2,1)S(1)}, bf16[768,768]{1,0:T(8,128)(2,1)}, u32[]{:S(2)}) copy-start(bf16[768,768]{1,0:T(8,128)(2,1)} %get-tuple-element.99) | copy-start | bytes 3538948
  379.0 7.3 %copy-start.12 = (bf16[768,768]{1,0:T(8,128)(2,1)S(1)}, bf16[768,768]{1,0:T(8,128)(2,1)}, u32[]{:S(2)}) copy-start(bf16[768,768]{1,0:T(8,128)(2,1)} %get-tuple-element.100) | copy-start | bytes 3538948
  379.0 7.3 %copy-start.13 = (bf16[768,768]{1,0:T(8,128)(2,1)S(1)}, bf16[768,768]{1,0:T(8,128)(2,1)}, u32[]{:S(2)}) copy-start(bf16[768,768]{1,0:T(8,128)(2,1)} %get-tuple-element.101) | copy-start | bytes 3538948
  383.4 2.3 copy-start.23
  383.4 2.3 copy-start.29
  383.4 2.3 copy-start.30
  383.4 3.3 copy-start
  383.4 4.0 %copy-start.4 = (f32[1,768,768]{2,1,0:T(8,128)S(1)}, f32[1,768,768]{2,1,0:T(8,128)}, u32[]{:S(2)}) copy-start(f32[1,768,768]{2,1,0:T(8,128)} %param.41) | copy-start | bytes 7077892
  387.4 4.2 %copy-start.16 = (f32[112,768]{1,0:T(8,128)S(1)}, f32[112,768]{1,0:T(8,128)}, u32[]{:S(2)}) copy-start(f32[112,768]{1,0:T(8,128)} %get-tuple-element.97) | copy-start | bytes 1032196
  387.4 4.2 %copy-start.14 = (f32[4,24,768]{2,1,0:T(8,128)S(1)}, f32[4,24,768]{2,1,0:T(8,128)}, u32[]{:S(2)}) copy-start(f32[4,24,768]{2,1,0:T(8,128)} %param.31) | copy-start | bytes 884740
  387.4 4.2 %copy-start.17 = (f32[4,24,768]{2,1,0:T(8,128)S(1)}, f32[4,24,768]{2,1,0:T(8,128)}, u32[]{:S(2)}) copy-start(f32[4,24,768]{2,1,0:T(8,128)} %param.38) | copy-start | bytes 884740
  387.4 4.2 %copy-start.18 = (f32[4,24,768]{2,1,0:T(8,128)S(1)}, f32[4,24,768]{2,1,0:T(8,128)}, u32[]{:S(2)}) copy-start(f32[4,24,768]{2,1,0:T(8,128)} %param.45) | copy-start | bytes 884740
  391.5 1.2 copy-start.21
  391.5 1.2 copy-start.24
  391.5 1.2 copy-start.25
  391.5 1.9 copy-start.22
  391.5 1.9 copy-start.27
  391.5 1.9 copy-start.28
  391.5 2.6 copy-start.10
  391.6 3.7 copy-start.15
  391.6 3.6 copy-start.9

commit v6 on v5

--- a/solution.py
+++ b/solution.py
@@ -985,14 +985,14 @@
             step_far(1)
             step_on(0)
     step_on(1)
+    step_middle(2)
+    step_middle(3)
 
     small = jnp.concatenate([vector_acc[...], router_acc[: extra - 8, :]], axis=0).astype(b16)
     if not inside:
         dense_ref[:extra, :] = jnp.concatenate([vector_acc[...], router_acc[: extra - 8, :]], axis=0)
         for k in range(4):
             dense_ref[extra + k * D : extra + (k + 1) * D, :] = weights_acc[k]
-        step_middle(2)
-        step_middle(3)
     for core_ in range(2 if inside else 0):
         for y_ in range(side):
             for x_ in range(side):
@@ -1021,8 +1021,6 @@
             send(stage.at[place], b_buf.at[place], b_s.at[place], b_r.at[place], second[kb - 1])
         else:
             total = parts[mine_].astype(f32) + c_buf[place].astype(f32)
-            if ka:
-                step_middle(2)
             for k in range(1, side):
                 slot = ka * side + k
                 remote(b_buf.at[slot], b_buf.at[slot], b_s.at[slot], b_r.at[slot], sibling).wait_recv()
@@ -1031,7 +1029,6 @@
                 stage[place] = total.astype(b16)
                 send(stage.at[place], a_buf.at[ka], a_s.at[ka], a_r.at[ka], first[ka - 1])
             else:
-                step_middle(3)
                 for k in range(1, side):
                     remote(a_buf.at[k], a_buf.at[k], a_s.at[k], a_r.at[k], sibling).wait_recv()
                     total = total + a_buf[k].astype(f32)

time: 405 us -> 394 us (0.973)
  the two profiles are of different devices: /device:TPU:24 before, /device:TPU:25 now
where the time goes in v6:
time: 394 us; the launch traced here: 386 us
  Pallas kernels  346 us (88%)
  other arithmetic  25.5 us (6%)
  local copies, waits for them, and re-layouts  9.36 us (2%)
  matrix products  4.22 us (1%)
    pallas_call x1, Pallas kernels, begin(): pl.pallas_call(functools.partial(begin_kernel, n, cols, blocks, part), ou...  209 us
    pallas_call x1, Pallas kernels, finish(): pl.pallas_call(functools.partial(finish_kernel, n, cols, extra, count //...  137 us
    add x7, other arithmetic, adam_step(): return (weight + update, new_first, new_square)  12.2 us

profile of v6, /device:TPU:25, one launch (start us, length us, event | category | flops | bytes accessed | tf_op | source)
XLA Modules:
  0.0 386.3 jit_solution(8037715772959870367)
XLA Ops:
  0.7 0.7 convert_element_type.82
  1.4 0.5 dynamic_update_slice.9
  1.9 0.7 convert_element_type.83
  2.6 0.4 dynamic_update_slice.10
  3.0 1.0 convert_element_type.81
  4.0 0.7 pad_maximum_fusion.1.in_ref
  4.7 0.7 convert_element_type.88
  5.4 0.7 convert_element_type.89
  6.1 0.2 dynamic_update_slice.11
  6.3 2.6 convert_bitcast_fusion.1
  8.9 0.0 copy-start.20
  8.9 1.5 pad_maximum_fusion.own_ref
  10.5 0.1 copy.76.routes_ref
  10.6 0.0 copy-start.2
  10.7 0.2 eq.47
  10.8 0.3 fusion.15
  11.1 0.2 convert_element_type.98
  11.3 0.7 fusion.26
  12.1 0.1 copy.78
  12.2 0.2 convert_element_type.93
  12.4 0.1 copy.79
  12.5 0.5 fusion
  13.0 0.6 copy.80
  13.6 2.7 convert_bitcast_fusion.slots_ref
  16.3 0.2 fusion.18
  16.5 1.3 fusion.11.marks_ref
  17.8 208.5 %begin.1 = (bf16[4,768,768]{2,1,0:T(8,128)(2,1)}, f32[8,768]{1,0:T(8,128)}, bf16[128,768]{1,0:T(8,128)(2,1)}, bf16[512,768]{1,0:T(8,128)(2,1)}, bf16[512,768]{1,...) custom-call(s32[2]{0:T(128)} %lengths_ref.3, ...), custom_call_target="tpu_custom_call" | custom-call | bytes 1024 | tf_op jit(solution)/shard_map/begin/pallas_call | solution.py:828
  226.3 137.1 %finish.1 = (f32[512,768]{1,0:T(8,128)}, f32[512,768]{1,0:T(8,128)}, f32[112,768]{1,0:T(8,128)}, bf16[768,768]{1,0:T(8,128)(2,1)}, bf16[784,768]{1,0:T(8,128)(2,...) custom-call(s32[2]{0:T(128)} %lengths_ref.3, f32[8,768]{1,0:T(8,128)} %get-tuple-element.74.vector_ref, ...), custom_call_target="tpu_custom_call" | custom-call | bytes 1024 | tf_op jit(solution)/shard_map/finish/pallas_call | solution.py:1078
  363.5 0.0 copy-start.7
  363.5 0.0 copy-start.8
  363.5 3.4 select_add_fusion
  366.9 0.1 copy-done.1
  367.0 0.7 copy-done.7
  367.7 0.7 copy-done.8
  368.5 4.4 %multiply_add_fusion = (f32[1,768,768]{2,1,0:T(8,128)}, f32[1,768,768]{2,1,0:T(8,128)}, f32[1,768,768]{2,1,0:T(8,128)}) fusion(f32[1,768,768]{2,1,0:T(8,128)S(1)} %copy-done.1, f32[784,768]{1,0:T(8,128)S(1)} %select_add_fusion, f32[1,768,768]{2,1,0:T(8,128)S(1)} %copy-done.7, f32[1,768,768]{2,1,0:T(8,128)S(1)} %copy-done.8), kind=kLoop, calls=%fused_computation.13 | loop fusion | flops 8847360 | bytes 16515072 | tf_op jit(solution)/shard_map/add | solution.py:38
  372.8 0.0 copy-start.4
  372.8 1.6 slice_bitcast_fusion
  374.4 0.7 multiply_add_fusion.10
  375.1 0.6 multiply_add_fusion.8
  375.7 0.4 copy-done
  376.1 0.7 copy-done.4
  376.8 4.1 %multiply_add_fusion.1 = (f32[1,768,768]{2,1,0:T(8,128)}, f32[1,768,768]{2,1,0:T(8,128)}, f32[1,768,768]{2,1,0:T(8,128)}, f32[768,768]{1,0:T(8,128)}) fusion(f32[1,768,768]{2,1,0:T(8,128)S(1)} %copy-done, f32[1,768,768]{2,1,0:T(8,128)S(1)} %copy-done.4, f32[1,768,768]{2,1,0:T(8,128)S(1)} %copy-done.5, f32[768,768]{1,0:T(8,128)S(1)} %copy-done.6, ...), kind=kLoop, calls=%fused_computation.14 | loop fusion | flops 12386304 | bytes 22413312 | tf_op jit(solution)/shard_map/add | solution.py:38
  381.0 0.0 copy-start.15
  381.1 1.0 multiply_add_fusion.2
  382.2 0.7 multiply_add_fusion.4
  382.9 0.7 multiply_add_fusion.6
  383.6 1.1 copy.107
  384.7 1.1 copy.108
  (61 shorter events, 0.2 us)
Async XLA Ops:
  8.9 1.6 copy-start.20
  10.5 3.1 copy-start.3
  10.6 5.6 %copy-start.2 = (s32[512,2]{1,0:T(8,128)}, s32[512,2]{1,0:T(8,128)S(1)}, u32[]{:S(2)}) copy-start(s32[512,2]{1,0:T(8,128)S(1)} %copy.76.routes_ref) | copy-start | bytes 12292
  12.5 3.8 copy-start.19
  363.5 3.5 copy-start.1
  363.5 4.2 %copy-start.7 = (f32[1,768,768]{2,1,0:T(8,128)S(1)}, f32[1,768,768]{2,1,0:T(8,128)}, u32[]{:S(2)}) copy-start(f32[1,768,768]{2,1,0:T(8,128)} %param.43) | copy-start | bytes 7077892
  363.5 4.9 %copy-start.8 = (f32[1,768,768]{2,1,0:T(8,128)S(1)}, f32[1,768,768]{2,1,0:T(8,128)}, u32[]{:S(2)}) copy-start(f32[1,768,768]{2,1,0:T(8,128)} %param.50) | copy-start | bytes 7077892
  368.4 6.0 %copy-start.26 = (f32[1,192]{1,0:T(1,128)S(1)}, f32[1,192]{1,0:T(1,128)}, u32[]{:S(2)}) copy-start(f32[1,192]{1,0:T(1,128)} %param.37) | copy-start | bytes 2308
  368.4 6.0 %copy-start.31 = (f32[1,192]{1,0:T(1,128)S(1)}, f32[1,192]{1,0:T(1,128)}, u32[]{:S(2)}) copy-start(f32[1,192]{1,0:T(1,128)} %param.44) | copy-start | bytes 2308
  368.4 6.0 %copy-start.32 = (f32[1,192]{1,0:T(1,128)S(1)}, f32[1,192]{1,0:T(1,128)}, u32[]{:S(2)}) copy-start(f32[1,192]{1,0:T(1,128)} %param.51) | copy-start | bytes 2308
  368.4 7.3 %copy-start.5 = (f32[1,768,768]{2,1,0:T(8,128)S(1)}, f32[1,768,768]{2,1,0:T(8,128)}, u32[]{:S(2)}) copy-start(f32[1,768,768]{2,1,0:T(8,128)} %param.48) | copy-start | bytes 7077892
  368.4 7.3 %copy-start.6 = (f32[768,768]{1,0:T(8,128)S(1)}, f32[768,768]{1,0:T(8,128)}, u32[]{:S(2)}) copy-start(f32[768,768]{1,0:T(8,128)} %get-tuple-element.98) | copy-start | bytes 7077892
  368.4 7.3 %copy-start.11 = (bf16[768,768]{1,0:T(8,128)(2,1)S(1)}, bf16[768,768]{1,0:T(8,128)(2,1)}, u32[]{:S(2)}) copy-start(bf16[768,768]{1,0:T(8,128)(2,1)} %get-tuple-element.99) | copy-start | bytes 3538948
  368.4 7.3 %copy-start.12 = (bf16[768,768]{1,0:T(8,128)(2,1)S(1)}, bf16[768,768]{1,0:T(8,128)(2,1)}, u32[]{:S(2)}) copy-start(bf16[768,768]{1,0:T(8,128)(2,1)} %get-tuple-element.100) | copy-start | bytes 3538948
  368.5 7.3 %copy-start.13 = (bf16[768,768]{1,0:T(8,128)(2,1)S(1)}, bf16[768,768]{1,0:T(8,128)(2,1)}, u32[]{:S(2)}) copy-start(bf16[768,768]{1,0:T(8,128)(2,1)} %get-tuple-element.101) | copy-start | bytes 3538948
  372.8 2.3 copy-start.23
  372.8 2.3 copy-start.29
  372.8 2.3 copy-start.30
  372.8 3.3 copy-start
  372.8 4.0 %copy-start.4 = (f32[1,768,768]{2,1,0:T(8,128)S(1)}, f32[1,768,768]{2,1,0:T(8,128)}, u32[]{:S(2)}) copy-start(f32[1,768,768]{2,1,0:T(8,128)} %param.41) | copy-start | bytes 7077892
  376.8 4.2 %copy-start.16 = (f32[112,768]{1,0:T(8,128)S(1)}, f32[112,768]{1,0:T(8,128)}, u32[]{:S(2)}) copy-start(f32[112,768]{1,0:T(8,128)} %get-tuple-element.97) | copy-start | bytes 1032196
  376.8 4.2 %copy-start.14 = (f32[4,24,768]{2,1,0:T(8,128)S(1)}, f32[4,24,768]{2,1,0:T(8,128)}, u32[]{:S(2)}) copy-start(f32[4,24,768]{2,1,0:T(8,128)} %param.31) | copy-start | bytes 884740
  376.8 4.2 %copy-start.17 = (f32[4,24,768]{2,1,0:T(8,128)S(1)}, f32[4,24,768]{2,1,0:T(8,128)}, u32[]{:S(2)}) copy-start(f32[4,24,768]{2,1,0:T(8,128)} %param.38) | copy-start | bytes 884740
  376.8 4.2 %copy-start.18 = (f32[4,24,768]{2,1,0:T(8,128)S(1)}, f32[4,24,768]{2,1,0:T(8,128)}, u32[]{:S(2)}) copy-start(f32[4,24,768]{2,1,0:T(8,128)} %param.45) | copy-start | bytes 884740
  380.9 1.2 copy-start.21
  380.9 1.2 copy-start.24
  380.9 1.2 copy-start.25
  381.0 1.9 copy-start.22
  381.0 1.9 copy-start.27
  381.0 1.9 copy-start.28
  381.0 2.6 copy-start.10
  381.0 3.7 copy-start.15
  381.1 3.6 copy-start.9
